TPU v7x, 256 devices: a whole 4x4x8 slice. The times are simulated.
256 devices in a mesh: row: 16 (over y, z_lo, core), col: 4 (over z_hi), hour: 4 (over x).
Axes of the slice: x: 4, y: 4, z: 8 (z_hi: 4, z_lo: 2; z = z_hi * 2 + z_lo), core: 2. Of those that a mesh axis runs over, the one named last changes fastest.
Arguments:
- spectra: bfloat16 [8, 2, 256, 8192], P(None, None, 'hour', ('row', 'col')), may hold values from -6 to 6
- quality: int32 [256], P('hour'), may hold values 0 or 1
- column_blocks: int32 [16], replicated, may hold values from 0 to 15, each once
Outputs:
- cross: bfloat16 [8, 2, 8192, 8192], P('hour', None, 'row', 'col')
Inputs may be any that keep to these rules, and one draw needn't show every extreme that they name: `column_blocks`: each channel block appears once.
All inputs are finite; a program needn't handle non-finite values. No bound on the sum of `quality` on one device may be relied on, other than what follows from the above.
Results may differ from a plain program's by a relative error of at most 0.012.
Values may be sent and summed in bfloat16 or wider, within the bound.
No kernel may reach another device: no remote copies, remote signals or barrier semaphores. Data moves between devices by JAX's collectives and lax.ppermute only.
A program may use at most 256 MiB of HBM per device.

v0:
```python
import jax
import jax.numpy as jnp
from jax import lax
from jax.sharding import PartitionSpec as P

CB = 512


def spread(value, axis, source):
    kept = jnp.where(lax.axis_index(axis) == source, value, 0).astype(value.dtype)
    return lax.psum(kept, axis)


def whiten(spectra, quality):
    values = spectra.astype(jnp.float32)
    power = jnp.mean(values * values, axis=(0, 1))
    keep = quality.astype(jnp.float32)[None, None, :, None]
    return (values * keep * lax.rsqrt(power + 1e-06)[None, None]).astype(jnp.bfloat16)


def products(left, right):
    real_part = jnp.einsum(
        "fwi,fwj->fij", left[:, 0], right[:, 0], preferred_element_type=jnp.float32
    )
    real_part = real_part + jnp.einsum(
        "fwi,fwj->fij", left[:, 1], right[:, 1], preferred_element_type=jnp.float32
    )
    imag_part = jnp.einsum(
        "fwi,fwj->fij", left[:, 1], right[:, 0], preferred_element_type=jnp.float32
    )
    imag_part = imag_part - jnp.einsum(
        "fwi,fwj->fij", left[:, 0], right[:, 1], preferred_element_type=jnp.float32
    )
    return jnp.stack([real_part, imag_part], axis=1)


def per_device(spectra, quality, column_blocks):
    hours = lax.axis_size("hour")
    group_windows = spectra.shape[2]
    total_windows = group_windows * hours
    factor = 1.0 / jnp.sqrt(jnp.float32(total_windows))
    white = whiten(spectra, quality)
    white = lax.all_to_all(white, "hour", split_axis=0, concat_axis=2, tiled=True)
    row_side = lax.all_gather(white, "col", axis=3, tiled=True)
    per_row = row_side.shape[3] // CB
    count_cols = column_blocks.shape[0] // lax.axis_size("col")
    col_index = lax.axis_index("col")
    gathered = []
    for offset in range(count_cols):
        block = column_blocks[col_index * count_cols + offset]
        gathered.append(spread(row_side, "row", block // per_row))
    col_side = jnp.concatenate(gathered, axis=3)
    total = None
    for group in range(hours):
        lower = group * group_windows
        upper = lower + group_windows
        part = products(row_side[:, :, lower:upper], col_side[:, :, lower:upper]) * factor
        rounded = lax.optimization_barrier(part.astype(jnp.bfloat16)).astype(jnp.float32)
        total = rounded if total is None else total + rounded
    return total.astype(jnp.bfloat16)


def solution(mesh):
    return jax.shard_map(
        per_device,
        mesh=mesh,
        in_specs=(P(None, None, "hour", ("row", "col")), P("hour"), P()),
        out_specs=P("hour", None, "row", "col"),
        check_vma=False,
    )
```

profile of v0, /device:TPU:2, one launch (start us, length us, event | category | flops | bytes accessed | tf_op | source)
XLA Modules:
  0.0 323.1 jit_solution(2055893305366161280)
XLA Ops:
  8.2 1.1 fusion.5
  9.3 9.9 %all_to_all.18 = bf16[8,2,64,128]{3,2,1,0:T(8,128)(2,1)S(1)} all-to-all(bf16[8,2,64,128]{3,2,1,0:T(8,128)(2,1)S(1)} %fusion.5), channel_id=1, replica_groups=mesh['row'=16,'col'=4,'hour'=4] {'hour'}, dimensions={0} | all-to-all | bytes 524288 | tf_op jit(solution)/shard_map/all_to_all | solution.py:43
  20.0 1.5 fusion.15
  24.0 37.5 %all-gather.2.cloned.1.call-done = bf16[2,2,256,512]{3,2,0,1:T(8,128)(2,1)} async-done(((bf16[2,2,256,128]{3,2,0,1:T(8,128)(2,1)}), bf16[2,2,256,512]{3,2,0,1:T(8,128)(2,1)}) %all-gather.2.cloned.1.call-update) | async-done | bytes 1048592 | tf_op jit(solution)/shard_map/all_gather | solution.py:44
  61.4 3.4 %broadcast_select_fusion = (bf16[2,2,256,512]{3,2,0,1:T(8,128)(2,1)}, bf16[2,2,256,512]{3,2,0,1:T(8,128)(2,1)}, bf16[2,2,256,512]{3,2,0,1:T(8,128)(2,1)}, bf16[2,2,256,512]{3,2,0,1:T(8,128)(2,1)}) fusion(bf16[2,2,256,512]{3,2,0,1:T(8,128)(2,1)} %all-gather.2.cloned.1.call-done, pred[]{:T(512)S(6)} %eq.15, pred[]{:T(512)S(6)} %eq.14, pred[]{:T(512)S(6)} %eq.13, ...), kind=kLoop, calls=%fused_computation.17 | loop fusion | flops 2097152 | bytes 5242884 | tf_op jit(solution)/shard_map/jit(_where)/select_n | solution.py:10
  64.9 138.3 %all-reduce.3.cloned.1.call-done = (bf16[2,2,256,512]{3,2,0,1:T(8,128)(2,1)}, bf16[2,2,256,512]{3,2,0,1:T(8,128)(2,1)}, bf16[2,2,256,512]{3,2,0,1:T(8,128)(2,1)}, bf16[2,2,256,512]{3,2,0,1:T(8,128)(2,1)}) async-done(((bf16[2,2,256,512]{3,2,0,1:T(8,128)(2,1)}, bf16[2,2,256,512]{3,2,0,1:T(8,128)(2,1)}, bf16[2,2,256,512]{3,2,0,1:T(8,128)(2,1)}, bf16[2,2,256,512]{3,2,0,1:T(8,128)(2,1)}), ...) | async-done | bytes 4194320 | tf_op jit(solution)/shard_map/psum | solution.py:11
  203.2 1.4 constant_dynamic-update-slice_fusion.3
  204.6 1.4 constant_dynamic-update-slice_fusion.2
  206.0 1.4 constant_dynamic-update-slice_fusion.1
  207.4 1.4 constant_dynamic-update-slice_fusion
  208.8 1.3 fusion.8
  210.1 1.3 fusion.7
  211.4 1.3 add_bitcast_fusion.3
  212.7 1.3 subtract_bitcast_fusion.3
  214.0 2.3 fusion
  216.3 4.7 %fusion.10 = f32[2,512,2048]{2,1,0:T(8,128)} fusion(bf16[2,2,256,2048]{3,2,0,1:T(8,128)(2,1)S(1)} %constant_dynamic-update-slice_fusion, bf16[2,2,256,512]{3,2,0,1:T(8,128)(2,1)S(1)} %copy-done), kind=kOutput, calls=%fused_computation.37 | convolution fusion | flops 268435456 | bytes 9043968 | tf_op jit(solution)/shard_map/fwi,fwj->fij/dot_general | solution.py:22
  220.9 1.3 fusion.9
  222.2 4.7 %add_bitcast_fusion.2 = f32[2,1,512,2048]{3,2,0,1:T(8,128)S(1)} fusion(f32[2,512,2048]{2,1,0:T(8,128)} %fusion.10, bf16[2,2,256,2048]{3,2,0,1:T(8,128)(2,1)S(1)} %constant_dynamic-update-slice_fusion, bf16[2,2,256,512]{3,2,0,1:T(8,128)(2,1)S(1)} %copy-done), kind=kOutput, calls=%fused_computation.14 | convolution fusion | flops 270532608 | bytes 17432576 | tf_op jit(solution)/shard_map/fwi,fwj->fij/dot_general | solution.py:25
  226.9 4.7 %subtract_bitcast_fusion.2 = f32[2,1,512,2048]{3,2,0,1:T(8,128)} fusion(f32[2,512,2048]{2,1,0:T(8,128)S(1)} %fusion.9, bf16[2,2,256,2048]{3,2,0,1:T(8,128)(2,1)S(1)} %constant_dynamic-update-slice_fusion, bf16[2,2,256,512]{3,2,0,1:T(8,128)(2,1)S(1)} %copy-done), kind=kOutput, calls=%fused_computation.13 | convolution fusion | flops 270532608 | bytes 17432576 | tf_op jit(solution)/shard_map/fwi,fwj->fij/dot_general | solution.py:31
  231.6 5.0 %fusion.1 = bf16[2,2,512,2048]{3,2,0,1:T(8,128)(2,1)S(1)} fusion(f32[2,1,512,2048]{3,2,0,1:T(8,128)} %subtract_bitcast_fusion.2, f32[2,1,512,2048]{3,2,0,1:T(8,128)S(1)} %add_bitcast_fusion.2), kind=kLoop, calls=%fused_computation.3 | loop fusion | flops 12582912 | bytes 25165824 | tf_op jit(solution)/shard_map/convert_element_type | solution.py:58
  236.6 4.7 %fusion.12 = f32[2,512,2048]{2,1,0:T(8,128)} fusion(bf16[2,2,256,2048]{3,2,0,1:T(8,128)(2,1)S(1)} %constant_dynamic-update-slice_fusion, bf16[2,2,256,512]{3,2,0,1:T(8,128)(2,1)S(1)} %copy-done), kind=kOutput, calls=%fused_computation.39 | convolution fusion | flops 268435456 | bytes 9043968 | tf_op jit(solution)/shard_map/fwi,fwj->fij/dot_general | solution.py:22
  241.3 1.3 fusion.11
  242.6 7.9 %add_bitcast_fusion.1 = f32[2,1,512,2048]{3,2,0,1:T(8,128)} fusion(f32[2,512,2048]{2,1,0:T(8,128)} %fusion.12, bf16[2,2,256,2048]{3,2,0,1:T(8,128)(2,1)S(1)} %constant_dynamic-update-slice_fusion, bf16[2,2,256,512]{3,2,0,1:T(8,128)(2,1)S(1)} %copy-done), kind=kOutput, calls=%fused_computation.12 | convolution fusion | flops 270532608 | bytes 17432576 | tf_op jit(solution)/shard_map/fwi,fwj->fij/dot_general | solution.py:25
  250.5 4.7 %subtract_bitcast_fusion.1 = f32[2,1,512,2048]{3,2,0,1:T(8,128)} fusion(f32[2,512,2048]{2,1,0:T(8,128)S(1)} %fusion.11, bf16[2,2,256,2048]{3,2,0,1:T(8,128)(2,1)S(1)} %constant_dynamic-update-slice_fusion, bf16[2,2,256,512]{3,2,0,1:T(8,128)(2,1)S(1)} %copy-done), kind=kOutput, calls=%fused_computation.11 | convolution fusion | flops 270532608 | bytes 17432576 | tf_op jit(solution)/shard_map/fwi,fwj->fij/dot_general | solution.py:31
  255.2 7.2 %fusion.2 = bf16[2,2,512,2048]{3,2,0,1:T(8,128)(2,1)S(1)} fusion(f32[2,1,512,2048]{3,2,0,1:T(8,128)} %subtract_bitcast_fusion.1, f32[2,1,512,2048]{3,2,0,1:T(8,128)} %add_bitcast_fusion.1), kind=kLoop, calls=%fused_computation.5 | loop fusion | flops 12582912 | bytes 25165824 | tf_op jit(solution)/shard_map/convert_element_type | solution.py:58
  262.3 4.5 %fusion.14 = f32[2,512,2048]{2,1,0:T(8,128)} fusion(bf16[2,2,256,2048]{3,2,0,1:T(8,128)(2,1)S(1)} %constant_dynamic-update-slice_fusion, bf16[2,2,256,512]{3,2,0,1:T(8,128)(2,1)S(1)} %copy-done), kind=kOutput, calls=%fused_computation.41 | convolution fusion | flops 268435456 | bytes 9043968 | tf_op jit(solution)/shard_map/fwi,fwj->fij/dot_general | solution.py:22
  266.8 4.7 %fusion.13 = f32[2,512,2048]{2,1,0:T(8,128)} fusion(bf16[2,2,256,2048]{3,2,0,1:T(8,128)(2,1)S(1)} %constant_dynamic-update-slice_fusion, bf16[2,2,256,512]{3,2,0,1:T(8,128)(2,1)S(1)} %copy-done), kind=kOutput, calls=%fused_computation.40 | convolution fusion | flops 268435456 | bytes 9043968 | tf_op jit(solution)/shard_map/fwi,fwj->fij/dot_general | solution.py:28
  271.5 7.9 %add_bitcast_fusion = f32[2,1,512,2048]{3,2,0,1:T(8,128)} fusion(f32[2,512,2048]{2,1,0:T(8,128)} %fusion.14, bf16[2,2,256,2048]{3,2,0,1:T(8,128)(2,1)S(1)} %constant_dynamic-update-slice_fusion, bf16[2,2,256,512]{3,2,0,1:T(8,128)(2,1)S(1)} %copy-done), kind=kOutput, calls=%fused_computation.10 | convolution fusion | flops 270532608 | bytes 17432576 | tf_op jit(solution)/shard_map/fwi,fwj->fij/dot_general | solution.py:25
  279.4 8.1 %subtract_bitcast_fusion = f32[2,1,512,2048]{3,2,0,1:T(8,128)} fusion(f32[2,512,2048]{2,1,0:T(8,128)} %fusion.13, bf16[2,2,256,2048]{3,2,0,1:T(8,128)(2,1)S(1)} %constant_dynamic-update-slice_fusion, bf16[2,2,256,512]{3,2,0,1:T(8,128)(2,1)S(1)} %copy-done), kind=kOutput, calls=%fused_computation.9 | convolution fusion | flops 270532608 | bytes 17432576 | tf_op jit(solution)/shard_map/fwi,fwj->fij/dot_general | solution.py:31
  287.5 9.5 %fusion.3 = bf16[2,2,512,2048]{3,2,0,1:T(8,128)(2,1)} fusion(f32[2,1,512,2048]{3,2,0,1:T(8,128)} %subtract_bitcast_fusion, f32[2,1,512,2048]{3,2,0,1:T(8,128)} %add_bitcast_fusion), kind=kLoop, calls=%fused_computation.7 | loop fusion | flops 12582912 | bytes 25165824 | tf_op jit(solution)/shard_map/convert_element_type | solution.py:58
  297.0 10.9 %add_convert_fusion = bf16[2,2,512,2048]{3,2,0,1:T(8,128)(2,1)} fusion(bf16[2,2,512,2048]{3,2,0,1:T(8,128)(2,1)} %fusion.3, bf16[2,2,512,2048]{3,2,0,1:T(8,128)(2,1)S(1)} %fusion.2, bf16[2,2,512,2048]{3,2,0,1:T(8,128)(2,1)S(1)} %fusion.1, bf16[2,2,512,2048]{3,2,0,1:T(8,128)(2,1)S(1)} %fusion), kind=kLoop, calls=%fused_computation.8 | loop fusion | flops 33554432 | bytes 41943040 | tf_op jit(solution)/shard_map/convert_element_type | solution.py:60
  307.9 8.4 %copy.5 = bf16[2,2,512,2048]{3,2,1,0:T(8,128)(2,1)} copy(bf16[2,2,512,2048]{3,2,0,1:T(8,128)(2,1)} %add_convert_fusion) | data formatting | bytes 16777216 | tf_op jit(solution)/shard_map/convert_element_type | solution.py:60
  (10 shorter events, 2.5 us)
Async XLA Ops:
  6.5 54.9 %all-gather.2.cloned.1.call-start = ((), (), s32[]{:S(2)}) async-start(), calls=%async_computation.1 | async-start | bytes 1310720 | tf_op jit(solution)/shard_map/all_gather | solution.py:44
  20.0 183.3 %all-reduce.3.cloned.1.call-start = ((), (), s32[]{:S(2)}) async-start(), calls=%async_computation.2 | async-start | bytes 8388608 | tf_op jit(solution)/shard_map/psum | solution.py:11
  61.4 147.3 %copy-start = (bf16[2,2,256,512]{3,2,0,1:T(8,128)(2,1)S(1)}, bf16[2,2,256,512]{3,2,0,1:T(8,128)(2,1)}, u32[]{:S(2)}) copy-start(bf16[2,2,256,512]{3,2,0,1:T(8,128)(2,1)} %all-gather.2.cloned.1.call-done) | copy-start | bytes 3145732
Sparse Core Ops, SparseCore 0:
  20.1 41.3 all-gather.1
  65.0 138.1 all-reduce.2
where the time goes:
time: 324 us; the launch traced here: 323 us
  waiting for transfers between devices  176 us (54%)
  matrix products  64.3 us (20%)
  other arithmetic  41 us (13%)
  local copies, waits for them, and re-layouts  16.1 us (5%)
  between operations  16 us (5%)
  blocking collectives  9.88 us (3%)
    psum x1, waiting for transfers between devices, spread(): return lax.psum(kept, axis)  138 us
    all_gather x1, waiting for transfers between devices, per_device(): row_side = lax.all_gather(white, 'col', axis=3, tiled=True)  37.5 us
    convert_element_type x4, other arithmetic, per_device(): part.astype(jnp.bfloat16)  23.9 us
    dot_general x4, matrix products, products(): jnp.einsum('fwi,fwj->fij', left[:, 1], right[:, 1], preferred_element_typ...  21.8 us
    dot_general x4, matrix products, products(): jnp.einsum('fwi,fwj->fij', left[:, 0], right[:, 1], preferred_element_typ...  18.8 us
    dot_general x4, matrix products, products(): jnp.einsum('fwi,fwj->fij', left[:, 0], right[:, 0], preferred_element_typ...  15.2 us
    convert_element_type x1, other arithmetic, per_device(): return total.astype(jnp.bfloat16)  10.9 us
    all_to_all x1, blocking collectives, per_device(): lax.all_to_all(white, 'hour', split_axis=0, concat_axis=2, tiled=True)  9.88 us
  transfers between devices with their start and end apart: 2, of which 2 were waited for; matrix products, arithmetic and copies ran while one was open for 0% of the time, Pallas kernels for 0%

commit v1 on v0

v1 whole, which is shorter than its diff:
```python
import functools

import jax
import jax.numpy as jnp
from jax import lax
from jax.experimental import pallas as pl
from jax.experimental.pallas import tpu as pltpu
from jax.sharding import PartitionSpec as P

CB = 512
BF = jnp.bfloat16
VMEM = pl.BlockSpec(memory_space=pltpu.VMEM)
SMEM = pl.BlockSpec(memory_space=pltpu.SMEM)
LIMIT = 40 * 1024 * 1024


def struct(*shape):
    return jax.ShapeDtypeStruct(shape, BF)


def params():
    return pltpu.CompilerParams(vmem_limit_bytes=LIMIT)


def whiten_kernel(spectra, quality, white, spread):
    values = spectra[...].astype(jnp.float32)
    power = jnp.sum(jnp.sum(values * values, axis=0), axis=0) * (1.0 / 16.0)
    scale = lax.rsqrt(power + 1e-06)
    keep = quality[...].astype(jnp.float32)
    result = (values * keep[None, None] * scale[None, None]).astype(BF)
    white[...] = result
    for h in range(4):
        for k in range(2):
            for z in range(2):
                for y in range(4):
                    spread[h, y, z, k] = result[2 * h + k, z, 16 * y : 16 * y + 16]


def whiten(spectra, quality):
    return pl.pallas_call(
        whiten_kernel,
        out_shape=[struct(8, 2, 64, 128), struct(4, 4, 2, 2, 16, 128)],
        in_specs=[VMEM, VMEM],
        out_specs=[VMEM, VMEM],
        compiler_params=params(),
        name="whiten",
    )(spectra, quality.reshape(64, 1))


def select_kernel(col, blocks, pieces, *refs):
    outs = refs[-4:]
    for d in range(4):
        group = lax.rem(col[0] + d, 4)
        for s in range(4):
            index = blocks[group * 4 + s]
            for h in range(4):
                outs[d][16 * h : 16 * h + 16, 128 * s : 128 * s + 128] = pieces[h, index]


def select(col, blocks, pieces, after):
    return pl.pallas_call(
        select_kernel,
        out_shape=[struct(64, 512)] * 4,
        in_specs=[SMEM, SMEM, VMEM] + [pl.BlockSpec(memory_space=pl.ANY)] * len(after),
        out_specs=[VMEM] * 4,
        compiler_params=params(),
        name="select",
    )(col, blocks, pieces, *after)


def merge_kernel(col, *refs):
    out = refs[4]
    for d in range(4):
        quarter = lax.rem(col[0] + d, 4)
        for s in range(4):
            at = pl.multiple_of(s * 512 + quarter * 128, 128)
            out[:, pl.ds(at, 128)] = refs[d][:, 128 * s : 128 * s + 128]


def merge(col, parts):
    return pl.pallas_call(
        merge_kernel,
        out_shape=struct(64, 2048),
        in_specs=[SMEM] + [VMEM] * 4,
        out_specs=VMEM,
        compiler_params=params(),
        name="merge",
    )(col, *parts)


def stack_kernel(count, *refs):
    out = refs[-1]
    at = 0
    for ref in refs[:count]:
        rows = ref.shape[0]
        out[at : at + rows] = ref[...]
        at += rows


def stack(parts, after=()):
    return pl.pallas_call(
        functools.partial(stack_kernel, len(parts)),
        out_shape=struct(sum(p.shape[0] for p in parts), parts[0].shape[1]),
        in_specs=[VMEM] * len(parts) + [pl.BlockSpec(memory_space=pl.ANY)] * len(after),
        out_specs=VMEM,
        compiler_params=params(),
        name="stack",
    )(*parts, *after)


def rows_out_kernel(place, own, before, after, far_low, far_high, *outs):
    col, hour = place[0], place[1]
    for d in range(4):
        pair = lax.rem(hour + d, 4)
        for ref, shift in ((own, 0), (after, 1), (before, 3)):
            quarter = lax.rem(col + shift, 4)
            outs[d][quarter] = ref[pl.ds(pair * 2, 2)]
        quarter = lax.rem(col + 2, 4)

        @pl.when(pair < 2)
        def _():
            outs[d][quarter] = far_low[pl.ds(lax.rem(pair, 2) * 2, 2)]

        @pl.when(pair >= 2)
        def _():
            outs[d][quarter] = far_high[pl.ds(lax.rem(pair, 2) * 2, 2)]


def rows_out(place, *refs):
    return pl.pallas_call(
        rows_out_kernel,
        out_shape=[struct(4, 2, 2, 64, 128)] * 4,
        in_specs=[SMEM] + [VMEM] * 5,
        out_specs=[VMEM] * 4,
        compiler_params=params(),
        name="rows_out",
    )(place, *refs)


def rows_in_kernel(place, *refs):
    out, held = refs[4], refs[5]
    for f in range(2):
        for p in range(2):
            for d in range(4):
                hour = lax.rem(place[1] + 4 - d, 4)
                for y in range(4):
                    at = pl.multiple_of(y * 64 + hour * 16, 16)
                    for q in range(4):
                        held[f, p, pl.ds(at, 16), 128 * q : 128 * q + 128] = refs[d][q, f, p, 16 * y : 16 * y + 16]
    for f in range(2):
        for p in range(2):
            out[f, p] = held[f, p].T


def rows_in(place, parts):
    return pl.pallas_call(
        rows_in_kernel,
        out_shape=struct(2, 2, 512, 256),
        in_specs=[SMEM] + [VMEM] * 4,
        out_specs=VMEM,
        scratch_shapes=[pltpu.VMEM((2, 2, 256, 512), BF)],
        compiler_params=params(),
        name="rows_in",
    )(place, *parts)


def product_kernel(place, left, near, far, *refs):
    out, held = refs[-2], refs[-1]
    y, z = place[0], place[1]
    spots = [(near, 0, 0), (near, 0, 1), (near, 3, 0), (near, 1, 0), (far, 3, 1), (far, 1, 1), (far, 2, 0), (far, 2, 1)]
    for i, (ref, dy, dz) in enumerate(spots):
        part = lax.rem(z + dz, 2)
        at = pl.multiple_of(lax.rem(y + dy, 4) * 64, 64)
        held[part, pl.ds(at, 64)] = ref[64 * (i % 4) : 64 * (i % 4) + 64]
    dot = functools.partial(jnp.dot, preferred_element_type=jnp.float32)
    factor = 1.0 / 16.0
    l0, l1 = left[0, 0], left[0, 1]
    r0, r1 = held[0], held[1]
    out[0, 0] = ((dot(l0, r0) + dot(l1, r1)) * factor).astype(BF)
    out[0, 1] = ((dot(l1, r0) - dot(l0, r1)) * factor).astype(BF)


def product(place, left, near, far, into=None):
    wide = 512
    extra = [] if into is None else [into]
    return pl.pallas_call(
        product_kernel,
        out_shape=struct(2, 2, 512, 2048),
        grid_spec=pltpu.PrefetchScalarGridSpec(
            num_scalar_prefetch=1,
            grid=(2048 // wide,),
            in_specs=[
                pl.BlockSpec((1, 2, 512, 256), lambda j, place: (place[2], 0, 0, 0)),
                pl.BlockSpec((256, wide), lambda j, place: (0, j)),
                pl.BlockSpec((256, wide), lambda j, place: (0, j)),
            ]
            + [pl.BlockSpec(memory_space=pl.ANY)] * len(extra),
            out_specs=pl.BlockSpec((1, 2, 512, wide), lambda j, place: (place[2], 0, 0, j)),
            scratch_shapes=[pltpu.VMEM((2, 256, wide), BF)],
        ),
        input_output_aliases={} if into is None else {4: 0},
        compiler_params=params(),
        cost_estimate=pl.CostEstimate(flops=2 * 4 * 512 * 256 * 2048, bytes_accessed=8 << 20, transcendentals=0),
        name="product",
    )(place, left, near, far, *extra)


def shift(value, axis, size, by):
    return lax.ppermute(value, axis, [(i, (i + by) % size) for i in range(size)])


def flip(value, bit):
    return lax.ppermute(value, "row", [(i, i ^ bit) for i in range(16)])


def per_device(spectra, quality, column_blocks):
    row, col, hour = (lax.axis_index(a) for a in ("row", "col", "hour"))
    y, z, k = row // 4, (row // 2) % 2, row % 2
    here = jnp.stack([col, hour]).astype(jnp.int32)
    white, spread = whiten(spectra, quality)

    before = shift(white, "col", 4, 1)
    after = shift(white, "col", 4, -1)

    pieces = lax.all_to_all(spread.reshape(64, 16, 128), ("hour", "row"), 0, 0, tiled=True)
    sent = select(here, column_blocks, pieces.reshape(4, 16, 16, 128), [before, after])
    from_before = shift(sent[1], "col", 4, 1)
    from_after = shift(sent[3], "col", 4, -1)
    from_far = shift(sent[2], "col", 4, 2)
    own = merge(here, [sent[0], from_after, from_far, from_before])

    far_low = shift(before[:4], "col", 4, 1)
    far_high = shift(after[4:], "col", 4, -1)
    own, far_low, far_high = lax.optimization_barrier((own, far_low, far_high))
    other = flip(own, 2)
    prev = shift(own, "row", 16, 4)
    succ = shift(own, "row", 16, -4)
    rows = rows_out(here, white, before, after, far_low, far_high)
    rows = [rows[0]] + [shift(rows[d], "hour", 4, d) for d in range(1, 4)]
    left = rows_in(here, rows)
    other_prev = shift(other, "row", 16, 4)
    other_succ = shift(other, "row", 16, -4)
    two_low = shift(prev[:32], "row", 16, 4)
    two_high = shift(succ[32:], "row", 16, -4)
    other_two_low = shift(other_prev[:32], "row", 16, 4)
    other_two_high = shift(other_succ[32:], "row", 16, -4)
    near = stack([own, other, prev, succ], rows[1:])
    far = stack([other_prev, other_succ, two_low, two_high, other_two_low, other_two_high])
    near_core = flip(near, 1)
    far_core = flip(far, 1)
    place = jnp.stack([y, z, k]).astype(jnp.int32)
    place_core = jnp.stack([y, z, 1 - k]).astype(jnp.int32)
    out = product(place, left, near, far)
    return product(place_core, left, near_core, far_core, out)


def solution(mesh):
    return jax.shard_map(
        per_device,
        mesh=mesh,
        in_specs=(P(None, None, "hour", ("row", "col")), P("hour"), P()),
        out_specs=P("hour", None, "row", "col"),
        check_vma=False,
    )
```

time: 324 us -> 97.8 us (0.30)
  the two profiles are of different devices: /device:TPU:2 before, /device:TPU:1 now
where the time goes in v1:
time: 97.8 us; the launch traced here: 97.4 us
  starting transfers between devices  54.4 us (56%)
  waiting for transfers between devices  22.5 us (23%)
  Pallas kernels  14.9 us (15%)
  local copies, waits for them, and re-layouts  5.27 us (5%)
    ppermute x18, starting transfers between devices, shift(): lax.ppermute(value, axis, [(i, (i + by) % size) for i in range(size)])  31.4 us
    ppermute x18, waiting for transfers between devices, shift(): lax.ppermute(value, axis, [(i, (i + by) % size) for i in range(size)])  20.3 us
    ppermute x3, starting transfers between devices, flip(): return lax.ppermute(value, 'row', [(i, i ^ bit) for i in range(16)])  12.6 us
    pallas_call x2, Pallas kernels, product(): pl.pallas_call(product_kernel, out_shape=struct(2, 2, 512, 2048), grid_sp...  11.1 us
    all_to_all x1, starting transfers between devices, per_device(): lax.all_to_all(spread.reshape(64, 16, 128), ('hour', 'row'), 0, 0, tiled=...  10.3 us
    unnamed x16, local copies, waits for them, and re-layouts  4.47 us
    ppermute x3, waiting for transfers between devices, flip(): return lax.ppermute(value, 'row', [(i, i ^ bit) for i in range(16)])  2.22 us
  transfers between devices with their start and end apart: 22, of which 6 were waited for; matrix products, arithmetic and copies ran while one was open for 0% of the time, Pallas kernels for 8%

profile of v1, /device:TPU:1, one launch (start us, length us, event | category | flops | bytes accessed | tf_op | source)
XLA Modules:
  0.0 97.4 jit_solution(10974328020076358842)
XLA Ops:
  0.0 0.7 copy.5.quality
  0.7 0.9 copy-done.6
  1.7 0.9 whiten.1
  2.5 10.3 %all-to-all-start = ((bf16[64,16,128]{2,1,0:T(8,128)(2,1)}), bf16[64,16,128]{2,1,0:T(8,128)(2,1)S(1)}, u32[]{:S(2)}, u32[]{:S(2)}) async-start(bf16[64,16,128]{2,1,0:T(8,128)(2,1)} %bitcast.6), calls=%async_computation | async-start | bytes 524288 | tf_op jit(solution)/shard_map/all_to_all | solution.py:225
  12.9 5.2 %collective-permute-start.1 = (bf16[8,2,64,128]{3,2,1,0:T(8,128)(2,1)S(1)}, bf16[8,2,64,128]{3,2,1,0:T(8,128)(2,1)S(1)}, u32[]{:S(2)}, u32[]{:S(2)}) collective-permute-start(bf16[8,2,64,128]{3,2,1,0:T(8,128)(2,1)S(1)} %get-tuple-element.18.own), channel_id=1, source_target_pairs={{0,12},{4,0},{8,4},{12,8},{1,13},{5,1},{9,5},{13,9},{2,14},{6,2},{... | collective-permute-start | bytes 786440 | tf_op jit(solution)/shard_map/ppermute | solution.py:209
  18.1 10.7 %collective-permute-done.1.refs_1_.after = bf16[8,2,64,128]{3,2,1,0:T(8,128)(2,1)S(1)} collective-permute-done((bf16[8,2,64,128]{3,2,1,0:T(8,128)(2,1)S(1)}, bf16[8,2,64,128]{3,2,1,0:T(8,128)(2,1)S(1)}, u32[]{:S(2)}, u32[]{:S(2)}) %collective-permute-start.1) | collective-permute-done | bytes 262176 | tf_op jit(solution)/shard_map/ppermute | solution.py:209
  28.9 4.5 %collective-permute-start.6 = (bf16[4,2,64,128]{3,2,1,0:T(8,128)(2,1)S(1)}, bf16[4,2,64,128]{3,2,1,0:T(8,128)(2,1)S(1)}, u32[]{:S(2)}, u32[]{:S(2)}) collective-permute-start(bf16[4,2,64,128]{3,2,1,0:T(8,128)(2,1)S(1)} %slice.25), channel_id=1, source_target_pairs={{0,12},{4,0},{8,4},{12,8},{1,13},{5,1},{9,5},{13,9},{2,14},{6,2},{... | collective-permute-start | bytes 393224 | tf_op jit(solution)/shard_map/ppermute | solution.py:209
  33.6 0.7 copy-done.7
  34.2 0.6 select.13
  34.8 3.6 %collective-permute-start.2 = (bf16[64,512]{1,0:T(8,128)(2,1)S(1)}, bf16[64,512]{1,0:T(8,128)(2,1)S(1)}, u32[]{:S(2)}, u32[]{:S(2)}) collective-permute-start(bf16[64,512]{1,0:T(8,128)(2,1)S(1)} %get-tuple-element.21), channel_id=1, source_target_pairs={{0,12},{4,0},{8,4},{12,8},{1,13},{5,1},{9,5},{13,9},{2,14},{6,2},{... | collective-permute-start | bytes 196616 | tf_op jit(solution)/shard_map/ppermute | solution.py:209
  38.5 2.2 %collective-permute-start.4 = (bf16[64,512]{1,0:T(8,128)(2,1)S(1)}, bf16[64,512]{1,0:T(8,128)(2,1)S(1)}, u32[]{:S(2)}, u32[]{:S(2)}) collective-permute-start(bf16[64,512]{1,0:T(8,128)(2,1)S(1)} %get-tuple-element.23), channel_id=1, source_target_pairs={{0,4},{4,8},{8,12},{12,0},{1,5},{5,9},{9,13},{13,1},{2,6},{6,10},{... | collective-permute-start | bytes 196616 | tf_op jit(solution)/shard_map/ppermute | solution.py:209
  40.7 5.7 %collective-permute-done.3.refs_2_ = bf16[64,512]{1,0:T(8,128)(2,1)S(1)} collective-permute-done((bf16[64,512]{1,0:T(8,128)(2,1)S(1)}, bf16[64,512]{1,0:T(8,128)(2,1)S(1)}, u32[]{:S(2)}, u32[]{:S(2)}) %collective-permute-start.3) | collective-permute-done | bytes 65568 | tf_op jit(solution)/shard_map/ppermute | solution.py:209
  47.0 4.0 %collective-permute-start.10 = (bf16[64,2048]{1,0:T(8,128)(2,1)S(1)}, bf16[64,2048]{1,0:T(8,128)(2,1)S(1)}, u32[]{:S(2)}, u32[]{:S(2)}) collective-permute-start(bf16[64,2048]{1,0:T(8,128)(2,1)S(1)} %merge.1.refs_0_), channel_id=1, source_target_pairs={{0,32},{16,48},{32,0},{48,16},{64,96},{80,112},{96,64},{112,80},{1... | collective-permute-start | bytes 786440 | tf_op jit(solution)/shard_map/ppermute | solution.py:213
  51.0 2.5 %collective-permute-start.12 = (bf16[64,2048]{1,0:T(8,128)(2,1)S(1)}, bf16[64,2048]{1,0:T(8,128)(2,1)S(1)}, u32[]{:S(2)}, u32[]{:S(2)}) collective-permute-start(bf16[64,2048]{1,0:T(8,128)(2,1)S(1)} %merge.1.refs_0_), channel_id=1, source_target_pairs={{0,192},{16,208},{32,224},{48,240},{64,0},{80,16},{96,32},{112,48}... | collective-permute-start | bytes 786440 | tf_op jit(solution)/shard_map/ppermute | solution.py:209
  53.6 2.2 %collective-permute-done.10.refs_1_ = bf16[64,2048]{1,0:T(8,128)(2,1)S(1)} collective-permute-done((bf16[64,2048]{1,0:T(8,128)(2,1)S(1)}, bf16[64,2048]{1,0:T(8,128)(2,1)S(1)}, u32[]{:S(2)}, u32[]{:S(2)}) %collective-permute-start.10) | collective-permute-done | bytes 262176 | tf_op jit(solution)/shard_map/ppermute | solution.py:213
  55.8 2.7 %collective-permute-start.15 = (bf16[64,2048]{1,0:T(8,128)(2,1)S(1)}, bf16[64,2048]{1,0:T(8,128)(2,1)S(1)}, u32[]{:S(2)}, u32[]{:S(2)}) collective-permute-start(bf16[64,2048]{1,0:T(8,128)(2,1)S(1)} %collective-permute-done.10.refs_1_), channel_id=1, source_target_pairs={{0,192},{16,208},{32,224},{48,240},{64,0},{80,16},{96,32},{112,48}... | collective-permute-start | bytes 786440 | tf_op jit(solution)/shard_map/ppermute | solution.py:209
  58.5 0.7 rows_out.1
  59.2 1.3 %collective-permute-start.7 = (bf16[4,2,2,64,128]{4,3,2,1,0:T(8,128)(2,1)S(1)}, bf16[4,2,2,64,128]{4,3,2,1,0:T(8,128)(2,1)S(1)}, u32[]{:S(2)}, u32[]{:S(2)}) collective-permute-start(bf16[4,2,2,64,128]{4,3,2,1,0:T(8,128)(2,1)S(1)} %get-tuple-element.27), channel_id=1, source_target_pairs={{0,1},{1,2},{2,3},{3,0},{4,5},{5,6},{6,7},{7,4},{8,9},{9,10},{10,1... | collective-permute-start | bytes 786440 | tf_op jit(solution)/shard_map/ppermute | solution.py:209
  60.6 2.6 %collective-permute-start.8 = (bf16[4,2,2,64,128]{4,3,2,1,0:T(8,128)(2,1)S(1)}, bf16[4,2,2,64,128]{4,3,2,1,0:T(8,128)(2,1)S(1)}, u32[]{:S(2)}, u32[]{:S(2)}) collective-permute-start(bf16[4,2,2,64,128]{4,3,2,1,0:T(8,128)(2,1)S(1)} %get-tuple-element.28), channel_id=1, source_target_pairs={{0,2},{1,3},{2,0},{3,1},{4,6},{5,7},{6,4},{7,5},{8,10},{9,11},{10,... | collective-permute-start | bytes 786440 | tf_op jit(solution)/shard_map/ppermute | solution.py:209
  63.2 1.1 %collective-permute-start.9 = (bf16[4,2,2,64,128]{4,3,2,1,0:T(8,128)(2,1)S(1)}, bf16[4,2,2,64,128]{4,3,2,1,0:T(8,128)(2,1)S(1)}, u32[]{:S(2)}, u32[]{:S(2)}) collective-permute-start(bf16[4,2,2,64,128]{4,3,2,1,0:T(8,128)(2,1)S(1)} %get-tuple-element.29), channel_id=1, source_target_pairs={{0,3},{1,0},{2,1},{3,2},{4,7},{5,4},{6,5},{7,6},{8,11},{9,8},{10,9... | collective-permute-start | bytes 786440 | tf_op jit(solution)/shard_map/ppermute | solution.py:209
  64.3 2.7 %collective-permute-start.17 = (bf16[32,2048]{1,0:T(8,128)(2,1)S(1)}, bf16[32,2048]{1,0:T(8,128)(2,1)S(1)}, u32[]{:S(2)}, u32[]{:S(2)}) collective-permute-start(bf16[32,2048]{1,0:T(8,128)(2,1)S(1)} %slice.27), channel_id=1, source_target_pairs={{0,192},{16,208},{32,224},{48,240},{64,0},{80,16},{96,32},{112,48}... | collective-permute-start | bytes 393224 | tf_op jit(solution)/shard_map/ppermute | solution.py:209
  67.1 2.7 %collective-permute-start.19 = (bf16[32,2048]{1,0:T(8,128)(2,1)S(1)}, bf16[32,2048]{1,0:T(8,128)(2,1)S(1)}, u32[]{:S(2)}, u32[]{:S(2)}) collective-permute-start(bf16[32,2048]{1,0:T(8,128)(2,1)S(1)} %slice.29), channel_id=1, source_target_pairs={{0,192},{16,208},{32,224},{48,240},{64,0},{80,16},{96,32},{112,48}... | collective-permute-start | bytes 393224 | tf_op jit(solution)/shard_map/ppermute | solution.py:209
  69.8 2.3 %collective-permute-done.8.refs_2_.refs_5_ = bf16[4,2,2,64,128]{4,3,2,1,0:T(8,128)(2,1)S(1)} collective-permute-done((bf16[4,2,2,64,128]{4,3,2,1,0:T(8,128)(2,1)S(1)}, bf16[4,2,2,64,128]{4,3,2,1,0:T(8,128)(2,1)S(1)}, u32[]{:S(2)}, u32[]{:S(2)}) %collective-permute-start.8) | collective-permute-done | bytes 262176 | tf_op jit(solution)/shard_map/ppermute | solution.py:209
  72.4 4.2 %collective-permute-start.13 = (bf16[256,2048]{1,0:T(8,128)(2,1)S(1)}, bf16[256,2048]{1,0:T(8,128)(2,1)S(1)}, u32[]{:S(2)}, u32[]{:S(2)}) collective-permute-start(bf16[256,2048]{1,0:T(8,128)(2,1)S(1)} %stack.40.near), channel_id=1, source_target_pairs={{0,16},{16,0},{32,48},{48,32},{64,80},{80,64},{96,112},{112,96},{1... | collective-permute-start | bytes 3145736 | tf_op jit(solution)/shard_map/ppermute | solution.py:213
  76.7 1.4 %collective-permute-done.18.refs_4_ = bf16[32,2048]{1,0:T(8,128)(2,1)S(1)} collective-permute-done((bf16[32,2048]{1,0:T(8,128)(2,1)S(1)}, bf16[32,2048]{1,0:T(8,128)(2,1)S(1)}, u32[]{:S(2)}, u32[]{:S(2)}) %collective-permute-start.18) | collective-permute-done | bytes 131104 | tf_op jit(solution)/shard_map/ppermute | solution.py:209
  78.1 4.3 %collective-permute-start.20 = (bf16[256,2048]{1,0:T(8,128)(2,1)S(1)}, bf16[256,2048]{1,0:T(8,128)(2,1)}, u32[]{:S(2)}, u32[]{:S(2)}) collective-permute-start(bf16[256,2048]{1,0:T(8,128)(2,1)S(1)} %stack.41.far), channel_id=1, source_target_pairs={{0,16},{16,0},{32,48},{48,32},{64,80},{80,64},{96,112},{112,96},{1... | collective-permute-start | bytes 3145736 | tf_op jit(solution)/shard_map/ppermute | solution.py:213
  82.5 0.9 copy-done.1
  83.4 0.9 copy-done.3
  84.4 0.9 copy-done.5
  85.3 1.0 %rows_in.1.left = bf16[2,2,512,256]{3,2,1,0:T(8,128)(2,1)S(1)} custom-call(s32[2]{0:T(128)S(1)} %pad_add_fusion.2.col.place, bf16[4,2,2,64,128]{4,3,2,1,0:T(8,128)(2,1)S(1)} %copy-done.5, bf16[4,2,2,64,128]{4,3,2,1,0:T(8,128)(2,1)S(1)} %collective-permute-done.7.refs_1_.refs_4_, bf16[4,2,2,64,128]{4,3,2,1,0:T(8,128)(2,1)S(1)} %copy-done.1, ...), custom_call_target="tpu_custom_call" | custom-call | tf_op jit(solution)/shard_map/rows_in/pallas_call | solution.py:156
  86.4 4.9 %product.2.refs_0_ = bf16[2,2,512,2048]{3,2,1,0:T(8,128)(2,1)} custom-call(s32[3]{0:T(128)S(1)} %get-tuple-element.32.place, bf16[2,2,512,256]{3,2,1,0:T(8,128)(2,1)S(1)} %rows_in.1.left, bf16[256,2048]{1,0:T(8,128)(2,1)S(1)} %stack.40.near, bf16[256,2048]{1,0:T(8,128)(2,1)S(1)} %stack.41.far), custom_call_target="tpu_custom_call" | custom-call | flops 2147483648 | bytes 8388608 | tf_op jit(solution)/shard_map/product/pallas_call | solution.py:186
  91.3 6.2 %product.3 = bf16[2,2,512,2048]{3,2,1,0:T(8,128)(2,1)} custom-call(s32[3]{0:T(128)S(1)} %get-tuple-element.31.place, bf16[2,2,512,256]{3,2,1,0:T(8,128)(2,1)S(1)} %rows_in.1.left, bf16[256,2048]{1,0:T(8,128)(2,1)S(1)} %collective-permute-done.13.near, bf16[256,2048]{1,0:T(8,128)(2,1)} %collective-permute-done.20.far, ...), custom_call_target="tpu_custom_call", output_to_operand_aliasing={{}: (4, {})} | custom-call | flops 2147483648 | bytes 8388608 | tf_op jit(solution)/shard_map/product/pallas_call | solution.py:186
  (46 shorter events, 1.4 us)
Async XLA Ops:
  0.7 0.9 copy-start.6
  2.5 31.0 %all-to-all-start = ((bf16[64,16,128]{2,1,0:T(8,128)(2,1)}), bf16[64,16,128]{2,1,0:T(8,128)(2,1)S(1)}, u32[]{:S(2)}, u32[]{:S(2)}) async-start(bf16[64,16,128]{2,1,0:T(8,128)(2,1)} %bitcast.6), calls=%async_computation | async-start | bytes 524288 | tf_op jit(solution)/shard_map/all_to_all | solution.py:225
  12.9 15.9 %collective-permute-start.1 = (bf16[8,2,64,128]{3,2,1,0:T(8,128)(2,1)S(1)}, bf16[8,2,64,128]{3,2,1,0:T(8,128)(2,1)S(1)}, u32[]{:S(2)}, u32[]{:S(2)}) collective-permute-start(bf16[8,2,64,128]{3,2,1,0:T(8,128)(2,1)S(1)} %get-tuple-element.18.own), channel_id=1, source_target_pairs={{0,12},{4,0},{8,4},{12,8},{1,13},{5,1},{9,5},{13,9},{2,14},{6,2},{... | collective-permute-start | bytes 786440 | tf_op jit(solution)/shard_map/ppermute | solution.py:209
  18.1 15.3 %collective-permute-start = (bf16[8,2,64,128]{3,2,1,0:T(8,128)(2,1)S(1)}, bf16[8,2,64,128]{3,2,1,0:T(8,128)(2,1)S(1)}, u32[]{:S(2)}, u32[]{:S(2)}) collective-permute-start(bf16[8,2,64,128]{3,2,1,0:T(8,128)(2,1)S(1)} %get-tuple-element.18.own), channel_id=1, source_target_pairs={{0,4},{4,8},{8,12},{12,0},{1,5},{5,9},{9,13},{13,1},{2,6},{6,10},{... | collective-permute-start | bytes 786440 | tf_op jit(solution)/shard_map/ppermute | solution.py:209
  28.9 18.1 %collective-permute-start.6 = (bf16[4,2,64,128]{3,2,1,0:T(8,128)(2,1)S(1)}, bf16[4,2,64,128]{3,2,1,0:T(8,128)(2,1)S(1)}, u32[]{:S(2)}, u32[]{:S(2)}) collective-permute-start(bf16[4,2,64,128]{3,2,1,0:T(8,128)(2,1)S(1)} %slice.25), channel_id=1, source_target_pairs={{0,12},{4,0},{8,4},{12,8},{1,13},{5,1},{9,5},{13,9},{2,14},{6,2},{... | collective-permute-start | bytes 393224 | tf_op jit(solution)/shard_map/ppermute | solution.py:209
  33.4 13.6 %collective-permute-start.5 = (bf16[4,2,64,128]{3,2,1,0:T(8,128)(2,1)S(1)}, bf16[4,2,64,128]{3,2,1,0:T(8,128)(2,1)S(1)}, u32[]{:S(2)}, u32[]{:S(2)}) collective-permute-start(bf16[4,2,64,128]{3,2,1,0:T(8,128)(2,1)S(1)} %slice.24), channel_id=1, source_target_pairs={{0,4},{4,8},{8,12},{12,0},{1,5},{5,9},{9,13},{13,1},{2,6},{6,10},{... | collective-permute-start | bytes 393224 | tf_op jit(solution)/shard_map/ppermute | solution.py:209
  33.6 0.7 copy-start.7
  34.8 5.8 %collective-permute-start.2 = (bf16[64,512]{1,0:T(8,128)(2,1)S(1)}, bf16[64,512]{1,0:T(8,128)(2,1)S(1)}, u32[]{:S(2)}, u32[]{:S(2)}) collective-permute-start(bf16[64,512]{1,0:T(8,128)(2,1)S(1)} %get-tuple-element.21), channel_id=1, source_target_pairs={{0,12},{4,0},{8,4},{12,8},{1,13},{5,1},{9,5},{13,9},{2,14},{6,2},{... | collective-permute-start | bytes 196616 | tf_op jit(solution)/shard_map/ppermute | solution.py:209
  38.5 7.9 %collective-permute-start.3 = (bf16[64,512]{1,0:T(8,128)(2,1)S(1)}, bf16[64,512]{1,0:T(8,128)(2,1)S(1)}, u32[]{:S(2)}, u32[]{:S(2)}) collective-permute-start(bf16[64,512]{1,0:T(8,128)(2,1)S(1)} %get-tuple-element.22), channel_id=1, source_target_pairs={{0,8},{4,12},{8,0},{12,4},{1,9},{5,13},{9,1},{13,5},{2,10},{6,14},... | collective-permute-start | bytes 196616 | tf_op jit(solution)/shard_map/ppermute | solution.py:209
  38.5 7.9 %collective-permute-start.4 = (bf16[64,512]{1,0:T(8,128)(2,1)S(1)}, bf16[64,512]{1,0:T(8,128)(2,1)S(1)}, u32[]{:S(2)}, u32[]{:S(2)}) collective-permute-start(bf16[64,512]{1,0:T(8,128)(2,1)S(1)} %get-tuple-element.23), channel_id=1, source_target_pairs={{0,4},{4,8},{8,12},{12,0},{1,5},{5,9},{9,13},{13,1},{2,6},{6,10},{... | collective-permute-start | bytes 196616 | tf_op jit(solution)/shard_map/ppermute | solution.py:209
  47.0 8.8 %collective-permute-start.10 = (bf16[64,2048]{1,0:T(8,128)(2,1)S(1)}, bf16[64,2048]{1,0:T(8,128)(2,1)S(1)}, u32[]{:S(2)}, u32[]{:S(2)}) collective-permute-start(bf16[64,2048]{1,0:T(8,128)(2,1)S(1)} %merge.1.refs_0_), channel_id=1, source_target_pairs={{0,32},{16,48},{32,0},{48,16},{64,96},{80,112},{96,64},{112,80},{1... | collective-permute-start | bytes 786440 | tf_op jit(solution)/shard_map/ppermute | solution.py:213
  51.0 9.5 %collective-permute-start.12 = (bf16[64,2048]{1,0:T(8,128)(2,1)S(1)}, bf16[64,2048]{1,0:T(8,128)(2,1)S(1)}, u32[]{:S(2)}, u32[]{:S(2)}) collective-permute-start(bf16[64,2048]{1,0:T(8,128)(2,1)S(1)} %merge.1.refs_0_), channel_id=1, source_target_pairs={{0,192},{16,208},{32,224},{48,240},{64,0},{80,16},{96,32},{112,48}... | collective-permute-start | bytes 786440 | tf_op jit(solution)/shard_map/ppermute | solution.py:209
  53.6 9.6 %collective-permute-start.11 = (bf16[64,2048]{1,0:T(8,128)(2,1)S(1)}, bf16[64,2048]{1,0:T(8,128)(2,1)S(1)}, u32[]{:S(2)}, u32[]{:S(2)}) collective-permute-start(bf16[64,2048]{1,0:T(8,128)(2,1)S(1)} %merge.1.refs_0_), channel_id=1, source_target_pairs={{0,64},{16,80},{32,96},{48,112},{64,128},{80,144},{96,160},{112,17... | collective-permute-start | bytes 786440 | tf_op jit(solution)/shard_map/ppermute | solution.py:209
  55.8 8.5 %collective-permute-start.15 = (bf16[64,2048]{1,0:T(8,128)(2,1)S(1)}, bf16[64,2048]{1,0:T(8,128)(2,1)S(1)}, u32[]{:S(2)}, u32[]{:S(2)}) collective-permute-start(bf16[64,2048]{1,0:T(8,128)(2,1)S(1)} %collective-permute-done.10.refs_1_), channel_id=1, source_target_pairs={{0,192},{16,208},{32,224},{48,240},{64,0},{80,16},{96,32},{112,48}... | collective-permute-start | bytes 786440 | tf_op jit(solution)/shard_map/ppermute | solution.py:209
  59.1 13.1 %copy-start.4 = (bf16[4,2,2,64,128]{4,3,2,1,0:T(8,128)(2,1)}, bf16[4,2,2,64,128]{4,3,2,1,0:T(8,128)(2,1)S(1)}, u32[]{:S(2)}) copy-start(bf16[4,2,2,64,128]{4,3,2,1,0:T(8,128)(2,1)S(1)} %get-tuple-element.26.refs_0_) | copy-start | bytes 786436
  59.1 7.8 %collective-permute-start.14 = (bf16[64,2048]{1,0:T(8,128)(2,1)S(1)}, bf16[64,2048]{1,0:T(8,128)(2,1)S(1)}, u32[]{:S(2)}, u32[]{:S(2)}) collective-permute-start(bf16[64,2048]{1,0:T(8,128)(2,1)S(1)} %collective-permute-done.10.refs_1_), channel_id=1, source_target_pairs={{0,64},{16,80},{32,96},{48,112},{64,128},{80,144},{96,160},{112,17... | collective-permute-start | bytes 786440 | tf_op jit(solution)/shard_map/ppermute | solution.py:209
  59.2 7.9 %collective-permute-start.7 = (bf16[4,2,2,64,128]{4,3,2,1,0:T(8,128)(2,1)S(1)}, bf16[4,2,2,64,128]{4,3,2,1,0:T(8,128)(2,1)S(1)}, u32[]{:S(2)}, u32[]{:S(2)}) collective-permute-start(bf16[4,2,2,64,128]{4,3,2,1,0:T(8,128)(2,1)S(1)} %get-tuple-element.27), channel_id=1, source_target_pairs={{0,1},{1,2},{2,3},{3,0},{4,5},{5,6},{6,7},{7,4},{8,9},{9,10},{10,1... | collective-permute-start | bytes 786440 | tf_op jit(solution)/shard_map/ppermute | solution.py:209
  60.6 11.6 %collective-permute-start.8 = (bf16[4,2,2,64,128]{4,3,2,1,0:T(8,128)(2,1)S(1)}, bf16[4,2,2,64,128]{4,3,2,1,0:T(8,128)(2,1)S(1)}, u32[]{:S(2)}, u32[]{:S(2)}) collective-permute-start(bf16[4,2,2,64,128]{4,3,2,1,0:T(8,128)(2,1)S(1)} %get-tuple-element.28), channel_id=1, source_target_pairs={{0,2},{1,3},{2,0},{3,1},{4,6},{5,7},{6,4},{7,5},{8,10},{9,11},{10,... | collective-permute-start | bytes 786440 | tf_op jit(solution)/shard_map/ppermute | solution.py:209
  63.2 9.1 %collective-permute-start.9 = (bf16[4,2,2,64,128]{4,3,2,1,0:T(8,128)(2,1)S(1)}, bf16[4,2,2,64,128]{4,3,2,1,0:T(8,128)(2,1)S(1)}, u32[]{:S(2)}, u32[]{:S(2)}) collective-permute-start(bf16[4,2,2,64,128]{4,3,2,1,0:T(8,128)(2,1)S(1)} %get-tuple-element.29), channel_id=1, source_target_pairs={{0,3},{1,0},{2,1},{3,2},{4,7},{5,4},{6,5},{7,6},{8,11},{9,8},{10,9... | collective-permute-start | bytes 786440 | tf_op jit(solution)/shard_map/ppermute | solution.py:209
  64.3 12.3 %collective-permute-start.17 = (bf16[32,2048]{1,0:T(8,128)(2,1)S(1)}, bf16[32,2048]{1,0:T(8,128)(2,1)S(1)}, u32[]{:S(2)}, u32[]{:S(2)}) collective-permute-start(bf16[32,2048]{1,0:T(8,128)(2,1)S(1)} %slice.27), channel_id=1, source_target_pairs={{0,192},{16,208},{32,224},{48,240},{64,0},{80,16},{96,32},{112,48}... | collective-permute-start | bytes 393224 | tf_op jit(solution)/shard_map/ppermute | solution.py:209
  67.0 9.6 %collective-permute-start.16 = (bf16[32,2048]{1,0:T(8,128)(2,1)S(1)}, bf16[32,2048]{1,0:T(8,128)(2,1)S(1)}, u32[]{:S(2)}, u32[]{:S(2)}) collective-permute-start(bf16[32,2048]{1,0:T(8,128)(2,1)S(1)} %slice.26), channel_id=1, source_target_pairs={{0,64},{16,80},{32,96},{48,112},{64,128},{80,144},{96,160},{112,17... | collective-permute-start | bytes 393224 | tf_op jit(solution)/shard_map/ppermute | solution.py:209
  67.1 9.5 %collective-permute-start.19 = (bf16[32,2048]{1,0:T(8,128)(2,1)S(1)}, bf16[32,2048]{1,0:T(8,128)(2,1)S(1)}, u32[]{:S(2)}, u32[]{:S(2)}) collective-permute-start(bf16[32,2048]{1,0:T(8,128)(2,1)S(1)} %slice.29), channel_id=1, source_target_pairs={{0,192},{16,208},{32,224},{48,240},{64,0},{80,16},{96,32},{112,48}... | collective-permute-start | bytes 393224 | tf_op jit(solution)/shard_map/ppermute | solution.py:209
  72.2 4.4 %copy-start = (bf16[4,2,2,64,128]{4,3,2,1,0:T(8,128)(2,1)}, bf16[4,2,2,64,128]{4,3,2,1,0:T(8,128)(2,1)S(1)}, u32[]{:S(2)}) copy-start(bf16[4,2,2,64,128]{4,3,2,1,0:T(8,128)(2,1)S(1)} %collective-permute-done.8.refs_2_.refs_5_) | copy-start | bytes 786436
  72.2 5.8 %collective-permute-start.18 = (bf16[32,2048]{1,0:T(8,128)(2,1)S(1)}, bf16[32,2048]{1,0:T(8,128)(2,1)S(1)}, u32[]{:S(2)}, u32[]{:S(2)}) collective-permute-start(bf16[32,2048]{1,0:T(8,128)(2,1)S(1)} %slice.28), channel_id=1, source_target_pairs={{0,64},{16,80},{32,96},{48,112},{64,128},{80,144},{96,160},{112,17... | collective-permute-start | bytes 393224 | tf_op jit(solution)/shard_map/ppermute | solution.py:209
  72.3 4.3 %copy-start.2 = (bf16[4,2,2,64,128]{4,3,2,1,0:T(8,128)(2,1)}, bf16[4,2,2,64,128]{4,3,2,1,0:T(8,128)(2,1)S(1)}, u32[]{:S(2)}) copy-start(bf16[4,2,2,64,128]{4,3,2,1,0:T(8,128)(2,1)S(1)} %collective-permute-done.9.refs_3_.refs_6_) | copy-start | bytes 786436
  72.4 18.9 %collective-permute-start.13 = (bf16[256,2048]{1,0:T(8,128)(2,1)S(1)}, bf16[256,2048]{1,0:T(8,128)(2,1)S(1)}, u32[]{:S(2)}, u32[]{:S(2)}) collective-permute-start(bf16[256,2048]{1,0:T(8,128)(2,1)S(1)} %stack.40.near), channel_id=1, source_target_pairs={{0,16},{16,0},{32,48},{48,32},{64,80},{80,64},{96,112},{112,96},{1... | collective-permute-start | bytes 3145736 | tf_op jit(solution)/shard_map/ppermute | solution.py:213
  78.1 13.2 %collective-permute-start.20 = (bf16[256,2048]{1,0:T(8,128)(2,1)S(1)}, bf16[256,2048]{1,0:T(8,128)(2,1)}, u32[]{:S(2)}, u32[]{:S(2)}) collective-permute-start(bf16[256,2048]{1,0:T(8,128)(2,1)S(1)} %stack.41.far), channel_id=1, source_target_pairs={{0,16},{16,0},{32,48},{48,32},{64,80},{80,64},{96,112},{112,96},{1... | collective-permute-start | bytes 3145736 | tf_op jit(solution)/shard_map/ppermute | solution.py:213
  82.5 1.0 copy-start.1
  83.4 0.9 copy-start.3
  84.4 0.9 copy-start.5

commit v2 on v0

v2 whole, which is shorter than its diff:
```python
import functools

import jax
import jax.numpy as jnp
from jax import lax
from jax.experimental import pallas as pl
from jax.experimental.pallas import tpu as pltpu
from jax.sharding import PartitionSpec as P

BF = jnp.bfloat16
VMEM = pl.BlockSpec(memory_space=pltpu.VMEM)
SMEM = pl.BlockSpec(memory_space=pltpu.SMEM)
ANY = pl.BlockSpec(memory_space=pl.ANY)


def struct(*shape):
    return jax.ShapeDtypeStruct(shape, BF)


def call(kernel, name, out_shape, in_specs, *operands, aliases={}, cost=None):
    return pl.pallas_call(
        kernel,
        out_shape=out_shape,
        input_output_aliases=aliases,
        in_specs=in_specs,
        out_specs=[VMEM] * len(out_shape) if isinstance(out_shape, list) else VMEM,
        compiler_params=pltpu.CompilerParams(vmem_limit_bytes=12 * 1024 * 1024),
        cost_estimate=cost,
        name=name,
    )(*operands)


def whiten_kernel(spectra, quality, white, spread):
    values = spectra[...].astype(jnp.float32)
    power = jnp.sum(jnp.sum(values * values, axis=0), axis=0) * (1.0 / 16.0)
    scale = lax.rsqrt(power + 1e-06)
    keep = jnp.broadcast_to(quality[...].astype(jnp.float32), (128, 64)).T
    result = (values * keep[None, None] * scale[None, None]).astype(BF)
    white[...] = result
    for h in range(4):
        for k in range(2):
            for z in range(2):
                for y in range(4):
                    spread[h, y, z, k] = result[2 * h + k, z, 16 * y : 16 * y + 16]


def whiten(spectra, quality):
    shapes = [struct(8, 2, 64, 128), struct(4, 4, 2, 2, 16, 128)]
    return call(whiten_kernel, "whiten", shapes, [VMEM] * 2, spectra, quality.reshape(1, 64))


def select_kernel(place, pieces, *outs):
    for d in range(4):
        group = place[0] ^ d
        for s in range(4):
            index = place[4 + group * 4 + s]
            for h in range(4):
                outs[d][16 * h : 16 * h + 16, 128 * s : 128 * s + 128] = pieces[h, index]


def select(place, pieces):
    return call(select_kernel, "select", [struct(64, 512)] * 4, [SMEM, VMEM], place, pieces)


def merge_kernel(place, *refs):
    out = refs[-1]
    for d in range(4):
        quarter = place[0] ^ d
        for s in range(4):
            at = pl.multiple_of(s * 512 + quarter * 128, 128)
            out[:, pl.ds(at, 128)] = refs[d][:, 128 * s : 128 * s + 128]


def merge(place, parts, after):
    specs = [SMEM] + [VMEM] * (4 + len(after))
    return call(merge_kernel, "merge", struct(64, 2048), specs, place, *parts, *after)


def relay_kernel(other, one, three, after, up, down):
    up[0:64] = other[...]
    up[64:96] = three[0:32]
    down[0:64] = other[...]
    down[64:96] = one[32:64]


def relay(*parts):
    return call(relay_kernel, "relay", [struct(96, 2048)] * 2, [VMEM] * 4, *parts)


def stack_kernel(*refs):
    out, at = refs[-1], 0
    for ref in refs[:-1]:
        rows = ref.shape[0]
        out[at : at + rows] = ref[...]
        at += rows


def stack(*parts):
    return call(stack_kernel, "stack", struct(256, 2048), [VMEM] * len(parts), *parts)


def hours_kernel(place, *refs):
    out = refs[-1]
    for d in range(4):
        hour = place[1] ^ d
        for i, dy in enumerate((0, 1, 3, 2)):
            at = pl.multiple_of(64 * i + hour * 16, 16)
            taken = pl.ds(pl.multiple_of((place[2] ^ dy) * 16, 16), 16)
            out[:, :, pl.ds(at, 16)] = refs[d][:, :, taken]


def hours(place, parts, after):
    specs = [SMEM] + [VMEM] * (4 + len(after))
    return call(hours_kernel, "hours", struct(2, 2, 256, 128), specs, place, *parts, *after)


WINDOWS = (
    (0, 0, 64), (1, 0, 64), (0, 64, 128), (0, 128, 192), (1, 64, 128),
    (0, 192, 224), (1, 128, 192), (0, 224, 256), (1, 192, 256),
)


def put_left(place, out, f, d, ref, ref_f):
    z = place[3]
    rows = ref[ref_f, z] * 0.0625, ref[ref_f, 1 - z] * 0.0625
    sign = jnp.where(z == 0, 1.0, -1.0)
    signed = (rows[1] * sign).astype(BF), (rows[0] * -sign).astype(BF)
    for part, of in enumerate((rows, signed)):
        ordered = jnp.concatenate([of[side][a:b] for side, a, b in WINDOWS], axis=0)
        out[f, part, 128 * d : 128 * d + 128] = ordered.T


def left_near_kernel(place, *refs):
    for d, ref in enumerate(refs[:3]):
        for f in range(2):
            put_left(place, refs[3], f, d, ref, f)


def left_near(place, *parts):
    return call(left_near_kernel, "left_near", struct(2, 2, 512, 512), [SMEM] + [VMEM] * 3, place, *parts)


def left_far_kernel(place, low, high, left, out):
    for f, ref in enumerate((low, high)):
        put_left(place, out, f, 3, ref, 0)


def left_far(place, *parts):
    cost = pl.CostEstimate(flops=50_000_000_000, bytes_accessed=1 << 20, transcendentals=0)
    specs, shape = [SMEM] + [VMEM] * 3, struct(2, 2, 512, 512)
    return call(left_far_kernel, "left_far", shape, specs, place, *parts, aliases={3: 0}, cost=cost)


WIDE, STRIPS = 512, 4


def product_kernel(place, left, *refs):
    out, held, sem = refs[4:]
    copies = []
    for n in range(2):
        near, far = refs[2 * n : 2 * n + 2]
        f = place[1] if n == 0 else 1 - place[1]
        both = left[f].reshape(1024, 512)
        for j in range(STRIPS):
            columns = slice(WIDE * j, WIDE * j + WIDE)
            right = jnp.concatenate([near[:, columns], far[:, columns]], axis=0)
            result = jnp.dot(both, right, preferred_element_type=jnp.float32)
            held[n, j] = result.astype(BF).reshape(2, 512, WIDE)
            for i, d in enumerate((0, 1, 3, 2)):
                rows = pl.ds(pl.multiple_of((place[0] ^ d) * 128, 128), 128)
                copy = pltpu.make_async_copy(
                    held.at[n, j, :, pl.ds(128 * i, 128)], out.at[f, :, rows, columns], sem.at[n, j, i]
                )
                copy.start()
                copies.append(copy)
    for copy in copies:
        copy.wait()


def product(*operands):
    return pl.pallas_call(
        product_kernel,
        out_shape=struct(2, 2, 512, 2048),
        in_specs=[SMEM] + [VMEM] * 5,
        out_specs=ANY,
        scratch_shapes=[
            pltpu.VMEM((2, STRIPS, 2, 512, WIDE), BF),
            pltpu.SemaphoreType.DMA((2, STRIPS, 4)),
        ],
        compiler_params=pltpu.CompilerParams(vmem_limit_bytes=16 * 1024 * 1024),
        name="product",
    )(*operands)


def swap(value, axis, bits):
    return lax.ppermute(value, axis, [(i, i ^ bits) for i in range(lax.axis_size(axis))])


def per_device(spectra, quality, column_blocks):
    row, col, hour = (lax.axis_index(a) for a in ("row", "col", "hour"))
    y, z, k = row // 4, (row // 2) % 2, row % 2
    place = jnp.concatenate([jnp.stack([col, hour, y, z]).astype(jnp.int32), column_blocks])
    white, spread = whiten(spectra, quality)
    parts = [lax.dynamic_slice_in_dim(white, 2 * (hour ^ d), 2, 0) for d in range(4)]
    parts = [parts[0]] + [swap(parts[d], "hour", d) for d in range(1, 4)]

    pieces = lax.all_to_all(spread.reshape(64, 16, 128), ("hour", "row"), 0, 0, tiled=True)
    sent = select(place, pieces.reshape(4, 16, 16, 128))
    sent = [sent[0]] + [swap(sent[d], "col", d) for d in range(1, 4)]
    own = merge(place, sent, parts[1:])

    other = swap(own, "row", 2)
    one = swap(own, "row", 4)
    three = swap(own, "row", 12)
    rows = hours(place, parts, [own])
    rows_one = swap(rows, "col", 1)
    rows_three = swap(rows, "col", 3)

    up, down = relay(other, one, three, rows)
    near = stack(own, other, one, three)
    up = swap(up, "row", 4)
    down = swap(down, "row", 12)
    other_two = swap(other, "row", 8)
    far_low = swap(rows_one[:1], "col", 3)
    far_high = swap(rows_three[1:], "col", 1)
    left = left_near(place, rows, rows_one, rows_three)
    up, down, other_two, left = lax.optimization_barrier((up, down, other_two, left))
    far = stack(up, down, other_two)
    near_core = swap(near, "row", 1)
    far_core = swap(far, "row", 1)

    bin_place = jnp.stack([col, k]).astype(jnp.int32)
    left = left_far(place, far_low, far_high, left)
    return product(bin_place, left, near, far, near_core, far_core)


def solution(mesh):
    return jax.shard_map(
        per_device,
        mesh=mesh,
        in_specs=(P(None, None, "hour", ("row", "col")), P("hour"), P()),
        out_specs=P("hour", None, "row", "col"),
        check_vma=False,
    )
```

time: 324 us -> 84.3 us (0.26)
  waiting for transfers between devices: 176 us -> 27.3 us
  matrix products: 64.3 us -> 0 us
  other arithmetic: 41 us -> 0.07 us
  starting transfers between devices: 0.04 us -> 39.1 us
  between operations: 16 us -> 0.32 us
  Pallas kernels: 0 us -> 12.8 us
  local copies, waits for them, and re-layouts: 16.1 us -> 3.67 us
  blocking collectives: 9.88 us -> 0 us
    psum x1 -> x0, waiting for transfers between devices: 138 us -> none  [spread(): return lax.psum(kept, axis)]
    dot_general x16 -> x0, matrix products: 64.3 us -> none  [the longest x4 21.8 us: products(): jnp.einsum('fwi,fwj->fij', left[:, 1], right[:, 1], preferred_element_typ...]
    all_gather x1 -> x0, waiting for transfers between devices: 37.5 us -> none  [per_device(): row_side = lax.all_gather(white, 'col', axis=3, tiled=True)]
    convert_element_type x7 -> x0, other arithmetic: 36.5 us -> none  [the longest x4 23.9 us: per_device(): part.astype(jnp.bfloat16)]
    ppermute x0 -> x18, starting transfers between devices: none -> 29.7 us  [swap(): lax.ppermute(value, axis, [(i, i ^ bits) for i in range(lax.axis_size(axi...]
    ppermute x0 -> x18, waiting for transfers between devices: none -> 23.4 us  [swap(): lax.ppermute(value, axis, [(i, i ^ bits) for i in range(lax.axis_size(axi...]
    pallas_call x0 -> x10, Pallas kernels: none -> 12.8 us  [the longest x1 7.53 us: product(): pl.pallas_call(product_kernel, out_shape=struct(2, 2, 512, 2048), in_spec...]
    all_to_all x1 -> x0, blocking collectives: 9.88 us -> none  [per_device(): lax.all_to_all(white, 'hour', split_axis=0, concat_axis=2, tiled=True)]
  transfers between devices with their start and end apart: 2 -> 19, of which waited for: 2 -> 7; matrix products, arithmetic and copies ran while one was open for 0% -> 3% of each run, Pallas kernels for 0% -> 4%
where the time goes in v2:
time: 84.3 us; the launch traced here: 83.3 us
  starting transfers between devices  39.1 us (46%)
  waiting for transfers between devices  27.3 us (32%)
  Pallas kernels  12.8 us (15%)
  local copies, waits for them, and re-layouts  3.67 us (4%)
    ppermute x18, starting transfers between devices, swap(): lax.ppermute(value, axis, [(i, i ^ bits) for i in range(lax.axis_size(axi...  29.7 us
    ppermute x18, waiting for transfers between devices, swap(): lax.ppermute(value, axis, [(i, i ^ bits) for i in range(lax.axis_size(axi...  23.4 us
    all_to_all x1, starting transfers between devices, per_device(): lax.all_to_all(spread.reshape(64, 16, 128), ('hour', 'row'), 0, 0, tiled=...  9.38 us
    pallas_call x1, Pallas kernels, product(): pl.pallas_call(product_kernel, out_shape=struct(2, 2, 512, 2048), in_spec...  7.53 us
    pallas_call x9, Pallas kernels, call(): pl.pallas_call(kernel, out_shape=out_shape, input_output_aliases=aliases,...  5.3 us
    all_to_all x1, waiting for transfers between devices, per_device(): lax.all_to_all(spread.reshape(64, 16, 128), ('hour', 'row'), 0, 0, tiled=...  3.92 us
  transfers between devices with their start and end apart: 19, of which 7 were waited for; matrix products, arithmetic and copies ran while one was open for 3% of the time, Pallas kernels for 4%

profile of v2, /device:TPU:2, one launch (start us, length us, event | category | flops | bytes accessed | tf_op | source)
XLA Modules:
  0.0 83.3 jit_solution(2613668519681375757)
XLA Ops:
  0.0 0.9 %copy-done = bf16[8,2,64,128]{3,2,1,0:T(8,128)(2,1)S(1)} copy-done((bf16[8,2,64,128]{3,2,1,0:T(8,128)(2,1)S(1)}, bf16[8,2,64,128]{3,2,1,0:T(8,128)(2,1)}, u32[]{:S(2)}) %copy-start) | copy-done | bytes 262168
  1.0 0.7 copy-done.1
  1.6 0.8 %whiten.1 = (bf16[8,2,64,128]{3,2,1,0:T(8,128)(2,1)S(1)}, bf16[4,4,2,2,16,128]{5,4,3,2,1,0:T(8,128)(2,1)}) custom-call(bf16[8,2,64,128]{3,2,1,0:T(8,128)(2,1)S(1)} %copy-done, s32[1,64]{1,0:T(1,128)S(1)} %bitcast.9), custom_call_target="tpu_custom_call" | custom-call | tf_op jit(solution)/shard_map/whiten/pallas_call | solution.py:21
  2.5 9.4 %all-to-all-start = ((bf16[64,16,128]{2,1,0:T(8,128)(2,1)}), bf16[64,16,128]{2,1,0:T(8,128)(2,1)S(1)}, u32[]{:S(2)}, u32[]{:S(2)}) async-start(bf16[64,16,128]{2,1,0:T(8,128)(2,1)} %bitcast.6), calls=%async_computation | async-start | bytes 524288 | tf_op jit(solution)/shard_map/all_to_all | solution.py:207
  11.9 1.6 %collective-permute-start.2 = (bf16[2,2,64,128]{3,2,1,0:T(8,128)(2,1)S(1)}, bf16[2,2,64,128]{3,2,1,0:T(8,128)(2,1)S(1)}, u32[]{:S(2)}, u32[]{:S(2)}) collective-permute-start(bf16[2,2,64,128]{3,2,1,0:T(8,128)(2,1)S(1)} %get-tuple-element.29), channel_id=1, source_target_pairs={{0,3},{1,2},{2,1},{3,0},{4,7},{5,6},{6,5},{7,4},{8,11},{9,10},{10,... | collective-permute-start | bytes 196616 | tf_op jit(solution)/shard_map/ppermute | solution.py:196
  13.5 1.0 %collective-permute-start.1 = (bf16[2,2,64,128]{3,2,1,0:T(8,128)(2,1)S(1)}, bf16[2,2,64,128]{3,2,1,0:T(8,128)(2,1)S(1)}, u32[]{:S(2)}, u32[]{:S(2)}) collective-permute-start(bf16[2,2,64,128]{3,2,1,0:T(8,128)(2,1)S(1)} %get-tuple-element.30), channel_id=1, source_target_pairs={{0,2},{1,3},{2,0},{3,1},{4,6},{5,7},{6,4},{7,5},{8,10},{9,11},{10,... | collective-permute-start | bytes 196616 | tf_op jit(solution)/shard_map/ppermute | solution.py:196
  14.5 1.6 %collective-permute-start = (bf16[2,2,64,128]{3,2,1,0:T(8,128)(2,1)S(1)}, bf16[2,2,64,128]{3,2,1,0:T(8,128)(2,1)S(1)}, u32[]{:S(2)}, u32[]{:S(2)}) collective-permute-start(bf16[2,2,64,128]{3,2,1,0:T(8,128)(2,1)S(1)} %get-tuple-element.31), channel_id=1, source_target_pairs={{0,1},{1,0},{2,3},{3,2},{4,5},{5,4},{6,7},{7,6},{8,9},{9,8},{10,11... | collective-permute-start | bytes 196616 | tf_op jit(solution)/shard_map/ppermute | solution.py:196
  16.1 0.7 concatenate.3.place
  16.8 3.9 %all-to-all-done = bf16[64,16,128]{2,1,0:T(8,128)(2,1)S(1)} async-done(((bf16[64,16,128]{2,1,0:T(8,128)(2,1)}), bf16[64,16,128]{2,1,0:T(8,128)(2,1)S(1)}, u32[]{:S(2)}, u32[]{:S(2)}) %all-to-all-start) | async-done | bytes 262176 | tf_op jit(solution)/shard_map/all_to_all | solution.py:207
  21.4 3.4 %collective-permute-start.3 = (bf16[64,512]{1,0:T(8,128)(2,1)S(1)}, bf16[64,512]{1,0:T(8,128)(2,1)S(1)}, u32[]{:S(2)}, u32[]{:S(2)}) collective-permute-start(bf16[64,512]{1,0:T(8,128)(2,1)S(1)} %get-tuple-element.20), channel_id=1, source_target_pairs={{0,4},{4,0},{8,12},{12,8},{1,5},{5,1},{9,13},{13,9},{2,6},{6,2},{1... | collective-permute-start | bytes 196616 | tf_op jit(solution)/shard_map/ppermute | solution.py:196
  24.7 4.5 %collective-permute-start.4 = (bf16[64,512]{1,0:T(8,128)(2,1)S(1)}, bf16[64,512]{1,0:T(8,128)(2,1)S(1)}, u32[]{:S(2)}, u32[]{:S(2)}) collective-permute-start(bf16[64,512]{1,0:T(8,128)(2,1)S(1)} %get-tuple-element.21), channel_id=1, source_target_pairs={{0,8},{4,12},{8,0},{12,4},{1,9},{5,13},{9,1},{13,5},{2,10},{6,14},... | collective-permute-start | bytes 196616 | tf_op jit(solution)/shard_map/ppermute | solution.py:196
  29.2 3.7 %collective-permute-done.4.refs_2_ = bf16[64,512]{1,0:T(8,128)(2,1)S(1)} collective-permute-done((bf16[64,512]{1,0:T(8,128)(2,1)S(1)}, bf16[64,512]{1,0:T(8,128)(2,1)S(1)}, u32[]{:S(2)}, u32[]{:S(2)}) %collective-permute-start.4) | collective-permute-done | bytes 65568 | tf_op jit(solution)/shard_map/ppermute | solution.py:196
  33.0 2.6 %collective-permute-done.5.refs_3_ = bf16[64,512]{1,0:T(8,128)(2,1)S(1)} collective-permute-done((bf16[64,512]{1,0:T(8,128)(2,1)S(1)}, bf16[64,512]{1,0:T(8,128)(2,1)S(1)}, u32[]{:S(2)}, u32[]{:S(2)}) %collective-permute-start.5) | collective-permute-done | bytes 65568 | tf_op jit(solution)/shard_map/ppermute | solution.py:196
  36.2 0.7 collective-permute-start.12
  37.0 1.8 %collective-permute-start.10 = (bf16[64,2048]{1,0:T(8,128)(2,1)S(1)}, bf16[64,2048]{1,0:T(8,128)(2,1)S(1)}, u32[]{:S(2)}, u32[]{:S(2)}) collective-permute-start(bf16[64,2048]{1,0:T(8,128)(2,1)S(1)} %merge.1.refs_4_.refs_0_), channel_id=1, source_target_pairs={{0,32},{16,48},{32,0},{48,16},{64,96},{80,112},{96,64},{112,80},{1... | collective-permute-start | bytes 786440 | tf_op jit(solution)/shard_map/ppermute | solution.py:196
  39.4 4.8 %collective-permute-done.12.three.refs_3_ = bf16[64,2048]{1,0:T(8,128)(2,1)S(1)} collective-permute-done((bf16[64,2048]{1,0:T(8,128)(2,1)S(1)}, bf16[64,2048]{1,0:T(8,128)(2,1)S(1)}, u32[]{:S(2)}, u32[]{:S(2)}) %collective-permute-start.12) | collective-permute-done | bytes 262176 | tf_op jit(solution)/shard_map/ppermute | solution.py:196
  44.3 0.8 relay.1
  45.1 1.1 %collective-permute-start.13 = (bf16[96,2048]{1,0:T(8,128)(2,1)}, bf16[96,2048]{1,0:T(8,128)(2,1)S(1)}, u32[]{:S(2)}, u32[]{:S(2)}) collective-permute-start(bf16[96,2048]{1,0:T(8,128)(2,1)} %get-tuple-element.23), channel_id=1, source_target_pairs={{0,64},{16,80},{32,96},{48,112},{64,0},{80,16},{96,32},{112,48},{1... | collective-permute-start | bytes 1179656 | tf_op jit(solution)/shard_map/ppermute | solution.py:196
  46.2 2.5 %collective-permute-start.14 = (bf16[96,2048]{1,0:T(8,128)(2,1)S(1)}, bf16[96,2048]{1,0:T(8,128)(2,1)S(1)}, u32[]{:S(2)}, u32[]{:S(2)}) collective-permute-start(bf16[96,2048]{1,0:T(8,128)(2,1)S(1)} %get-tuple-element.24), channel_id=1, source_target_pairs={{0,192},{16,208},{32,224},{48,240},{64,128},{80,144},{96,160},{112... | collective-permute-start | bytes 1179656 | tf_op jit(solution)/shard_map/ppermute | solution.py:196
  48.7 4.6 %collective-permute-start.8 = (bf16[2,2,256,128]{3,2,1,0:T(8,128)(2,1)S(1)}, bf16[2,2,256,128]{3,2,1,0:T(8,128)(2,1)S(1)}, u32[]{:S(2)}, u32[]{:S(2)}) collective-permute-start(bf16[2,2,256,128]{3,2,1,0:T(8,128)(2,1)S(1)} %hours.1.after.refs_0_), channel_id=1, source_target_pairs={{0,12},{4,8},{8,4},{12,0},{1,13},{5,9},{9,5},{13,1},{2,14},{6,10},... | collective-permute-start | bytes 786440 | tf_op jit(solution)/shard_map/ppermute | solution.py:196
  53.3 1.3 %collective-permute-start.15 = (bf16[64,2048]{1,0:T(8,128)(2,1)S(1)}, bf16[64,2048]{1,0:T(8,128)(2,1)S(1)}, u32[]{:S(2)}, u32[]{:S(2)}) collective-permute-start(bf16[64,2048]{1,0:T(8,128)(2,1)S(1)} %collective-permute-done.10.other.refs_1_), channel_id=1, source_target_pairs={{0,128},{16,144},{32,160},{48,176},{64,192},{80,208},{96,224},{112... | collective-permute-start | bytes 786440 | tf_op jit(solution)/shard_map/ppermute | solution.py:196
  54.6 8.0 %collective-permute-done.8.refs_2_ = bf16[2,2,256,128]{3,2,1,0:T(8,128)(2,1)S(1)} collective-permute-done((bf16[2,2,256,128]{3,2,1,0:T(8,128)(2,1)S(1)}, bf16[2,2,256,128]{3,2,1,0:T(8,128)(2,1)S(1)}, u32[]{:S(2)}, u32[]{:S(2)}) %collective-permute-start.8) | collective-permute-done | bytes 262176 | tf_op jit(solution)/shard_map/ppermute | solution.py:196
  62.6 0.7 slice.9
  63.3 3.4 %collective-permute-start.9 = (bf16[1,2,256,128]{3,2,1,0:T(8,128)(2,1)}, bf16[1,2,256,128]{3,2,1,0:T(8,128)(2,1)S(1)}, u32[]{:S(2)}, u32[]{:S(2)}) collective-permute-start(bf16[1,2,256,128]{3,2,1,0:T(8,128)(2,1)} %slice.9), channel_id=1, source_target_pairs={{0,4},{4,0},{8,12},{12,8},{1,5},{5,1},{9,13},{13,9},{2,6},{6,2},{1... | collective-permute-start | bytes 393224 | tf_op jit(solution)/shard_map/ppermute | solution.py:196
  66.7 0.6 slice.8
  67.4 1.1 %collective-permute-start.7 = (bf16[1,2,256,128]{3,2,1,0:T(8,128)(2,1)}, bf16[1,2,256,128]{3,2,1,0:T(8,128)(2,1)S(1)}, u32[]{:S(2)}, u32[]{:S(2)}) collective-permute-start(bf16[1,2,256,128]{3,2,1,0:T(8,128)(2,1)} %slice.8), channel_id=1, source_target_pairs={{0,12},{4,8},{8,4},{12,0},{1,13},{5,9},{9,5},{13,1},{2,14},{6,10},... | collective-permute-start | bytes 393224 | tf_op jit(solution)/shard_map/ppermute | solution.py:196
  68.7 1.0 %left_near.1.left = bf16[2,2,512,512]{3,2,1,0:T(8,128)(2,1)S(1)} custom-call(s32[20]{0:T(128)S(1)} %concatenate.3.place, bf16[2,2,256,128]{3,2,1,0:T(8,128)(2,1)S(1)} %hours.1.after.refs_0_, bf16[2,2,256,128]{3,2,1,0:T(8,128)(2,1)S(1)} %collective-permute-done.6.refs_1_, bf16[2,2,256,128]{3,2,1,0:T(8,128)(2,1)S(1)} %collective-permute-done.8.refs_2_), custom_call_target="tpu_custom_call" | custom-call | tf_op jit(solution)/shard_map/left_near/pallas_call | solution.py:21
  69.9 0.7 collective-permute-start.17
  70.7 1.4 %collective-permute-done.9.high = bf16[1,2,256,128]{3,2,1,0:T(8,128)(2,1)S(1)} collective-permute-done((bf16[1,2,256,128]{3,2,1,0:T(8,128)(2,1)}, bf16[1,2,256,128]{3,2,1,0:T(8,128)(2,1)S(1)}, u32[]{:S(2)}, u32[]{:S(2)}) %collective-permute-start.9) | collective-permute-done | bytes 131104 | tf_op jit(solution)/shard_map/ppermute | solution.py:196
  72.0 2.8 %collective-permute-done.7.low = bf16[1,2,256,128]{3,2,1,0:T(8,128)(2,1)S(1)} collective-permute-done((bf16[1,2,256,128]{3,2,1,0:T(8,128)(2,1)}, bf16[1,2,256,128]{3,2,1,0:T(8,128)(2,1)S(1)}, u32[]{:S(2)}, u32[]{:S(2)}) %collective-permute-start.7) | collective-permute-done | bytes 131104 | tf_op jit(solution)/shard_map/ppermute | solution.py:196
  74.8 0.7 left_far.1.left
  75.6 7.5 %product.1 = bf16[2,2,512,2048]{3,2,1,0:T(8,128)(2,1)} custom-call(s32[2]{0:T(128)S(1)} %pad_add_fusion.place, bf16[2,2,512,512]{3,2,1,0:T(8,128)(2,1)S(1)} %left_far.1.left, bf16[256,2048]{1,0:T(8,128)(2,1)S(1)} %stack.27.refs_0_, bf16[256,2048]{1,0:T(8,128)(2,1)S(1)} %stack.28.refs_1_, bf16[256,2048]{1,0:T(8,128)(2,1)S(1)} %collective-permute-done.16.refs_2_, ...), custom_call_target="tpu_custom_call" | custom-call | tf_op jit(solution)/shard_map/product/pallas_call | solution.py:181
  (25 shorter events, 2.3 us)
Async XLA Ops:
  0.0 0.9 %copy-start = (bf16[8,2,64,128]{3,2,1,0:T(8,128)(2,1)S(1)}, bf16[8,2,64,128]{3,2,1,0:T(8,128)(2,1)}, u32[]{:S(2)}) copy-start(bf16[8,2,64,128]{3,2,1,0:T(8,128)(2,1)} %spectra.1) | copy-start | bytes 786436
  1.0 0.7 copy-start.1
  2.5 18.3 %all-to-all-start = ((bf16[64,16,128]{2,1,0:T(8,128)(2,1)}), bf16[64,16,128]{2,1,0:T(8,128)(2,1)S(1)}, u32[]{:S(2)}, u32[]{:S(2)}) async-start(bf16[64,16,128]{2,1,0:T(8,128)(2,1)} %bitcast.6), calls=%async_computation | async-start | bytes 524288 | tf_op jit(solution)/shard_map/all_to_all | solution.py:207
  11.9 17.3 %collective-permute-start.2 = (bf16[2,2,64,128]{3,2,1,0:T(8,128)(2,1)S(1)}, bf16[2,2,64,128]{3,2,1,0:T(8,128)(2,1)S(1)}, u32[]{:S(2)}, u32[]{:S(2)}) collective-permute-start(bf16[2,2,64,128]{3,2,1,0:T(8,128)(2,1)S(1)} %get-tuple-element.29), channel_id=1, source_target_pairs={{0,3},{1,2},{2,1},{3,0},{4,7},{5,6},{6,5},{7,4},{8,11},{9,10},{10,... | collective-permute-start | bytes 196616 | tf_op jit(solution)/shard_map/ppermute | solution.py:196
  13.5 15.7 %collective-permute-start.1 = (bf16[2,2,64,128]{3,2,1,0:T(8,128)(2,1)S(1)}, bf16[2,2,64,128]{3,2,1,0:T(8,128)(2,1)S(1)}, u32[]{:S(2)}, u32[]{:S(2)}) collective-permute-start(bf16[2,2,64,128]{3,2,1,0:T(8,128)(2,1)S(1)} %get-tuple-element.30), channel_id=1, source_target_pairs={{0,2},{1,3},{2,0},{3,1},{4,6},{5,7},{6,4},{7,5},{8,10},{9,11},{10,... | collective-permute-start | bytes 196616 | tf_op jit(solution)/shard_map/ppermute | solution.py:196
  14.5 14.7 %collective-permute-start = (bf16[2,2,64,128]{3,2,1,0:T(8,128)(2,1)S(1)}, bf16[2,2,64,128]{3,2,1,0:T(8,128)(2,1)S(1)}, u32[]{:S(2)}, u32[]{:S(2)}) collective-permute-start(bf16[2,2,64,128]{3,2,1,0:T(8,128)(2,1)S(1)} %get-tuple-element.31), channel_id=1, source_target_pairs={{0,1},{1,0},{2,3},{3,2},{4,5},{5,4},{6,7},{7,6},{8,9},{9,8},{10,11... | collective-permute-start | bytes 196616 | tf_op jit(solution)/shard_map/ppermute | solution.py:196
  21.4 7.9 %collective-permute-start.3 = (bf16[64,512]{1,0:T(8,128)(2,1)S(1)}, bf16[64,512]{1,0:T(8,128)(2,1)S(1)}, u32[]{:S(2)}, u32[]{:S(2)}) collective-permute-start(bf16[64,512]{1,0:T(8,128)(2,1)S(1)} %get-tuple-element.20), channel_id=1, source_target_pairs={{0,4},{4,0},{8,12},{12,8},{1,5},{5,1},{9,13},{13,9},{2,6},{6,2},{1... | collective-permute-start | bytes 196616 | tf_op jit(solution)/shard_map/ppermute | solution.py:196
  24.7 8.2 %collective-permute-start.4 = (bf16[64,512]{1,0:T(8,128)(2,1)S(1)}, bf16[64,512]{1,0:T(8,128)(2,1)S(1)}, u32[]{:S(2)}, u32[]{:S(2)}) collective-permute-start(bf16[64,512]{1,0:T(8,128)(2,1)S(1)} %get-tuple-element.21), channel_id=1, source_target_pairs={{0,8},{4,12},{8,0},{12,4},{1,9},{5,13},{9,1},{13,5},{2,10},{6,14},... | collective-permute-start | bytes 196616 | tf_op jit(solution)/shard_map/ppermute | solution.py:196
  29.2 6.4 %collective-permute-start.5 = (bf16[64,512]{1,0:T(8,128)(2,1)S(1)}, bf16[64,512]{1,0:T(8,128)(2,1)S(1)}, u32[]{:S(2)}, u32[]{:S(2)}) collective-permute-start(bf16[64,512]{1,0:T(8,128)(2,1)S(1)} %get-tuple-element.22), channel_id=1, source_target_pairs={{0,12},{4,8},{8,4},{12,0},{1,13},{5,9},{9,5},{13,1},{2,14},{6,10},... | collective-permute-start | bytes 196616 | tf_op jit(solution)/shard_map/ppermute | solution.py:196
  36.2 8.1 %collective-permute-start.12 = (bf16[64,2048]{1,0:T(8,128)(2,1)S(1)}, bf16[64,2048]{1,0:T(8,128)(2,1)S(1)}, u32[]{:S(2)}, u32[]{:S(2)}) collective-permute-start(bf16[64,2048]{1,0:T(8,128)(2,1)S(1)} %merge.1.refs_4_.refs_0_), channel_id=1, source_target_pairs={{0,192},{16,208},{32,224},{48,240},{64,128},{80,144},{96,160},{112... | collective-permute-start | bytes 786440 | tf_op jit(solution)/shard_map/ppermute | solution.py:196
  36.9 7.4 %collective-permute-start.11 = (bf16[64,2048]{1,0:T(8,128)(2,1)S(1)}, bf16[64,2048]{1,0:T(8,128)(2,1)S(1)}, u32[]{:S(2)}, u32[]{:S(2)}) collective-permute-start(bf16[64,2048]{1,0:T(8,128)(2,1)S(1)} %merge.1.refs_4_.refs_0_), channel_id=1, source_target_pairs={{0,64},{16,80},{32,96},{48,112},{64,0},{80,16},{96,32},{112,48},{1... | collective-permute-start | bytes 786440 | tf_op jit(solution)/shard_map/ppermute | solution.py:196
  37.0 7.3 %collective-permute-start.10 = (bf16[64,2048]{1,0:T(8,128)(2,1)S(1)}, bf16[64,2048]{1,0:T(8,128)(2,1)S(1)}, u32[]{:S(2)}, u32[]{:S(2)}) collective-permute-start(bf16[64,2048]{1,0:T(8,128)(2,1)S(1)} %merge.1.refs_4_.refs_0_), channel_id=1, source_target_pairs={{0,32},{16,48},{32,0},{48,16},{64,96},{80,112},{96,64},{112,80},{1... | collective-permute-start | bytes 786440 | tf_op jit(solution)/shard_map/ppermute | solution.py:196
  45.1 24.7 %collective-permute-start.13 = (bf16[96,2048]{1,0:T(8,128)(2,1)}, bf16[96,2048]{1,0:T(8,128)(2,1)S(1)}, u32[]{:S(2)}, u32[]{:S(2)}) collective-permute-start(bf16[96,2048]{1,0:T(8,128)(2,1)} %get-tuple-element.23), channel_id=1, source_target_pairs={{0,64},{16,80},{32,96},{48,112},{64,0},{80,16},{96,32},{112,48},{1... | collective-permute-start | bytes 1179656 | tf_op jit(solution)/shard_map/ppermute | solution.py:196
  46.2 23.7 %collective-permute-start.14 = (bf16[96,2048]{1,0:T(8,128)(2,1)S(1)}, bf16[96,2048]{1,0:T(8,128)(2,1)S(1)}, u32[]{:S(2)}, u32[]{:S(2)}) collective-permute-start(bf16[96,2048]{1,0:T(8,128)(2,1)S(1)} %get-tuple-element.24), channel_id=1, source_target_pairs={{0,192},{16,208},{32,224},{48,240},{64,128},{80,144},{96,160},{112... | collective-permute-start | bytes 1179656 | tf_op jit(solution)/shard_map/ppermute | solution.py:196
  48.7 13.9 %collective-permute-start.8 = (bf16[2,2,256,128]{3,2,1,0:T(8,128)(2,1)S(1)}, bf16[2,2,256,128]{3,2,1,0:T(8,128)(2,1)S(1)}, u32[]{:S(2)}, u32[]{:S(2)}) collective-permute-start(bf16[2,2,256,128]{3,2,1,0:T(8,128)(2,1)S(1)} %hours.1.after.refs_0_), channel_id=1, source_target_pairs={{0,12},{4,8},{8,4},{12,0},{1,13},{5,9},{9,5},{13,1},{2,14},{6,10},... | collective-permute-start | bytes 786440 | tf_op jit(solution)/shard_map/ppermute | solution.py:196
  53.3 13.4 %collective-permute-start.6 = (bf16[2,2,256,128]{3,2,1,0:T(8,128)(2,1)S(1)}, bf16[2,2,256,128]{3,2,1,0:T(8,128)(2,1)S(1)}, u32[]{:S(2)}, u32[]{:S(2)}) collective-permute-start(bf16[2,2,256,128]{3,2,1,0:T(8,128)(2,1)S(1)} %hours.1.after.refs_0_), channel_id=1, source_target_pairs={{0,4},{4,0},{8,12},{12,8},{1,5},{5,1},{9,13},{13,9},{2,6},{6,2},{1... | collective-permute-start | bytes 786440 | tf_op jit(solution)/shard_map/ppermute | solution.py:196
  53.3 16.4 %collective-permute-start.15 = (bf16[64,2048]{1,0:T(8,128)(2,1)S(1)}, bf16[64,2048]{1,0:T(8,128)(2,1)S(1)}, u32[]{:S(2)}, u32[]{:S(2)}) collective-permute-start(bf16[64,2048]{1,0:T(8,128)(2,1)S(1)} %collective-permute-done.10.other.refs_1_), channel_id=1, source_target_pairs={{0,128},{16,144},{32,160},{48,176},{64,192},{80,208},{96,224},{112... | collective-permute-start | bytes 786440 | tf_op jit(solution)/shard_map/ppermute | solution.py:196
  63.3 8.7 %collective-permute-start.9 = (bf16[1,2,256,128]{3,2,1,0:T(8,128)(2,1)}, bf16[1,2,256,128]{3,2,1,0:T(8,128)(2,1)S(1)}, u32[]{:S(2)}, u32[]{:S(2)}) collective-permute-start(bf16[1,2,256,128]{3,2,1,0:T(8,128)(2,1)} %slice.9), channel_id=1, source_target_pairs={{0,4},{4,0},{8,12},{12,8},{1,5},{5,1},{9,13},{13,9},{2,6},{6,2},{1... | collective-permute-start | bytes 393224 | tf_op jit(solution)/shard_map/ppermute | solution.py:196
  67.4 7.4 %collective-permute-start.7 = (bf16[1,2,256,128]{3,2,1,0:T(8,128)(2,1)}, bf16[1,2,256,128]{3,2,1,0:T(8,128)(2,1)S(1)}, u32[]{:S(2)}, u32[]{:S(2)}) collective-permute-start(bf16[1,2,256,128]{3,2,1,0:T(8,128)(2,1)} %slice.8), channel_id=1, source_target_pairs={{0,12},{4,8},{8,4},{12,0},{1,13},{5,9},{9,5},{13,1},{2,14},{6,10},... | collective-permute-start | bytes 393224 | tf_op jit(solution)/shard_map/ppermute | solution.py:196
  69.7 5.9 %collective-permute-start.16 = (bf16[256,2048]{1,0:T(8,128)(2,1)S(1)}, bf16[256,2048]{1,0:T(8,128)(2,1)S(1)}, u32[]{:S(2)}, u32[]{:S(2)}) collective-permute-start(bf16[256,2048]{1,0:T(8,128)(2,1)S(1)} %stack.27.refs_0_), channel_id=1, source_target_pairs={{0,16},{16,0},{32,48},{48,32},{64,80},{80,64},{96,112},{112,96},{1... | collective-permute-start | bytes 3145736 | tf_op jit(solution)/shard_map/ppermute | solution.py:196
  69.9 5.7 %collective-permute-start.17 = (bf16[256,2048]{1,0:T(8,128)(2,1)S(1)}, bf16[256,2048]{1,0:T(8,128)(2,1)S(1)}, u32[]{:S(2)}, u32[]{:S(2)}) collective-permute-start(bf16[256,2048]{1,0:T(8,128)(2,1)S(1)} %stack.28.refs_1_), channel_id=1, source_target_pairs={{0,16},{16,0},{32,48},{48,32},{64,80},{80,64},{96,112},{112,96},{1... | collective-permute-start | bytes 3145736 | tf_op jit(solution)/shard_map/ppermute | solution.py:196

commit v3 on v2

--- a/solution.py
+++ b/solution.py
@@ -11,6 +11,11 @@
 VMEM = pl.BlockSpec(memory_space=pltpu.VMEM)
 SMEM = pl.BlockSpec(memory_space=pltpu.SMEM)
 ANY = pl.BlockSpec(memory_space=pl.ANY)
+
+
+def y_z_core():
+    row = lax.axis_index("row")
+    return row >> 2, (row >> 1) & 1, row & 1
 
 
 def struct(*shape):
@@ -24,7 +29,7 @@
         input_output_aliases=aliases,
         in_specs=in_specs,
         out_specs=[VMEM] * len(out_shape) if isinstance(out_shape, list) else VMEM,
-        compiler_params=pltpu.CompilerParams(vmem_limit_bytes=12 * 1024 * 1024),
+        compiler_params=pltpu.CompilerParams(vmem_limit_bytes=6 * 1024 * 1024),
         cost_estimate=cost,
         name=name,
     )(*operands)
@@ -53,7 +58,7 @@
     for d in range(4):
         group = place[0] ^ d
         for s in range(4):
-            index = place[4 + group * 4 + s]
+            index = place[1 + group * 4 + s]
             for h in range(4):
                 outs[d][16 * h : 16 * h + 16, 128 * s : 128 * s + 128] = pieces[h, index]
 
@@ -62,18 +67,18 @@
     return call(select_kernel, "select", [struct(64, 512)] * 4, [SMEM, VMEM], place, pieces)
 
 
-def merge_kernel(place, *refs):
-    out = refs[-1]
+def merge_kernel(*refs):
+    out, col = refs[-1], lax.axis_index("col")
     for d in range(4):
-        quarter = place[0] ^ d
+        quarter = col ^ d
         for s in range(4):
             at = pl.multiple_of(s * 512 + quarter * 128, 128)
             out[:, pl.ds(at, 128)] = refs[d][:, 128 * s : 128 * s + 128]
 
 
-def merge(place, parts, after):
-    specs = [SMEM] + [VMEM] * (4 + len(after))
-    return call(merge_kernel, "merge", struct(64, 2048), specs, place, *parts, *after)
+def merge(parts, after):
+    specs = [VMEM] * (4 + len(after))
+    return call(merge_kernel, "merge", struct(64, 2048), specs, *parts, *after)
 
 
 def relay_kernel(other, one, three, after, up, down):
@@ -99,19 +104,20 @@
     return call(stack_kernel, "stack", struct(256, 2048), [VMEM] * len(parts), *parts)
 
 
-def hours_kernel(place, *refs):
+def hours_kernel(*refs):
     out = refs[-1]
+    own_hour, y = lax.axis_index("hour"), y_z_core()[0]
     for d in range(4):
-        hour = place[1] ^ d
+        hour = own_hour ^ d
         for i, dy in enumerate((0, 1, 3, 2)):
             at = pl.multiple_of(64 * i + hour * 16, 16)
-            taken = pl.ds(pl.multiple_of((place[2] ^ dy) * 16, 16), 16)
+            taken = pl.ds(pl.multiple_of((y ^ dy) * 16, 16), 16)
             out[:, :, pl.ds(at, 16)] = refs[d][:, :, taken]
 
 
-def hours(place, parts, after):
-    specs = [SMEM] + [VMEM] * (4 + len(after))
-    return call(hours_kernel, "hours", struct(2, 2, 256, 128), specs, place, *parts, *after)
+def hours(parts, after):
+    specs = [VMEM] * (4 + len(after))
+    return call(hours_kernel, "hours", struct(2, 2, 256, 128), specs, *parts, *after)
 
 
 WINDOWS = (
@@ -120,8 +126,8 @@
 )
 
 
-def put_left(place, out, f, d, ref, ref_f):
-    z = place[3]
+def put_left(out, f, d, ref, ref_f):
+    z = y_z_core()[1]
     rows = ref[ref_f, z] * 0.0625, ref[ref_f, 1 - z] * 0.0625
     sign = jnp.where(z == 0, 1.0, -1.0)
     signed = (rows[1] * sign).astype(BF), (rows[0] * -sign).astype(BF)
@@ -130,36 +136,46 @@
         out[f, part, 128 * d : 128 * d + 128] = ordered.T
 
 
-def left_near_kernel(place, *refs):
+def left_near_kernel(*refs):
     for d, ref in enumerate(refs[:3]):
         for f in range(2):
-            put_left(place, refs[3], f, d, ref, f)
-
-
-def left_near(place, *parts):
-    return call(left_near_kernel, "left_near", struct(2, 2, 512, 512), [SMEM] + [VMEM] * 3, place, *parts)
-
-
-def left_far_kernel(place, low, high, left, out):
+            put_left(refs[3], f, d, ref, f)
+
+
+def left_near(*parts):
+    return call(left_near_kernel, "left_near", struct(2, 2, 512, 512), [VMEM] * 3, *parts)
+
+
+def halves_kernel(one, three, low, high):
+    low[0] = one[0]
+    high[0] = three[1]
+
+
+def halves(*parts):
+    cost = pl.CostEstimate(flops=4_000_000_000, bytes_accessed=1 << 20, transcendentals=0)
+    return call(halves_kernel, "halves", [struct(1, 2, 256, 128)] * 2, [VMEM] * 2, *parts, cost=cost)
+
+
+def left_far_kernel(low, high, left, out):
     for f, ref in enumerate((low, high)):
-        put_left(place, out, f, 3, ref, 0)
-
-
-def left_far(place, *parts):
+        put_left(out, f, 3, ref, 0)
+
+
+def left_far(*parts):
     cost = pl.CostEstimate(flops=50_000_000_000, bytes_accessed=1 << 20, transcendentals=0)
-    specs, shape = [SMEM] + [VMEM] * 3, struct(2, 2, 512, 512)
-    return call(left_far_kernel, "left_far", shape, specs, place, *parts, aliases={3: 0}, cost=cost)
+    return call(left_far_kernel, "left_far", struct(2, 2, 512, 512), [VMEM] * 3, *parts, aliases={2: 0}, cost=cost)
 
 
 WIDE, STRIPS = 512, 4
 
 
-def product_kernel(place, left, *refs):
+def product_kernel(left, *refs):
+    col, core = lax.axis_index("col"), y_z_core()[2]
     out, held, sem = refs[4:]
     copies = []
     for n in range(2):
         near, far = refs[2 * n : 2 * n + 2]
-        f = place[1] if n == 0 else 1 - place[1]
+        f = core ^ n
         both = left[f].reshape(1024, 512)
         for j in range(STRIPS):
             columns = slice(WIDE * j, WIDE * j + WIDE)
@@ -167,7 +183,7 @@
             result = jnp.dot(both, right, preferred_element_type=jnp.float32)
             held[n, j] = result.astype(BF).reshape(2, 512, WIDE)
             for i, d in enumerate((0, 1, 3, 2)):
-                rows = pl.ds(pl.multiple_of((place[0] ^ d) * 128, 128), 128)
+                rows = pl.ds(pl.multiple_of((col ^ d) * 128, 128), 128)
                 copy = pltpu.make_async_copy(
                     held.at[n, j, :, pl.ds(128 * i, 128)], out.at[f, :, rows, columns], sem.at[n, j, i]
                 )
@@ -181,7 +197,7 @@
     return pl.pallas_call(
         product_kernel,
         out_shape=struct(2, 2, 512, 2048),
-        in_specs=[SMEM] + [VMEM] * 5,
+        in_specs=[VMEM] * 5,
         out_specs=ANY,
         scratch_shapes=[
             pltpu.VMEM((2, STRIPS, 2, 512, WIDE), BF),
@@ -197,9 +213,8 @@
 
 
 def per_device(spectra, quality, column_blocks):
-    row, col, hour = (lax.axis_index(a) for a in ("row", "col", "hour"))
-    y, z, k = row // 4, (row // 2) % 2, row % 2
-    place = jnp.concatenate([jnp.stack([col, hour, y, z]).astype(jnp.int32), column_blocks])
+    col, hour = lax.axis_index("col"), lax.axis_index("hour")
+    place = jnp.concatenate([col.astype(jnp.int32).reshape(1), column_blocks])
     white, spread = whiten(spectra, quality)
     parts = [lax.dynamic_slice_in_dim(white, 2 * (hour ^ d), 2, 0) for d in range(4)]
     parts = [parts[0]] + [swap(parts[d], "hour", d) for d in range(1, 4)]
@@ -207,12 +222,12 @@
     pieces = lax.all_to_all(spread.reshape(64, 16, 128), ("hour", "row"), 0, 0, tiled=True)
     sent = select(place, pieces.reshape(4, 16, 16, 128))
     sent = [sent[0]] + [swap(sent[d], "col", d) for d in range(1, 4)]
-    own = merge(place, sent, parts[1:])
+    own = merge(sent, parts[1:])
 
     other = swap(own, "row", 2)
     one = swap(own, "row", 4)
     three = swap(own, "row", 12)
-    rows = hours(place, parts, [own])
+    rows = hours(parts, [own])
     rows_one = swap(rows, "col", 1)
     rows_three = swap(rows, "col", 3)
 
@@ -221,17 +236,17 @@
     up = swap(up, "row", 4)
     down = swap(down, "row", 12)
     other_two = swap(other, "row", 8)
-    far_low = swap(rows_one[:1], "col", 3)
-    far_high = swap(rows_three[1:], "col", 1)
-    left = left_near(place, rows, rows_one, rows_three)
+    far_low, far_high = halves(rows_one, rows_three)
+    far_low = swap(far_low, "col", 3)
+    far_high = swap(far_high, "col", 1)
+    left = left_near(rows, rows_one, rows_three)
     up, down, other_two, left = lax.optimization_barrier((up, down, other_two, left))
     far = stack(up, down, other_two)
     near_core = swap(near, "row", 1)
     far_core = swap(far, "row", 1)
 
-    bin_place = jnp.stack([col, k]).astype(jnp.int32)
-    left = left_far(place, far_low, far_high, left)
-    return product(bin_place, left, near, far, near_core, far_core)
+    left = left_far(far_low, far_high, left)
+    return product(left, near, far, near_core, far_core)
 
 
 def solution(mesh):

time: 84.3 us -> 78.2 us (0.928)
  the two profiles are of different devices: /device:TPU:2 before, /device:TPU:67 now
where the time goes in v3:
time: 78.2 us; the launch traced here: 78 us
  starting transfers between devices  39 us (50%)
  waiting for transfers between devices  27 us (35%)
  Pallas kernels  9.34 us (12%)
  local copies, waits for them, and re-layouts  1.63 us (2%)
    ppermute x18, starting transfers between devices, swap(): lax.ppermute(value, axis, [(i, i ^ bits) for i in range(lax.axis_size(axi...  29.3 us
    ppermute x18, waiting for transfers between devices, swap(): lax.ppermute(value, axis, [(i, i ^ bits) for i in range(lax.axis_size(axi...  22.3 us
    all_to_all x1, starting transfers between devices, per_device(): lax.all_to_all(spread.reshape(64, 16, 128), ('hour', 'row'), 0, 0, tiled=...  9.7 us
    pallas_call x1, Pallas kernels, product(): pl.pallas_call(product_kernel, out_shape=struct(2, 2, 512, 2048), in_spec...  6.91 us
    all_to_all x1, waiting for transfers between devices, per_device(): lax.all_to_all(spread.reshape(64, 16, 128), ('hour', 'row'), 0, 0, tiled=...  4.73 us
    pallas_call x10, Pallas kernels, call(): pl.pallas_call(kernel, out_shape=out_shape, input_output_aliases=aliases,...  2.43 us
    unnamed x4, local copies, waits for them, and re-layouts  1.6 us
  transfers between devices with their start and end apart: 19, of which 8 were waited for; matrix products, arithmetic and copies ran while one was open for 1% of the time, Pallas kernels for 2%

profile of v3, /device:TPU:67, one launch (start us, length us, event | category | flops | bytes accessed | tf_op | source)
XLA Modules:
  0.0 78.0 jit_solution(3149014013230988442)
XLA Ops:
  0.0 0.9 %copy-done = bf16[8,2,64,128]{3,2,1,0:T(8,128)(2,1)S(1)} copy-done((bf16[8,2,64,128]{3,2,1,0:T(8,128)(2,1)S(1)}, bf16[8,2,64,128]{3,2,1,0:T(8,128)(2,1)}, u32[]{:S(2)}) %copy-start) | copy-done | bytes 262168
  1.0 0.7 copy-done.1
  1.6 0.8 %whiten.1 = (bf16[8,2,64,128]{3,2,1,0:T(8,128)(2,1)S(1)}, bf16[4,4,2,2,16,128]{5,4,3,2,1,0:T(8,128)(2,1)}) custom-call(bf16[8,2,64,128]{3,2,1,0:T(8,128)(2,1)S(1)} %copy-done, s32[1,64]{1,0:T(1,128)S(1)} %bitcast.5), custom_call_target="tpu_custom_call" | custom-call | tf_op jit(solution)/shard_map/whiten/pallas_call | solution.py:26
  2.5 9.7 %all-to-all-start = ((bf16[64,16,128]{2,1,0:T(8,128)(2,1)}), bf16[64,16,128]{2,1,0:T(8,128)(2,1)S(1)}, u32[]{:S(2)}, u32[]{:S(2)}) async-start(bf16[64,16,128]{2,1,0:T(8,128)(2,1)} %bitcast.2), calls=%async_computation | async-start | bytes 524288 | tf_op jit(solution)/shard_map/all_to_all | solution.py:222
  12.2 1.4 %collective-permute-start.2 = (bf16[2,2,64,128]{3,2,1,0:T(8,128)(2,1)S(1)}, bf16[2,2,64,128]{3,2,1,0:T(8,128)(2,1)S(1)}, u32[]{:S(2)}, u32[]{:S(2)}) collective-permute-start(bf16[2,2,64,128]{3,2,1,0:T(8,128)(2,1)S(1)} %get-tuple-element.33), channel_id=1, source_target_pairs={{0,3},{1,2},{2,1},{3,0},{4,7},{5,6},{6,5},{7,4},{8,11},{9,10},{10,... | collective-permute-start | bytes 196616 | tf_op jit(solution)/shard_map/ppermute | solution.py:212
  13.6 0.8 %collective-permute-start.1 = (bf16[2,2,64,128]{3,2,1,0:T(8,128)(2,1)S(1)}, bf16[2,2,64,128]{3,2,1,0:T(8,128)(2,1)S(1)}, u32[]{:S(2)}, u32[]{:S(2)}) collective-permute-start(bf16[2,2,64,128]{3,2,1,0:T(8,128)(2,1)S(1)} %get-tuple-element.34), channel_id=1, source_target_pairs={{0,2},{1,3},{2,0},{3,1},{4,6},{5,7},{6,4},{7,5},{8,10},{9,11},{10,... | collective-permute-start | bytes 196616 | tf_op jit(solution)/shard_map/ppermute | solution.py:212
  14.4 1.2 %collective-permute-start = (bf16[2,2,64,128]{3,2,1,0:T(8,128)(2,1)S(1)}, bf16[2,2,64,128]{3,2,1,0:T(8,128)(2,1)S(1)}, u32[]{:S(2)}, u32[]{:S(2)}) collective-permute-start(bf16[2,2,64,128]{3,2,1,0:T(8,128)(2,1)S(1)} %get-tuple-element.35), channel_id=1, source_target_pairs={{0,1},{1,0},{2,3},{3,2},{4,5},{5,4},{6,7},{7,6},{8,9},{9,8},{10,11... | collective-permute-start | bytes 196616 | tf_op jit(solution)/shard_map/ppermute | solution.py:212
  15.6 0.7 pad_add_fusion.place
  16.3 4.7 %all-to-all-done = bf16[64,16,128]{2,1,0:T(8,128)(2,1)S(1)} async-done(((bf16[64,16,128]{2,1,0:T(8,128)(2,1)}), bf16[64,16,128]{2,1,0:T(8,128)(2,1)S(1)}, u32[]{:S(2)}, u32[]{:S(2)}) %all-to-all-start) | async-done | bytes 262176 | tf_op jit(solution)/shard_map/all_to_all | solution.py:222
  21.0 0.6 select.1
  21.7 5.4 %collective-permute-start.4 = (bf16[64,512]{1,0:T(8,128)(2,1)S(1)}, bf16[64,512]{1,0:T(8,128)(2,1)S(1)}, u32[]{:S(2)}, u32[]{:S(2)}) collective-permute-start(bf16[64,512]{1,0:T(8,128)(2,1)S(1)} %get-tuple-element.23), channel_id=1, source_target_pairs={{0,8},{4,12},{8,0},{12,4},{1,9},{5,13},{9,1},{13,5},{2,10},{6,14},... | collective-permute-start | bytes 196616 | tf_op jit(solution)/shard_map/ppermute | solution.py:212
  27.1 0.3 collective-permute-start.5
  27.4 2.9 %collective-permute-done.4.refs_2_ = bf16[64,512]{1,0:T(8,128)(2,1)S(1)} collective-permute-done((bf16[64,512]{1,0:T(8,128)(2,1)S(1)}, bf16[64,512]{1,0:T(8,128)(2,1)S(1)}, u32[]{:S(2)}, u32[]{:S(2)}) %collective-permute-start.4) | collective-permute-done | bytes 65568 | tf_op jit(solution)/shard_map/ppermute | solution.py:212
  30.3 4.4 %collective-permute-done.5.refs_3_ = bf16[64,512]{1,0:T(8,128)(2,1)S(1)} collective-permute-done((bf16[64,512]{1,0:T(8,128)(2,1)S(1)}, bf16[64,512]{1,0:T(8,128)(2,1)S(1)}, u32[]{:S(2)}, u32[]{:S(2)}) %collective-permute-start.5) | collective-permute-done | bytes 65568 | tf_op jit(solution)/shard_map/ppermute | solution.py:212
  34.8 0.1 collective-permute-start.12
  34.9 0.1 collective-permute-start.11
  35.0 0.1 collective-permute-start.10
  35.2 4.1 %collective-permute-start.7 = (bf16[2,2,256,128]{3,2,1,0:T(8,128)(2,1)S(1)}, bf16[2,2,256,128]{3,2,1,0:T(8,128)(2,1)S(1)}, u32[]{:S(2)}, u32[]{:S(2)}) collective-permute-start(bf16[2,2,256,128]{3,2,1,0:T(8,128)(2,1)S(1)} %hours.1.after.refs_0_), channel_id=1, source_target_pairs={{0,12},{4,8},{8,4},{12,0},{1,13},{5,9},{9,5},{13,1},{2,14},{6,10},... | collective-permute-start | bytes 786440 | tf_op jit(solution)/shard_map/ppermute | solution.py:212
  39.2 4.1 %collective-permute-done.12.three.refs_3_ = bf16[64,2048]{1,0:T(8,128)(2,1)S(1)} collective-permute-done((bf16[64,2048]{1,0:T(8,128)(2,1)S(1)}, bf16[64,2048]{1,0:T(8,128)(2,1)S(1)}, u32[]{:S(2)}, u32[]{:S(2)}) %collective-permute-start.12) | collective-permute-done | bytes 262176 | tf_op jit(solution)/shard_map/ppermute | solution.py:212
  43.3 4.1 %collective-permute-done.10.other.refs_1_ = bf16[64,2048]{1,0:T(8,128)(2,1)S(1)} collective-permute-done((bf16[64,2048]{1,0:T(8,128)(2,1)S(1)}, bf16[64,2048]{1,0:T(8,128)(2,1)S(1)}, u32[]{:S(2)}, u32[]{:S(2)}) %collective-permute-start.10) | collective-permute-done | bytes 262176 | tf_op jit(solution)/shard_map/ppermute | solution.py:212
  47.4 1.2 %collective-permute-start.13 = (bf16[96,2048]{1,0:T(8,128)(2,1)S(1)}, bf16[96,2048]{1,0:T(8,128)(2,1)S(1)}, u32[]{:S(2)}, u32[]{:S(2)}) collective-permute-start(bf16[96,2048]{1,0:T(8,128)(2,1)S(1)} %get-tuple-element.27), channel_id=1, source_target_pairs={{0,64},{16,80},{32,96},{48,112},{64,0},{80,16},{96,32},{112,48},{1... | collective-permute-start | bytes 1179656 | tf_op jit(solution)/shard_map/ppermute | solution.py:212
  48.6 2.8 %collective-permute-start.14 = (bf16[96,2048]{1,0:T(8,128)(2,1)S(1)}, bf16[96,2048]{1,0:T(8,128)(2,1)S(1)}, u32[]{:S(2)}, u32[]{:S(2)}) collective-permute-start(bf16[96,2048]{1,0:T(8,128)(2,1)S(1)} %get-tuple-element.28), channel_id=1, source_target_pairs={{0,192},{16,208},{32,224},{48,240},{64,128},{80,144},{96,160},{112... | collective-permute-start | bytes 1179656 | tf_op jit(solution)/shard_map/ppermute | solution.py:212
  51.4 4.0 %collective-permute-start.8 = (bf16[1,2,256,128]{3,2,1,0:T(8,128)(2,1)S(1)}, bf16[1,2,256,128]{3,2,1,0:T(8,128)(2,1)S(1)}, u32[]{:S(2)}, u32[]{:S(2)}) collective-permute-start(bf16[1,2,256,128]{3,2,1,0:T(8,128)(2,1)S(1)} %get-tuple-element.25), channel_id=1, source_target_pairs={{0,12},{4,8},{8,4},{12,0},{1,13},{5,9},{9,5},{13,1},{2,14},{6,10},... | collective-permute-start | bytes 393224 | tf_op jit(solution)/shard_map/ppermute | solution.py:212
  55.4 2.8 %collective-permute-start.9 = (bf16[1,2,256,128]{3,2,1,0:T(8,128)(2,1)S(1)}, bf16[1,2,256,128]{3,2,1,0:T(8,128)(2,1)S(1)}, u32[]{:S(2)}, u32[]{:S(2)}) collective-permute-start(bf16[1,2,256,128]{3,2,1,0:T(8,128)(2,1)S(1)} %get-tuple-element.26), channel_id=1, source_target_pairs={{0,4},{4,0},{8,12},{12,8},{1,5},{5,1},{9,13},{13,9},{2,6},{6,2},{1... | collective-permute-start | bytes 393224 | tf_op jit(solution)/shard_map/ppermute | solution.py:212
  58.3 0.5 left_near.1.left
  58.8 4.0 %collective-permute-done.15.refs_2_ = bf16[64,2048]{1,0:T(8,128)(2,1)S(1)} collective-permute-done((bf16[64,2048]{1,0:T(8,128)(2,1)S(1)}, bf16[64,2048]{1,0:T(8,128)(2,1)S(1)}, u32[]{:S(2)}, u32[]{:S(2)}) %collective-permute-start.15) | collective-permute-done | bytes 262176 | tf_op jit(solution)/shard_map/ppermute | solution.py:212
  62.8 4.4 %collective-permute-start.16 = (bf16[256,2048]{1,0:T(8,128)(2,1)S(1)}, bf16[256,2048]{1,0:T(8,128)(2,1)S(1)}, u32[]{:S(2)}, u32[]{:S(2)}) collective-permute-start(bf16[256,2048]{1,0:T(8,128)(2,1)S(1)} %stack.2.refs_0_), channel_id=1, source_target_pairs={{0,16},{16,0},{32,48},{48,32},{64,80},{80,64},{96,112},{112,96},{1... | collective-permute-start | bytes 3145736 | tf_op jit(solution)/shard_map/ppermute | solution.py:212
  67.2 0.7 collective-permute-start.17
  67.9 0.2 left_far.1.left
  68.1 1.3 %collective-permute-done.16.refs_2_ = bf16[256,2048]{1,0:T(8,128)(2,1)S(1)} collective-permute-done((bf16[256,2048]{1,0:T(8,128)(2,1)S(1)}, bf16[256,2048]{1,0:T(8,128)(2,1)S(1)}, u32[]{:S(2)}, u32[]{:S(2)}) %collective-permute-start.16) | collective-permute-done | bytes 1048608 | tf_op jit(solution)/shard_map/ppermute | solution.py:212
  69.4 1.5 %collective-permute-done.17.refs_3_ = bf16[256,2048]{1,0:T(8,128)(2,1)S(1)} collective-permute-done((bf16[256,2048]{1,0:T(8,128)(2,1)S(1)}, bf16[256,2048]{1,0:T(8,128)(2,1)S(1)}, u32[]{:S(2)}, u32[]{:S(2)}) %collective-permute-start.17) | collective-permute-done | bytes 1048608 | tf_op jit(solution)/shard_map/ppermute | solution.py:212
  70.9 6.9 %product.1 = bf16[2,2,512,2048]{3,2,1,0:T(8,128)(2,1)} custom-call(bf16[2,2,512,512]{3,2,1,0:T(8,128)(2,1)S(1)} %left_far.1.left, bf16[256,2048]{1,0:T(8,128)(2,1)S(1)} %stack.2.refs_0_, bf16[256,2048]{1,0:T(8,128)(2,1)S(1)} %stack.3.refs_1_, bf16[256,2048]{1,0:T(8,128)(2,1)S(1)} %collective-permute-done.16.refs_2_, ...), custom_call_target="tpu_custom_call" | custom-call | tf_op jit(solution)/shard_map/product/pallas_call | solution.py:197
  (23 shorter events, 0.5 us)
Async XLA Ops:
  0.0 0.9 %copy-start = (bf16[8,2,64,128]{3,2,1,0:T(8,128)(2,1)S(1)}, bf16[8,2,64,128]{3,2,1,0:T(8,128)(2,1)}, u32[]{:S(2)}) copy-start(bf16[8,2,64,128]{3,2,1,0:T(8,128)(2,1)} %spectra.1) | copy-start | bytes 786436
  1.0 0.7 copy-start.1
  2.5 18.6 %all-to-all-start = ((bf16[64,16,128]{2,1,0:T(8,128)(2,1)}), bf16[64,16,128]{2,1,0:T(8,128)(2,1)S(1)}, u32[]{:S(2)}, u32[]{:S(2)}) async-start(bf16[64,16,128]{2,1,0:T(8,128)(2,1)} %bitcast.2), calls=%async_computation | async-start | bytes 524288 | tf_op jit(solution)/shard_map/all_to_all | solution.py:222
  12.2 14.9 %collective-permute-start.2 = (bf16[2,2,64,128]{3,2,1,0:T(8,128)(2,1)S(1)}, bf16[2,2,64,128]{3,2,1,0:T(8,128)(2,1)S(1)}, u32[]{:S(2)}, u32[]{:S(2)}) collective-permute-start(bf16[2,2,64,128]{3,2,1,0:T(8,128)(2,1)S(1)} %get-tuple-element.33), channel_id=1, source_target_pairs={{0,3},{1,2},{2,1},{3,0},{4,7},{5,6},{6,5},{7,4},{8,11},{9,10},{10,... | collective-permute-start | bytes 196616 | tf_op jit(solution)/shard_map/ppermute | solution.py:212
  13.6 13.8 %collective-permute-start.1 = (bf16[2,2,64,128]{3,2,1,0:T(8,128)(2,1)S(1)}, bf16[2,2,64,128]{3,2,1,0:T(8,128)(2,1)S(1)}, u32[]{:S(2)}, u32[]{:S(2)}) collective-permute-start(bf16[2,2,64,128]{3,2,1,0:T(8,128)(2,1)S(1)} %get-tuple-element.34), channel_id=1, source_target_pairs={{0,2},{1,3},{2,0},{3,1},{4,6},{5,7},{6,4},{7,5},{8,10},{9,11},{10,... | collective-permute-start | bytes 196616 | tf_op jit(solution)/shard_map/ppermute | solution.py:212
  14.4 13.0 %collective-permute-start = (bf16[2,2,64,128]{3,2,1,0:T(8,128)(2,1)S(1)}, bf16[2,2,64,128]{3,2,1,0:T(8,128)(2,1)S(1)}, u32[]{:S(2)}, u32[]{:S(2)}) collective-permute-start(bf16[2,2,64,128]{3,2,1,0:T(8,128)(2,1)S(1)} %get-tuple-element.35), channel_id=1, source_target_pairs={{0,1},{1,0},{2,3},{3,2},{4,5},{5,4},{6,7},{7,6},{8,9},{9,8},{10,11... | collective-permute-start | bytes 196616 | tf_op jit(solution)/shard_map/ppermute | solution.py:212
  21.6 5.8 %collective-permute-start.3 = (bf16[64,512]{1,0:T(8,128)(2,1)S(1)}, bf16[64,512]{1,0:T(8,128)(2,1)S(1)}, u32[]{:S(2)}, u32[]{:S(2)}) collective-permute-start(bf16[64,512]{1,0:T(8,128)(2,1)S(1)} %get-tuple-element.22), channel_id=1, source_target_pairs={{0,4},{4,0},{8,12},{12,8},{1,5},{5,1},{9,13},{13,9},{2,6},{6,2},{1... | collective-permute-start | bytes 196616 | tf_op jit(solution)/shard_map/ppermute | solution.py:212
  21.7 8.6 %collective-permute-start.4 = (bf16[64,512]{1,0:T(8,128)(2,1)S(1)}, bf16[64,512]{1,0:T(8,128)(2,1)S(1)}, u32[]{:S(2)}, u32[]{:S(2)}) collective-permute-start(bf16[64,512]{1,0:T(8,128)(2,1)S(1)} %get-tuple-element.23), channel_id=1, source_target_pairs={{0,8},{4,12},{8,0},{12,4},{1,9},{5,13},{9,1},{13,5},{2,10},{6,14},... | collective-permute-start | bytes 196616 | tf_op jit(solution)/shard_map/ppermute | solution.py:212
  27.1 7.6 %collective-permute-start.5 = (bf16[64,512]{1,0:T(8,128)(2,1)S(1)}, bf16[64,512]{1,0:T(8,128)(2,1)S(1)}, u32[]{:S(2)}, u32[]{:S(2)}) collective-permute-start(bf16[64,512]{1,0:T(8,128)(2,1)S(1)} %get-tuple-element.24), channel_id=1, source_target_pairs={{0,12},{4,8},{8,4},{12,0},{1,13},{5,9},{9,5},{13,1},{2,14},{6,10},... | collective-permute-start | bytes 196616 | tf_op jit(solution)/shard_map/ppermute | solution.py:212
  34.8 8.5 %collective-permute-start.12 = (bf16[64,2048]{1,0:T(8,128)(2,1)S(1)}, bf16[64,2048]{1,0:T(8,128)(2,1)S(1)}, u32[]{:S(2)}, u32[]{:S(2)}) collective-permute-start(bf16[64,2048]{1,0:T(8,128)(2,1)S(1)} %merge.1.refs_4_.refs_0_), channel_id=1, source_target_pairs={{0,192},{16,208},{32,224},{48,240},{64,128},{80,144},{96,160},{112... | collective-permute-start | bytes 786440 | tf_op jit(solution)/shard_map/ppermute | solution.py:212
  34.9 8.4 %collective-permute-start.11 = (bf16[64,2048]{1,0:T(8,128)(2,1)S(1)}, bf16[64,2048]{1,0:T(8,128)(2,1)S(1)}, u32[]{:S(2)}, u32[]{:S(2)}) collective-permute-start(bf16[64,2048]{1,0:T(8,128)(2,1)S(1)} %merge.1.refs_4_.refs_0_), channel_id=1, source_target_pairs={{0,64},{16,80},{32,96},{48,112},{64,0},{80,16},{96,32},{112,48},{1... | collective-permute-start | bytes 786440 | tf_op jit(solution)/shard_map/ppermute | solution.py:212
  35.0 12.4 %collective-permute-start.10 = (bf16[64,2048]{1,0:T(8,128)(2,1)S(1)}, bf16[64,2048]{1,0:T(8,128)(2,1)S(1)}, u32[]{:S(2)}, u32[]{:S(2)}) collective-permute-start(bf16[64,2048]{1,0:T(8,128)(2,1)S(1)} %merge.1.refs_4_.refs_0_), channel_id=1, source_target_pairs={{0,32},{16,48},{32,0},{48,16},{64,96},{80,112},{96,64},{112,80},{1... | collective-permute-start | bytes 786440 | tf_op jit(solution)/shard_map/ppermute | solution.py:212
  35.2 16.2 %collective-permute-start.7 = (bf16[2,2,256,128]{3,2,1,0:T(8,128)(2,1)S(1)}, bf16[2,2,256,128]{3,2,1,0:T(8,128)(2,1)S(1)}, u32[]{:S(2)}, u32[]{:S(2)}) collective-permute-start(bf16[2,2,256,128]{3,2,1,0:T(8,128)(2,1)S(1)} %hours.1.after.refs_0_), channel_id=1, source_target_pairs={{0,12},{4,8},{8,4},{12,0},{1,13},{5,9},{9,5},{13,1},{2,14},{6,10},... | collective-permute-start | bytes 786440 | tf_op jit(solution)/shard_map/ppermute | solution.py:212
  39.2 12.2 %collective-permute-start.6 = (bf16[2,2,256,128]{3,2,1,0:T(8,128)(2,1)S(1)}, bf16[2,2,256,128]{3,2,1,0:T(8,128)(2,1)S(1)}, u32[]{:S(2)}, u32[]{:S(2)}) collective-permute-start(bf16[2,2,256,128]{3,2,1,0:T(8,128)(2,1)S(1)} %hours.1.after.refs_0_), channel_id=1, source_target_pairs={{0,4},{4,0},{8,12},{12,8},{1,5},{5,1},{9,13},{13,9},{2,6},{6,2},{1... | collective-permute-start | bytes 786440 | tf_op jit(solution)/shard_map/ppermute | solution.py:212
  47.4 19.8 %collective-permute-start.13 = (bf16[96,2048]{1,0:T(8,128)(2,1)S(1)}, bf16[96,2048]{1,0:T(8,128)(2,1)S(1)}, u32[]{:S(2)}, u32[]{:S(2)}) collective-permute-start(bf16[96,2048]{1,0:T(8,128)(2,1)S(1)} %get-tuple-element.27), channel_id=1, source_target_pairs={{0,64},{16,80},{32,96},{48,112},{64,0},{80,16},{96,32},{112,48},{1... | collective-permute-start | bytes 1179656 | tf_op jit(solution)/shard_map/ppermute | solution.py:212
  48.6 18.6 %collective-permute-start.14 = (bf16[96,2048]{1,0:T(8,128)(2,1)S(1)}, bf16[96,2048]{1,0:T(8,128)(2,1)S(1)}, u32[]{:S(2)}, u32[]{:S(2)}) collective-permute-start(bf16[96,2048]{1,0:T(8,128)(2,1)S(1)} %get-tuple-element.28), channel_id=1, source_target_pairs={{0,192},{16,208},{32,224},{48,240},{64,128},{80,144},{96,160},{112... | collective-permute-start | bytes 1179656 | tf_op jit(solution)/shard_map/ppermute | solution.py:212
  51.4 11.4 %collective-permute-start.15 = (bf16[64,2048]{1,0:T(8,128)(2,1)S(1)}, bf16[64,2048]{1,0:T(8,128)(2,1)S(1)}, u32[]{:S(2)}, u32[]{:S(2)}) collective-permute-start(bf16[64,2048]{1,0:T(8,128)(2,1)S(1)} %collective-permute-done.10.other.refs_1_), channel_id=1, source_target_pairs={{0,128},{16,144},{32,160},{48,176},{64,192},{80,208},{96,224},{112... | collective-permute-start | bytes 786440 | tf_op jit(solution)/shard_map/ppermute | solution.py:212
  51.4 16.5 %collective-permute-start.8 = (bf16[1,2,256,128]{3,2,1,0:T(8,128)(2,1)S(1)}, bf16[1,2,256,128]{3,2,1,0:T(8,128)(2,1)S(1)}, u32[]{:S(2)}, u32[]{:S(2)}) collective-permute-start(bf16[1,2,256,128]{3,2,1,0:T(8,128)(2,1)S(1)} %get-tuple-element.25), channel_id=1, source_target_pairs={{0,12},{4,8},{8,4},{12,0},{1,13},{5,9},{9,5},{13,1},{2,14},{6,10},... | collective-permute-start | bytes 393224 | tf_op jit(solution)/shard_map/ppermute | solution.py:212
  55.4 12.5 %collective-permute-start.9 = (bf16[1,2,256,128]{3,2,1,0:T(8,128)(2,1)S(1)}, bf16[1,2,256,128]{3,2,1,0:T(8,128)(2,1)S(1)}, u32[]{:S(2)}, u32[]{:S(2)}) collective-permute-start(bf16[1,2,256,128]{3,2,1,0:T(8,128)(2,1)S(1)} %get-tuple-element.26), channel_id=1, source_target_pairs={{0,4},{4,0},{8,12},{12,8},{1,5},{5,1},{9,13},{13,9},{2,6},{6,2},{1... | collective-permute-start | bytes 393224 | tf_op jit(solution)/shard_map/ppermute | solution.py:212
  62.8 6.6 %collective-permute-start.16 = (bf16[256,2048]{1,0:T(8,128)(2,1)S(1)}, bf16[256,2048]{1,0:T(8,128)(2,1)S(1)}, u32[]{:S(2)}, u32[]{:S(2)}) collective-permute-start(bf16[256,2048]{1,0:T(8,128)(2,1)S(1)} %stack.2.refs_0_), channel_id=1, source_target_pairs={{0,16},{16,0},{32,48},{48,32},{64,80},{80,64},{96,112},{112,96},{1... | collective-permute-start | bytes 3145736 | tf_op jit(solution)/shard_map/ppermute | solution.py:212
  67.2 3.7 %collective-permute-start.17 = (bf16[256,2048]{1,0:T(8,128)(2,1)S(1)}, bf16[256,2048]{1,0:T(8,128)(2,1)S(1)}, u32[]{:S(2)}, u32[]{:S(2)}) collective-permute-start(bf16[256,2048]{1,0:T(8,128)(2,1)S(1)} %stack.3.refs_1_), channel_id=1, source_target_pairs={{0,16},{16,0},{32,48},{48,32},{64,80},{80,64},{96,112},{112,96},{1... | collective-permute-start | bytes 3145736 | tf_op jit(solution)/shard_map/ppermute | solution.py:212

commit v4 on v3

--- a/solution.py
+++ b/solution.py
@@ -46,11 +46,11 @@
         for k in range(2):
             for z in range(2):
                 for y in range(4):
-                    spread[h, y, z, k] = result[2 * h + k, z, 16 * y : 16 * y + 16]
+                    spread[y, z, k, h] = result[2 * h + k, z, 16 * y : 16 * y + 16]
 
 
 def whiten(spectra, quality):
-    shapes = [struct(8, 2, 64, 128), struct(4, 4, 2, 2, 16, 128)]
+    shapes = [struct(8, 2, 64, 128), struct(4, 2, 2, 4, 16, 128)]
     return call(whiten_kernel, "whiten", shapes, [VMEM] * 2, spectra, quality.reshape(1, 64))
 
 
@@ -60,7 +60,7 @@
         for s in range(4):
             index = place[1 + group * 4 + s]
             for h in range(4):
-                outs[d][16 * h : 16 * h + 16, 128 * s : 128 * s + 128] = pieces[h, index]
+                outs[d][16 * h : 16 * h + 16, 128 * s : 128 * s + 128] = pieces[index, h]
 
 
 def select(place, pieces):
@@ -81,7 +81,7 @@
     return call(merge_kernel, "merge", struct(64, 2048), specs, *parts, *after)
 
 
-def relay_kernel(other, one, three, after, up, down):
+def relay_kernel(three, one, other, after, up, down):
     up[0:64] = other[...]
     up[64:96] = three[0:32]
     down[0:64] = other[...]
@@ -101,7 +101,8 @@
 
 
 def stack(*parts):
-    return call(stack_kernel, "stack", struct(256, 2048), [VMEM] * len(parts), *parts)
+    shape = struct(sum(part.shape[0] for part in parts), 2048)
+    return call(stack_kernel, "stack", shape, [VMEM] * len(parts), *parts)
 
 
 def hours_kernel(*refs):
@@ -121,8 +122,8 @@
 
 
 WINDOWS = (
-    (0, 0, 64), (1, 0, 64), (0, 64, 128), (0, 128, 192), (1, 64, 128),
-    (0, 192, 224), (1, 128, 192), (0, 224, 256), (1, 192, 256),
+    (0, 0, 64), (1, 0, 64), (0, 64, 128), (0, 128, 192), (1, 192, 256),
+    (1, 64, 128), (0, 192, 224), (1, 128, 192), (0, 224, 256),
 )
 
 
@@ -169,41 +170,36 @@
 WIDE, STRIPS = 512, 4
 
 
-def product_kernel(left, *refs):
-    col, core = lax.axis_index("col"), y_z_core()[2]
-    out, held, sem = refs[4:]
+def product_kernel(other, left, near, far, *refs):
+    out, held, sem = refs[-3:]
+    col, f = lax.axis_index("col"), y_z_core()[2] ^ other
     copies = []
-    for n in range(2):
-        near, far = refs[2 * n : 2 * n + 2]
-        f = core ^ n
-        both = left[f].reshape(1024, 512)
-        for j in range(STRIPS):
-            columns = slice(WIDE * j, WIDE * j + WIDE)
-            right = jnp.concatenate([near[:, columns], far[:, columns]], axis=0)
-            result = jnp.dot(both, right, preferred_element_type=jnp.float32)
-            held[n, j] = result.astype(BF).reshape(2, 512, WIDE)
-            for i, d in enumerate((0, 1, 3, 2)):
-                rows = pl.ds(pl.multiple_of((col ^ d) * 128, 128), 128)
-                copy = pltpu.make_async_copy(
-                    held.at[n, j, :, pl.ds(128 * i, 128)], out.at[f, :, rows, columns], sem.at[n, j, i]
-                )
-                copy.start()
-                copies.append(copy)
+    both = left[f].reshape(1024, 512)
+    for j in range(STRIPS):
+        columns = slice(WIDE * j, WIDE * j + WIDE)
+        right = jnp.concatenate([near[:, columns], far[:, columns]], axis=0)
+        result = jnp.dot(both, right, preferred_element_type=jnp.float32)
+        held[j] = result.astype(BF).reshape(2, 512, WIDE)
+        for i, d in enumerate((0, 1, 3, 2)):
+            rows = pl.ds(pl.multiple_of((col ^ d) * 128, 128), 128)
+            copy = pltpu.make_async_copy(
+                held.at[j, :, pl.ds(128 * i, 128)], out.at[f, :, rows, columns], sem.at[j, i]
+            )
+            copy.start()
+            copies.append(copy)
     for copy in copies:
         copy.wait()
 
 
-def product(*operands):
+def product(other, *operands):
     return pl.pallas_call(
-        product_kernel,
+        functools.partial(product_kernel, other),
         out_shape=struct(2, 2, 512, 2048),
-        in_specs=[VMEM] * 5,
+        in_specs=[VMEM] * 3 + [ANY] * other,
         out_specs=ANY,
-        scratch_shapes=[
-            pltpu.VMEM((2, STRIPS, 2, 512, WIDE), BF),
-            pltpu.SemaphoreType.DMA((2, STRIPS, 4)),
-        ],
-        compiler_params=pltpu.CompilerParams(vmem_limit_bytes=16 * 1024 * 1024),
+        input_output_aliases={3: 0} if other else {},
+        scratch_shapes=[pltpu.VMEM((STRIPS, 2, 512, WIDE), BF), pltpu.SemaphoreType.DMA((STRIPS, 4))],
+        compiler_params=pltpu.CompilerParams(vmem_limit_bytes=10 * 1024 * 1024),
         name="product",
     )(*operands)
 
@@ -219,20 +215,19 @@
     parts = [lax.dynamic_slice_in_dim(white, 2 * (hour ^ d), 2, 0) for d in range(4)]
     parts = [parts[0]] + [swap(parts[d], "hour", d) for d in range(1, 4)]
 
-    pieces = lax.all_to_all(spread.reshape(64, 16, 128), ("hour", "row"), 0, 0, tiled=True)
-    sent = select(place, pieces.reshape(4, 16, 16, 128))
+    pieces = lax.all_to_all(spread.reshape(64, 16, 128), ("row", "hour"), 0, 0, tiled=True)
+    sent = select(place, pieces.reshape(16, 4, 16, 128))
     sent = [sent[0]] + [swap(sent[d], "col", d) for d in range(1, 4)]
     own = merge(sent, parts[1:])
 
+    three = swap(own, "row", 12)
+    one = swap(own, "row", 4)
     other = swap(own, "row", 2)
-    one = swap(own, "row", 4)
-    three = swap(own, "row", 12)
     rows = hours(parts, [own])
     rows_one = swap(rows, "col", 1)
     rows_three = swap(rows, "col", 3)
 
-    up, down = relay(other, one, three, rows)
-    near = stack(own, other, one, three)
+    up, down = relay(three, one, other, rows)
     up = swap(up, "row", 4)
     down = swap(down, "row", 12)
     other_two = swap(other, "row", 8)
@@ -240,13 +235,15 @@
     far_low = swap(far_low, "col", 3)
     far_high = swap(far_high, "col", 1)
     left = left_near(rows, rows_one, rows_three)
-    up, down, other_two, left = lax.optimization_barrier((up, down, other_two, left))
-    far = stack(up, down, other_two)
+    up, down, left = lax.optimization_barrier((up, down, left))
+    near = stack(own, other, one, three, other_two)
+    far = stack(up, down)
     near_core = swap(near, "row", 1)
     far_core = swap(far, "row", 1)
 
     left = left_far(far_low, far_high, left)
-    return product(left, near, far, near_core, far_core)
+    out = product(0, left, near, far)
+    return product(1, left, near_core, far_core, out)
 
 
 def solution(mesh):

time: 78.2 us -> 74.9 us (0.958)
  the two profiles are of different devices: /device:TPU:67 before, /device:TPU:2 now
where the time goes in v4:
time: 74.9 us; the launch traced here: 74.7 us
  starting transfers between devices  36.4 us (49%)
  waiting for transfers between devices  25.3 us (34%)
  Pallas kernels  10.3 us (14%)
  local copies, waits for them, and re-layouts  1.63 us (2%)
    ppermute x18, starting transfers between devices, swap(): lax.ppermute(value, axis, [(i, i ^ bits) for i in range(lax.axis_size(axi...  27 us
    ppermute x18, waiting for transfers between devices, swap(): lax.ppermute(value, axis, [(i, i ^ bits) for i in range(lax.axis_size(axi...  21.3 us
    all_to_all x1, starting transfers between devices, per_device(): lax.all_to_all(spread.reshape(64, 16, 128), ('row', 'hour'), 0, 0, tiled=...  9.37 us
    pallas_call x2, Pallas kernels, product(): pl.pallas_call(functools.partial(product_kernel, other), out_shape=struct...  7.92 us
    all_to_all x1, waiting for transfers between devices, per_device(): lax.all_to_all(spread.reshape(64, 16, 128), ('row', 'hour'), 0, 0, tiled=...  3.98 us
    pallas_call x10, Pallas kernels, call(): pl.pallas_call(kernel, out_shape=out_shape, input_output_aliases=aliases,...  2.4 us
    unnamed x4, local copies, waits for them, and re-layouts  1.6 us
  transfers between devices with their start and end apart: 19, of which 9 were waited for; matrix products, arithmetic and copies ran while one was open for 1% of the time, Pallas kernels for 7%

profile of v4, /device:TPU:2, one launch (start us, length us, event | category | flops | bytes accessed | tf_op | source)
XLA Modules:
  0.0 74.7 jit_solution(6492453547188695429)
XLA Ops:
  0.0 0.9 %copy-done = bf16[8,2,64,128]{3,2,1,0:T(8,128)(2,1)S(1)} copy-done((bf16[8,2,64,128]{3,2,1,0:T(8,128)(2,1)S(1)}, bf16[8,2,64,128]{3,2,1,0:T(8,128)(2,1)}, u32[]{:S(2)}) %copy-start) | copy-done | bytes 262168
  1.0 0.7 copy-done.1
  1.6 0.8 %whiten.1 = (bf16[8,2,64,128]{3,2,1,0:T(8,128)(2,1)S(1)}, bf16[4,2,2,4,16,128]{5,4,3,2,1,0:T(8,128)(2,1)}) custom-call(bf16[8,2,64,128]{3,2,1,0:T(8,128)(2,1)S(1)} %copy-done, s32[1,64]{1,0:T(1,128)S(1)} %bitcast.5), custom_call_target="tpu_custom_call" | custom-call | tf_op jit(solution)/shard_map/whiten/pallas_call | solution.py:26
  2.5 9.4 %all-to-all-start = ((bf16[64,16,128]{2,1,0:T(8,128)(2,1)}), bf16[64,16,128]{2,1,0:T(8,128)(2,1)S(1)}, u32[]{:S(2)}, u32[]{:S(2)}) async-start(bf16[64,16,128]{2,1,0:T(8,128)(2,1)} %bitcast.2), calls=%async_computation | async-start | bytes 524288 | tf_op jit(solution)/shard_map/all_to_all | solution.py:218
  11.9 1.6 %collective-permute-start.2 = (bf16[2,2,64,128]{3,2,1,0:T(8,128)(2,1)S(1)}, bf16[2,2,64,128]{3,2,1,0:T(8,128)(2,1)S(1)}, u32[]{:S(2)}, u32[]{:S(2)}) collective-permute-start(bf16[2,2,64,128]{3,2,1,0:T(8,128)(2,1)S(1)} %get-tuple-element.31), channel_id=1, source_target_pairs={{0,3},{1,2},{2,1},{3,0},{4,7},{5,6},{6,5},{7,4},{8,11},{9,10},{10,... | collective-permute-start | bytes 196616 | tf_op jit(solution)/shard_map/ppermute | solution.py:208
  13.4 1.1 %collective-permute-start.1 = (bf16[2,2,64,128]{3,2,1,0:T(8,128)(2,1)S(1)}, bf16[2,2,64,128]{3,2,1,0:T(8,128)(2,1)S(1)}, u32[]{:S(2)}, u32[]{:S(2)}) collective-permute-start(bf16[2,2,64,128]{3,2,1,0:T(8,128)(2,1)S(1)} %get-tuple-element.32), channel_id=1, source_target_pairs={{0,2},{1,3},{2,0},{3,1},{4,6},{5,7},{6,4},{7,5},{8,10},{9,11},{10,... | collective-permute-start | bytes 196616 | tf_op jit(solution)/shard_map/ppermute | solution.py:208
  14.5 1.6 %collective-permute-start = (bf16[2,2,64,128]{3,2,1,0:T(8,128)(2,1)S(1)}, bf16[2,2,64,128]{3,2,1,0:T(8,128)(2,1)S(1)}, u32[]{:S(2)}, u32[]{:S(2)}) collective-permute-start(bf16[2,2,64,128]{3,2,1,0:T(8,128)(2,1)S(1)} %get-tuple-element.33), channel_id=1, source_target_pairs={{0,1},{1,0},{2,3},{3,2},{4,5},{5,4},{6,7},{7,6},{8,9},{9,8},{10,11... | collective-permute-start | bytes 196616 | tf_op jit(solution)/shard_map/ppermute | solution.py:208
  16.1 0.7 pad_add_fusion.place
  16.8 4.0 %all-to-all-done = bf16[64,16,128]{2,1,0:T(8,128)(2,1)S(1)} async-done(((bf16[64,16,128]{2,1,0:T(8,128)(2,1)}), bf16[64,16,128]{2,1,0:T(8,128)(2,1)S(1)}, u32[]{:S(2)}, u32[]{:S(2)}) %all-to-all-start) | async-done | bytes 262176 | tf_op jit(solution)/shard_map/all_to_all | solution.py:218
  20.8 0.6 select.1
  21.4 3.4 %collective-permute-start.3 = (bf16[64,512]{1,0:T(8,128)(2,1)S(1)}, bf16[64,512]{1,0:T(8,128)(2,1)S(1)}, u32[]{:S(2)}, u32[]{:S(2)}) collective-permute-start(bf16[64,512]{1,0:T(8,128)(2,1)S(1)} %get-tuple-element.21), channel_id=1, source_target_pairs={{0,4},{4,0},{8,12},{12,8},{1,5},{5,1},{9,13},{13,9},{2,6},{6,2},{1... | collective-permute-start | bytes 196616 | tf_op jit(solution)/shard_map/ppermute | solution.py:208
  24.7 4.5 %collective-permute-start.4 = (bf16[64,512]{1,0:T(8,128)(2,1)S(1)}, bf16[64,512]{1,0:T(8,128)(2,1)S(1)}, u32[]{:S(2)}, u32[]{:S(2)}) collective-permute-start(bf16[64,512]{1,0:T(8,128)(2,1)S(1)} %get-tuple-element.22), channel_id=1, source_target_pairs={{0,8},{4,12},{8,0},{12,4},{1,9},{5,13},{9,1},{13,5},{2,10},{6,14},... | collective-permute-start | bytes 196616 | tf_op jit(solution)/shard_map/ppermute | solution.py:208
  29.3 3.7 %collective-permute-done.4.refs_2_ = bf16[64,512]{1,0:T(8,128)(2,1)S(1)} collective-permute-done((bf16[64,512]{1,0:T(8,128)(2,1)S(1)}, bf16[64,512]{1,0:T(8,128)(2,1)S(1)}, u32[]{:S(2)}, u32[]{:S(2)}) %collective-permute-start.4) | collective-permute-done | bytes 65568 | tf_op jit(solution)/shard_map/ppermute | solution.py:208
  33.0 2.7 %collective-permute-done.5.refs_3_ = bf16[64,512]{1,0:T(8,128)(2,1)S(1)} collective-permute-done((bf16[64,512]{1,0:T(8,128)(2,1)S(1)}, bf16[64,512]{1,0:T(8,128)(2,1)S(1)}, u32[]{:S(2)}, u32[]{:S(2)}) %collective-permute-start.5) | collective-permute-done | bytes 65568 | tf_op jit(solution)/shard_map/ppermute | solution.py:208
  35.7 1.7 %collective-permute-start.12 = (bf16[64,2048]{1,0:T(8,128)(2,1)S(1)}, bf16[64,2048]{1,0:T(8,128)(2,1)S(1)}, u32[]{:S(2)}, u32[]{:S(2)}) collective-permute-start(bf16[64,2048]{1,0:T(8,128)(2,1)S(1)} %merge.1.refs_4_.refs_0_), channel_id=1, source_target_pairs={{0,32},{16,48},{32,0},{48,16},{64,96},{80,112},{96,64},{112,80},{1... | collective-permute-start | bytes 786440 | tf_op jit(solution)/shard_map/ppermute | solution.py:208
  37.3 0.4 collective-permute-start.11
  37.8 1.0 %collective-permute-start.10 = (bf16[64,2048]{1,0:T(8,128)(2,1)S(1)}, bf16[64,2048]{1,0:T(8,128)(2,1)S(1)}, u32[]{:S(2)}, u32[]{:S(2)}) collective-permute-start(bf16[64,2048]{1,0:T(8,128)(2,1)S(1)} %merge.1.refs_4_.refs_0_), channel_id=1, source_target_pairs={{0,192},{16,208},{32,224},{48,240},{64,128},{80,144},{96,160},{112... | collective-permute-start | bytes 786440 | tf_op jit(solution)/shard_map/ppermute | solution.py:208
  38.8 1.9 %collective-permute-start.7 = (bf16[2,2,256,128]{3,2,1,0:T(8,128)(2,1)S(1)}, bf16[2,2,256,128]{3,2,1,0:T(8,128)(2,1)S(1)}, u32[]{:S(2)}, u32[]{:S(2)}) collective-permute-start(bf16[2,2,256,128]{3,2,1,0:T(8,128)(2,1)S(1)} %hours.1.after.refs_0_), channel_id=1, source_target_pairs={{0,12},{4,8},{8,4},{12,0},{1,13},{5,9},{9,5},{13,1},{2,14},{6,10},... | collective-permute-start | bytes 786440 | tf_op jit(solution)/shard_map/ppermute | solution.py:208
  40.8 2.6 %collective-permute-start.6 = (bf16[2,2,256,128]{3,2,1,0:T(8,128)(2,1)S(1)}, bf16[2,2,256,128]{3,2,1,0:T(8,128)(2,1)S(1)}, u32[]{:S(2)}, u32[]{:S(2)}) collective-permute-start(bf16[2,2,256,128]{3,2,1,0:T(8,128)(2,1)S(1)} %hours.1.after.refs_0_), channel_id=1, source_target_pairs={{0,4},{4,0},{8,12},{12,8},{1,5},{5,1},{9,13},{13,9},{2,6},{6,2},{1... | collective-permute-start | bytes 786440 | tf_op jit(solution)/shard_map/ppermute | solution.py:208
  43.4 5.8 %collective-permute-done.12.other.refs_1_ = bf16[64,2048]{1,0:T(8,128)(2,1)S(1)} collective-permute-done((bf16[64,2048]{1,0:T(8,128)(2,1)S(1)}, bf16[64,2048]{1,0:T(8,128)(2,1)S(1)}, u32[]{:S(2)}, u32[]{:S(2)}) %collective-permute-start.12) | collective-permute-done | bytes 262176 | tf_op jit(solution)/shard_map/ppermute | solution.py:208
  49.4 4.0 %collective-permute-start.15 = (bf16[64,2048]{1,0:T(8,128)(2,1)S(1)}, bf16[64,2048]{1,0:T(8,128)(2,1)S(1)}, u32[]{:S(2)}, u32[]{:S(2)}) collective-permute-start(bf16[64,2048]{1,0:T(8,128)(2,1)S(1)} %collective-permute-done.12.other.refs_1_), channel_id=1, source_target_pairs={{0,128},{16,144},{32,160},{48,176},{64,192},{80,208},{96,224},{112... | collective-permute-start | bytes 786440 | tf_op jit(solution)/shard_map/ppermute | solution.py:208
  53.4 2.9 %collective-permute-done.7.three.refs_2_ = bf16[2,2,256,128]{3,2,1,0:T(8,128)(2,1)S(1)} collective-permute-done((bf16[2,2,256,128]{3,2,1,0:T(8,128)(2,1)S(1)}, bf16[2,2,256,128]{3,2,1,0:T(8,128)(2,1)S(1)}, u32[]{:S(2)}, u32[]{:S(2)}) %collective-permute-start.7) | collective-permute-done | bytes 262176 | tf_op jit(solution)/shard_map/ppermute | solution.py:208
  56.3 2.8 %collective-permute-start.8 = (bf16[1,2,256,128]{3,2,1,0:T(8,128)(2,1)S(1)}, bf16[1,2,256,128]{3,2,1,0:T(8,128)(2,1)S(1)}, u32[]{:S(2)}, u32[]{:S(2)}) collective-permute-start(bf16[1,2,256,128]{3,2,1,0:T(8,128)(2,1)S(1)} %get-tuple-element.24), channel_id=1, source_target_pairs={{0,12},{4,8},{8,4},{12,0},{1,13},{5,9},{9,5},{13,1},{2,14},{6,10},... | collective-permute-start | bytes 393224 | tf_op jit(solution)/shard_map/ppermute | solution.py:208
  59.1 0.5 left_near.1.left
  59.6 0.6 collective-permute-done.15.refs_4_
  60.4 2.0 %collective-permute-done.14.refs_1_ = bf16[96,2048]{1,0:T(8,128)(2,1)S(1)} collective-permute-done((bf16[96,2048]{1,0:T(8,128)(2,1)S(1)}, bf16[96,2048]{1,0:T(8,128)(2,1)S(1)}, u32[]{:S(2)}, u32[]{:S(2)}) %collective-permute-start.14) | collective-permute-done | bytes 393248 | tf_op jit(solution)/shard_map/ppermute | solution.py:208
  62.5 0.3 collective-permute-start.17
  62.7 2.6 %collective-permute-done.8.low = bf16[1,2,256,128]{3,2,1,0:T(8,128)(2,1)S(1)} collective-permute-done((bf16[1,2,256,128]{3,2,1,0:T(8,128)(2,1)S(1)}, bf16[1,2,256,128]{3,2,1,0:T(8,128)(2,1)S(1)}, u32[]{:S(2)}, u32[]{:S(2)}) %collective-permute-start.8) | collective-permute-done | bytes 131104 | tf_op jit(solution)/shard_map/ppermute | solution.py:208
  65.3 1.1 %collective-permute-done.9.high = bf16[1,2,256,128]{3,2,1,0:T(8,128)(2,1)S(1)} collective-permute-done((bf16[1,2,256,128]{3,2,1,0:T(8,128)(2,1)S(1)}, bf16[1,2,256,128]{3,2,1,0:T(8,128)(2,1)S(1)}, u32[]{:S(2)}, u32[]{:S(2)}) %collective-permute-start.9) | collective-permute-done | bytes 131104 | tf_op jit(solution)/shard_map/ppermute | solution.py:208
  66.4 0.2 left_far.1.left
  66.6 4.0 %product.2.refs_0_ = bf16[2,2,512,2048]{3,2,1,0:T(8,128)(2,1)} custom-call(bf16[2,2,512,512]{3,2,1,0:T(8,128)(2,1)S(1)} %left_far.1.left, bf16[320,2048]{1,0:T(8,128)(2,1)S(1)} %stack.2.near, bf16[192,2048]{1,0:T(8,128)(2,1)S(1)} %stack.3.far), custom_call_target="tpu_custom_call" | custom-call | tf_op jit(solution)/shard_map/product/pallas_call | solution.py:195
  70.6 4.0 %product.3 = bf16[2,2,512,2048]{3,2,1,0:T(8,128)(2,1)} custom-call(bf16[2,2,512,512]{3,2,1,0:T(8,128)(2,1)S(1)} %left_far.1.left, bf16[320,2048]{1,0:T(8,128)(2,1)S(1)} %collective-permute-done.16.near, bf16[192,2048]{1,0:T(8,128)(2,1)S(1)} %collective-permute-done.17.far, bf16[2,2,512,2048]{3,2,1,0:T(8,128)(2,1)} %product.2.refs_0_), custom_call_target="tpu_custom_call", output_to_operand_aliasing={{}: (3, {})} | custom-call | tf_op jit(solution)/shard_map/product/pallas_call | solution.py:195
  (24 shorter events, 0.6 us)
Async XLA Ops:
  0.0 0.9 %copy-start = (bf16[8,2,64,128]{3,2,1,0:T(8,128)(2,1)S(1)}, bf16[8,2,64,128]{3,2,1,0:T(8,128)(2,1)}, u32[]{:S(2)}) copy-start(bf16[8,2,64,128]{3,2,1,0:T(8,128)(2,1)} %spectra.1) | copy-start | bytes 786436
  1.0 0.7 copy-start.1
  2.5 18.3 %all-to-all-start = ((bf16[64,16,128]{2,1,0:T(8,128)(2,1)}), bf16[64,16,128]{2,1,0:T(8,128)(2,1)S(1)}, u32[]{:S(2)}, u32[]{:S(2)}) async-start(bf16[64,16,128]{2,1,0:T(8,128)(2,1)} %bitcast.2), calls=%async_computation | async-start | bytes 524288 | tf_op jit(solution)/shard_map/all_to_all | solution.py:218
  11.9 17.4 %collective-permute-start.2 = (bf16[2,2,64,128]{3,2,1,0:T(8,128)(2,1)S(1)}, bf16[2,2,64,128]{3,2,1,0:T(8,128)(2,1)S(1)}, u32[]{:S(2)}, u32[]{:S(2)}) collective-permute-start(bf16[2,2,64,128]{3,2,1,0:T(8,128)(2,1)S(1)} %get-tuple-element.31), channel_id=1, source_target_pairs={{0,3},{1,2},{2,1},{3,0},{4,7},{5,6},{6,5},{7,4},{8,11},{9,10},{10,... | collective-permute-start | bytes 196616 | tf_op jit(solution)/shard_map/ppermute | solution.py:208
  13.4 15.8 %collective-permute-start.1 = (bf16[2,2,64,128]{3,2,1,0:T(8,128)(2,1)S(1)}, bf16[2,2,64,128]{3,2,1,0:T(8,128)(2,1)S(1)}, u32[]{:S(2)}, u32[]{:S(2)}) collective-permute-start(bf16[2,2,64,128]{3,2,1,0:T(8,128)(2,1)S(1)} %get-tuple-element.32), channel_id=1, source_target_pairs={{0,2},{1,3},{2,0},{3,1},{4,6},{5,7},{6,4},{7,5},{8,10},{9,11},{10,... | collective-permute-start | bytes 196616 | tf_op jit(solution)/shard_map/ppermute | solution.py:208
  14.5 14.8 %collective-permute-start = (bf16[2,2,64,128]{3,2,1,0:T(8,128)(2,1)S(1)}, bf16[2,2,64,128]{3,2,1,0:T(8,128)(2,1)S(1)}, u32[]{:S(2)}, u32[]{:S(2)}) collective-permute-start(bf16[2,2,64,128]{3,2,1,0:T(8,128)(2,1)S(1)} %get-tuple-element.33), channel_id=1, source_target_pairs={{0,1},{1,0},{2,3},{3,2},{4,5},{5,4},{6,7},{7,6},{8,9},{9,8},{10,11... | collective-permute-start | bytes 196616 | tf_op jit(solution)/shard_map/ppermute | solution.py:208
  21.4 7.9 %collective-permute-start.3 = (bf16[64,512]{1,0:T(8,128)(2,1)S(1)}, bf16[64,512]{1,0:T(8,128)(2,1)S(1)}, u32[]{:S(2)}, u32[]{:S(2)}) collective-permute-start(bf16[64,512]{1,0:T(8,128)(2,1)S(1)} %get-tuple-element.21), channel_id=1, source_target_pairs={{0,4},{4,0},{8,12},{12,8},{1,5},{5,1},{9,13},{13,9},{2,6},{6,2},{1... | collective-permute-start | bytes 196616 | tf_op jit(solution)/shard_map/ppermute | solution.py:208
  24.7 8.2 %collective-permute-start.4 = (bf16[64,512]{1,0:T(8,128)(2,1)S(1)}, bf16[64,512]{1,0:T(8,128)(2,1)S(1)}, u32[]{:S(2)}, u32[]{:S(2)}) collective-permute-start(bf16[64,512]{1,0:T(8,128)(2,1)S(1)} %get-tuple-element.22), channel_id=1, source_target_pairs={{0,8},{4,12},{8,0},{12,4},{1,9},{5,13},{9,1},{13,5},{2,10},{6,14},... | collective-permute-start | bytes 196616 | tf_op jit(solution)/shard_map/ppermute | solution.py:208
  29.2 6.4 %collective-permute-start.5 = (bf16[64,512]{1,0:T(8,128)(2,1)S(1)}, bf16[64,512]{1,0:T(8,128)(2,1)S(1)}, u32[]{:S(2)}, u32[]{:S(2)}) collective-permute-start(bf16[64,512]{1,0:T(8,128)(2,1)S(1)} %get-tuple-element.23), channel_id=1, source_target_pairs={{0,12},{4,8},{8,4},{12,0},{1,13},{5,9},{9,5},{13,1},{2,14},{6,10},... | collective-permute-start | bytes 196616 | tf_op jit(solution)/shard_map/ppermute | solution.py:208
  35.7 13.5 %collective-permute-start.12 = (bf16[64,2048]{1,0:T(8,128)(2,1)S(1)}, bf16[64,2048]{1,0:T(8,128)(2,1)S(1)}, u32[]{:S(2)}, u32[]{:S(2)}) collective-permute-start(bf16[64,2048]{1,0:T(8,128)(2,1)S(1)} %merge.1.refs_4_.refs_0_), channel_id=1, source_target_pairs={{0,32},{16,48},{32,0},{48,16},{64,96},{80,112},{96,64},{112,80},{1... | collective-permute-start | bytes 786440 | tf_op jit(solution)/shard_map/ppermute | solution.py:208
  37.3 11.8 %collective-permute-start.11 = (bf16[64,2048]{1,0:T(8,128)(2,1)S(1)}, bf16[64,2048]{1,0:T(8,128)(2,1)S(1)}, u32[]{:S(2)}, u32[]{:S(2)}) collective-permute-start(bf16[64,2048]{1,0:T(8,128)(2,1)S(1)} %merge.1.refs_4_.refs_0_), channel_id=1, source_target_pairs={{0,64},{16,80},{32,96},{48,112},{64,0},{80,16},{96,32},{112,48},{1... | collective-permute-start | bytes 786440 | tf_op jit(solution)/shard_map/ppermute | solution.py:208
  37.8 11.4 %collective-permute-start.10 = (bf16[64,2048]{1,0:T(8,128)(2,1)S(1)}, bf16[64,2048]{1,0:T(8,128)(2,1)S(1)}, u32[]{:S(2)}, u32[]{:S(2)}) collective-permute-start(bf16[64,2048]{1,0:T(8,128)(2,1)S(1)} %merge.1.refs_4_.refs_0_), channel_id=1, source_target_pairs={{0,192},{16,208},{32,224},{48,240},{64,128},{80,144},{96,160},{112... | collective-permute-start | bytes 786440 | tf_op jit(solution)/shard_map/ppermute | solution.py:208
  38.8 17.5 %collective-permute-start.7 = (bf16[2,2,256,128]{3,2,1,0:T(8,128)(2,1)S(1)}, bf16[2,2,256,128]{3,2,1,0:T(8,128)(2,1)S(1)}, u32[]{:S(2)}, u32[]{:S(2)}) collective-permute-start(bf16[2,2,256,128]{3,2,1,0:T(8,128)(2,1)S(1)} %hours.1.after.refs_0_), channel_id=1, source_target_pairs={{0,12},{4,8},{8,4},{12,0},{1,13},{5,9},{9,5},{13,1},{2,14},{6,10},... | collective-permute-start | bytes 786440 | tf_op jit(solution)/shard_map/ppermute | solution.py:208
  40.8 15.5 %collective-permute-start.6 = (bf16[2,2,256,128]{3,2,1,0:T(8,128)(2,1)S(1)}, bf16[2,2,256,128]{3,2,1,0:T(8,128)(2,1)S(1)}, u32[]{:S(2)}, u32[]{:S(2)}) collective-permute-start(bf16[2,2,256,128]{3,2,1,0:T(8,128)(2,1)S(1)} %hours.1.after.refs_0_), channel_id=1, source_target_pairs={{0,4},{4,0},{8,12},{12,8},{1,5},{5,1},{9,13},{13,9},{2,6},{6,2},{1... | collective-permute-start | bytes 786440 | tf_op jit(solution)/shard_map/ppermute | solution.py:208
  49.2 11.2 %collective-permute-start.13 = (bf16[96,2048]{1,0:T(8,128)(2,1)S(1)}, bf16[96,2048]{1,0:T(8,128)(2,1)S(1)}, u32[]{:S(2)}, u32[]{:S(2)}) collective-permute-start(bf16[96,2048]{1,0:T(8,128)(2,1)S(1)} %get-tuple-element.26), channel_id=1, source_target_pairs={{0,64},{16,80},{32,96},{48,112},{64,0},{80,16},{96,32},{112,48},{1... | collective-permute-start | bytes 1179656 | tf_op jit(solution)/shard_map/ppermute | solution.py:208
  49.3 13.1 %collective-permute-start.14 = (bf16[96,2048]{1,0:T(8,128)(2,1)S(1)}, bf16[96,2048]{1,0:T(8,128)(2,1)S(1)}, u32[]{:S(2)}, u32[]{:S(2)}) collective-permute-start(bf16[96,2048]{1,0:T(8,128)(2,1)S(1)} %get-tuple-element.27), channel_id=1, source_target_pairs={{0,192},{16,208},{32,224},{48,240},{64,128},{80,144},{96,160},{112... | collective-permute-start | bytes 1179656 | tf_op jit(solution)/shard_map/ppermute | solution.py:208
  49.4 10.8 %collective-permute-start.15 = (bf16[64,2048]{1,0:T(8,128)(2,1)S(1)}, bf16[64,2048]{1,0:T(8,128)(2,1)S(1)}, u32[]{:S(2)}, u32[]{:S(2)}) collective-permute-start(bf16[64,2048]{1,0:T(8,128)(2,1)S(1)} %collective-permute-done.12.other.refs_1_), channel_id=1, source_target_pairs={{0,128},{16,144},{32,160},{48,176},{64,192},{80,208},{96,224},{112... | collective-permute-start | bytes 786440 | tf_op jit(solution)/shard_map/ppermute | solution.py:208
  56.3 9.0 %collective-permute-start.8 = (bf16[1,2,256,128]{3,2,1,0:T(8,128)(2,1)S(1)}, bf16[1,2,256,128]{3,2,1,0:T(8,128)(2,1)S(1)}, u32[]{:S(2)}, u32[]{:S(2)}) collective-permute-start(bf16[1,2,256,128]{3,2,1,0:T(8,128)(2,1)S(1)} %get-tuple-element.24), channel_id=1, source_target_pairs={{0,12},{4,8},{8,4},{12,0},{1,13},{5,9},{9,5},{13,1},{2,14},{6,10},... | collective-permute-start | bytes 393224 | tf_op jit(solution)/shard_map/ppermute | solution.py:208
  59.1 7.3 %collective-permute-start.9 = (bf16[1,2,256,128]{3,2,1,0:T(8,128)(2,1)S(1)}, bf16[1,2,256,128]{3,2,1,0:T(8,128)(2,1)S(1)}, u32[]{:S(2)}, u32[]{:S(2)}) collective-permute-start(bf16[1,2,256,128]{3,2,1,0:T(8,128)(2,1)S(1)} %get-tuple-element.25), channel_id=1, source_target_pairs={{0,4},{4,0},{8,12},{12,8},{1,5},{5,1},{9,13},{13,9},{2,6},{6,2},{1... | collective-permute-start | bytes 393224 | tf_op jit(solution)/shard_map/ppermute | solution.py:208
  60.3 10.3 %collective-permute-start.16 = (bf16[320,2048]{1,0:T(8,128)(2,1)S(1)}, bf16[320,2048]{1,0:T(8,128)(2,1)S(1)}, u32[]{:S(2)}, u32[]{:S(2)}) collective-permute-start(bf16[320,2048]{1,0:T(8,128)(2,1)S(1)} %stack.2.near), channel_id=1, source_target_pairs={{0,16},{16,0},{32,48},{48,32},{64,80},{80,64},{96,112},{112,96},{1... | collective-permute-start | bytes 3932168 | tf_op jit(solution)/shard_map/ppermute | solution.py:208
  62.5 8.1 %collective-permute-start.17 = (bf16[192,2048]{1,0:T(8,128)(2,1)S(1)}, bf16[192,2048]{1,0:T(8,128)(2,1)S(1)}, u32[]{:S(2)}, u32[]{:S(2)}) collective-permute-start(bf16[192,2048]{1,0:T(8,128)(2,1)S(1)} %stack.3.far), channel_id=1, source_target_pairs={{0,16},{16,0},{32,48},{48,32},{64,80},{80,64},{96,112},{112,96},{1... | collective-permute-start | bytes 2359304 | tf_op jit(solution)/shard_map/ppermute | solution.py:208

commit v5 on v4

--- a/solution.py
+++ b/solution.py
@@ -69,11 +69,11 @@
 
 def merge_kernel(*refs):
     out, col = refs[-1], lax.axis_index("col")
-    for d in range(4):
+    for i, d in enumerate((0, 2, 3, 1)):
         quarter = col ^ d
         for s in range(4):
             at = pl.multiple_of(s * 512 + quarter * 128, 128)
-            out[:, pl.ds(at, 128)] = refs[d][:, 128 * s : 128 * s + 128]
+            out[:, pl.ds(at, 128)] = refs[i][:, 128 * s : 128 * s + 128]
 
 
 def merge(parts, after):
@@ -217,8 +217,9 @@
 
     pieces = lax.all_to_all(spread.reshape(64, 16, 128), ("row", "hour"), 0, 0, tiled=True)
     sent = select(place, pieces.reshape(16, 4, 16, 128))
-    sent = [sent[0]] + [swap(sent[d], "col", d) for d in range(1, 4)]
-    own = merge(sent, parts[1:])
+    moved = {d: swap(sent[d], "col", d) for d in (1, 3, 2)}
+    sent = [sent[0]] + [moved[d] for d in range(1, 4)]
+    own = merge([sent[0], sent[2], sent[3], sent[1]], parts[1:])
 
     three = swap(own, "row", 12)
     one = swap(own, "row", 4)

time: 74.9 us -> 73.5 us (0.981)
  waiting for transfers between devices: 25.3 us -> 21.8 us
  starting transfers between devices: 36.4 us -> 37.8 us
    ppermute x18, waiting for transfers between devices: 21.3 us -> 17.9 us  [swap(): lax.ppermute(value, axis, [(i, i ^ bits) for i in range(lax.axis_size(axi...]
    ppermute x18, starting transfers between devices: 27 us -> 28.5 us  [swap(): lax.ppermute(value, axis, [(i, i ^ bits) for i in range(lax.axis_size(axi...]
  transfers between devices with their start and end apart: 19 -> 19, of which waited for: 9 -> 8; matrix products, arithmetic and copies ran while one was open for 1% -> 1% of each run, Pallas kernels for 7% -> 8%
where the time goes in v5:
time: 73.5 us; the launch traced here: 72.7 us
  starting transfers between devices  37.8 us (51%)
  waiting for transfers between devices  21.8 us (30%)
  Pallas kernels  10.3 us (14%)
  local copies, waits for them, and re-layouts  1.63 us (2%)
    ppermute x18, starting transfers between devices, swap(): lax.ppermute(value, axis, [(i, i ^ bits) for i in range(lax.axis_size(axi...  28.5 us
    ppermute x18, waiting for transfers between devices, swap(): lax.ppermute(value, axis, [(i, i ^ bits) for i in range(lax.axis_size(axi...  17.9 us
    all_to_all x1, starting transfers between devices, per_device(): lax.all_to_all(spread.reshape(64, 16, 128), ('row', 'hour'), 0, 0, tiled=...  9.37 us
    pallas_call x2, Pallas kernels, product(): pl.pallas_call(functools.partial(product_kernel, other), out_shape=struct...  7.92 us
    all_to_all x1, waiting for transfers between devices, per_device(): lax.all_to_all(spread.reshape(64, 16, 128), ('row', 'hour'), 0, 0, tiled=...  3.98 us
    pallas_call x10, Pallas kernels, call(): pl.pallas_call(kernel, out_shape=out_shape, input_output_aliases=aliases,...  2.4 us
    unnamed x4, local copies, waits for them, and re-layouts  1.6 us
  transfers between devices with their start and end apart: 19, of which 8 were waited for; matrix products, arithmetic and copies ran while one was open for 1% of the time, Pallas kernels for 8%

profile of v5, /device:TPU:2, one launch (start us, length us, event | category | flops | bytes accessed | tf_op | source)
XLA Modules:
  0.0 72.7 jit_solution(6331551337574024130)
XLA Ops:
  0.0 0.9 %copy-done = bf16[8,2,64,128]{3,2,1,0:T(8,128)(2,1)S(1)} copy-done((bf16[8,2,64,128]{3,2,1,0:T(8,128)(2,1)S(1)}, bf16[8,2,64,128]{3,2,1,0:T(8,128)(2,1)}, u32[]{:S(2)}) %copy-start) | copy-done | bytes 262168
  1.0 0.7 copy-done.1
  1.6 0.8 %whiten.1 = (bf16[8,2,64,128]{3,2,1,0:T(8,128)(2,1)S(1)}, bf16[4,2,2,4,16,128]{5,4,3,2,1,0:T(8,128)(2,1)}) custom-call(bf16[8,2,64,128]{3,2,1,0:T(8,128)(2,1)S(1)} %copy-done, s32[1,64]{1,0:T(1,128)S(1)} %bitcast.5), custom_call_target="tpu_custom_call" | custom-call | tf_op jit(solution)/shard_map/whiten/pallas_call | solution.py:26
  2.5 9.4 %all-to-all-start = ((bf16[64,16,128]{2,1,0:T(8,128)(2,1)}), bf16[64,16,128]{2,1,0:T(8,128)(2,1)S(1)}, u32[]{:S(2)}, u32[]{:S(2)}) async-start(bf16[64,16,128]{2,1,0:T(8,128)(2,1)} %bitcast.2), calls=%async_computation | async-start | bytes 524288 | tf_op jit(solution)/shard_map/all_to_all | solution.py:218
  11.9 1.6 %collective-permute-start.2 = (bf16[2,2,64,128]{3,2,1,0:T(8,128)(2,1)S(1)}, bf16[2,2,64,128]{3,2,1,0:T(8,128)(2,1)S(1)}, u32[]{:S(2)}, u32[]{:S(2)}) collective-permute-start(bf16[2,2,64,128]{3,2,1,0:T(8,128)(2,1)S(1)} %get-tuple-element.31), channel_id=1, source_target_pairs={{0,3},{1,2},{2,1},{3,0},{4,7},{5,6},{6,5},{7,4},{8,11},{9,10},{10,... | collective-permute-start | bytes 196616 | tf_op jit(solution)/shard_map/ppermute | solution.py:208
  13.4 1.1 %collective-permute-start.1 = (bf16[2,2,64,128]{3,2,1,0:T(8,128)(2,1)S(1)}, bf16[2,2,64,128]{3,2,1,0:T(8,128)(2,1)S(1)}, u32[]{:S(2)}, u32[]{:S(2)}) collective-permute-start(bf16[2,2,64,128]{3,2,1,0:T(8,128)(2,1)S(1)} %get-tuple-element.32), channel_id=1, source_target_pairs={{0,2},{1,3},{2,0},{3,1},{4,6},{5,7},{6,4},{7,5},{8,10},{9,11},{10,... | collective-permute-start | bytes 196616 | tf_op jit(solution)/shard_map/ppermute | solution.py:208
  14.5 1.6 %collective-permute-start = (bf16[2,2,64,128]{3,2,1,0:T(8,128)(2,1)S(1)}, bf16[2,2,64,128]{3,2,1,0:T(8,128)(2,1)S(1)}, u32[]{:S(2)}, u32[]{:S(2)}) collective-permute-start(bf16[2,2,64,128]{3,2,1,0:T(8,128)(2,1)S(1)} %get-tuple-element.33), channel_id=1, source_target_pairs={{0,1},{1,0},{2,3},{3,2},{4,5},{5,4},{6,7},{7,6},{8,9},{9,8},{10,11... | collective-permute-start | bytes 196616 | tf_op jit(solution)/shard_map/ppermute | solution.py:208
  16.1 0.7 %pad_add_fusion.place = s32[17]{0:T(128)S(1)} fusion(s32[16]{0:T(128)} %param.5, s32[1]{0:T(128)} %bitcast.1), kind=kLoop, calls=%fused_computation.4 | loop fusion | flops 17 | bytes 136 | tf_op jit(solution)/shard_map/concatenate | solution.py:213
  16.8 4.0 %all-to-all-done = bf16[64,16,128]{2,1,0:T(8,128)(2,1)S(1)} async-done(((bf16[64,16,128]{2,1,0:T(8,128)(2,1)}), bf16[64,16,128]{2,1,0:T(8,128)(2,1)S(1)}, u32[]{:S(2)}, u32[]{:S(2)}) %all-to-all-start) | async-done | bytes 262176 | tf_op jit(solution)/shard_map/all_to_all | solution.py:218
  20.8 0.6 select.1
  21.4 6.4 %collective-permute-start.3 = (bf16[64,512]{1,0:T(8,128)(2,1)S(1)}, bf16[64,512]{1,0:T(8,128)(2,1)S(1)}, u32[]{:S(2)}, u32[]{:S(2)}) collective-permute-start(bf16[64,512]{1,0:T(8,128)(2,1)S(1)} %get-tuple-element.21), channel_id=1, source_target_pairs={{0,8},{4,12},{8,0},{12,4},{1,9},{5,13},{9,1},{13,5},{2,10},{6,14},... | collective-permute-start | bytes 196616 | tf_op jit(solution)/shard_map/ppermute | solution.py:208
  27.8 0.6 collective-permute-start.4
  28.3 0.9 %collective-permute-start.5 = (bf16[64,512]{1,0:T(8,128)(2,1)S(1)}, bf16[64,512]{1,0:T(8,128)(2,1)S(1)}, u32[]{:S(2)}, u32[]{:S(2)}) collective-permute-start(bf16[64,512]{1,0:T(8,128)(2,1)S(1)} %get-tuple-element.23), channel_id=1, source_target_pairs={{0,4},{4,0},{8,12},{12,8},{1,5},{5,1},{9,13},{13,9},{2,6},{6,2},{1... | collective-permute-start | bytes 196616 | tf_op jit(solution)/shard_map/ppermute | solution.py:208
  29.3 2.6 %collective-permute-done.3.refs_1_ = bf16[64,512]{1,0:T(8,128)(2,1)S(1)} collective-permute-done((bf16[64,512]{1,0:T(8,128)(2,1)S(1)}, bf16[64,512]{1,0:T(8,128)(2,1)S(1)}, u32[]{:S(2)}, u32[]{:S(2)}) %collective-permute-start.3) | collective-permute-done | bytes 65568 | tf_op jit(solution)/shard_map/ppermute | solution.py:208
  31.8 2.9 %collective-permute-done.4.refs_2_ = bf16[64,512]{1,0:T(8,128)(2,1)S(1)} collective-permute-done((bf16[64,512]{1,0:T(8,128)(2,1)S(1)}, bf16[64,512]{1,0:T(8,128)(2,1)S(1)}, u32[]{:S(2)}, u32[]{:S(2)}) %collective-permute-start.4) | collective-permute-done | bytes 65568 | tf_op jit(solution)/shard_map/ppermute | solution.py:208
  34.8 0.4 collective-permute-start.12
  35.2 0.6 collective-permute-start.11
  35.8 1.8 %collective-permute-start.10 = (bf16[64,2048]{1,0:T(8,128)(2,1)S(1)}, bf16[64,2048]{1,0:T(8,128)(2,1)S(1)}, u32[]{:S(2)}, u32[]{:S(2)}) collective-permute-start(bf16[64,2048]{1,0:T(8,128)(2,1)S(1)} %merge.1.refs_4_.refs_0_), channel_id=1, source_target_pairs={{0,192},{16,208},{32,224},{48,240},{64,128},{80,144},{96,160},{112... | collective-permute-start | bytes 786440 | tf_op jit(solution)/shard_map/ppermute | solution.py:208
  37.6 3.4 %collective-permute-start.7 = (bf16[2,2,256,128]{3,2,1,0:T(8,128)(2,1)S(1)}, bf16[2,2,256,128]{3,2,1,0:T(8,128)(2,1)S(1)}, u32[]{:S(2)}, u32[]{:S(2)}) collective-permute-start(bf16[2,2,256,128]{3,2,1,0:T(8,128)(2,1)S(1)} %hours.1.after.refs_0_), channel_id=1, source_target_pairs={{0,12},{4,8},{8,4},{12,0},{1,13},{5,9},{9,5},{13,1},{2,14},{6,10},... | collective-permute-start | bytes 786440 | tf_op jit(solution)/shard_map/ppermute | solution.py:208
  41.0 0.9 %collective-permute-start.6 = (bf16[2,2,256,128]{3,2,1,0:T(8,128)(2,1)S(1)}, bf16[2,2,256,128]{3,2,1,0:T(8,128)(2,1)S(1)}, u32[]{:S(2)}, u32[]{:S(2)}) collective-permute-start(bf16[2,2,256,128]{3,2,1,0:T(8,128)(2,1)S(1)} %hours.1.after.refs_0_), channel_id=1, source_target_pairs={{0,4},{4,0},{8,12},{12,8},{1,5},{5,1},{9,13},{13,9},{2,6},{6,2},{1... | collective-permute-start | bytes 786440 | tf_op jit(solution)/shard_map/ppermute | solution.py:208
  41.8 5.0 %collective-permute-done.12.other.refs_1_ = bf16[64,2048]{1,0:T(8,128)(2,1)S(1)} collective-permute-done((bf16[64,2048]{1,0:T(8,128)(2,1)S(1)}, bf16[64,2048]{1,0:T(8,128)(2,1)S(1)}, u32[]{:S(2)}, u32[]{:S(2)}) %collective-permute-start.12) | collective-permute-done | bytes 262176 | tf_op jit(solution)/shard_map/ppermute | solution.py:208
  46.9 3.2 %collective-permute-start.13 = (bf16[96,2048]{1,0:T(8,128)(2,1)S(1)}, bf16[96,2048]{1,0:T(8,128)(2,1)S(1)}, u32[]{:S(2)}, u32[]{:S(2)}) collective-permute-start(bf16[96,2048]{1,0:T(8,128)(2,1)S(1)} %get-tuple-element.26), channel_id=1, source_target_pairs={{0,64},{16,80},{32,96},{48,112},{64,0},{80,16},{96,32},{112,48},{1... | collective-permute-start | bytes 1179656 | tf_op jit(solution)/shard_map/ppermute | solution.py:208
  50.1 2.2 %collective-permute-start.15 = (bf16[64,2048]{1,0:T(8,128)(2,1)S(1)}, bf16[64,2048]{1,0:T(8,128)(2,1)S(1)}, u32[]{:S(2)}, u32[]{:S(2)}) collective-permute-start(bf16[64,2048]{1,0:T(8,128)(2,1)S(1)} %collective-permute-done.12.other.refs_1_), channel_id=1, source_target_pairs={{0,128},{16,144},{32,160},{48,176},{64,192},{80,208},{96,224},{112... | collective-permute-start | bytes 786440 | tf_op jit(solution)/shard_map/ppermute | solution.py:208
  52.2 3.1 %collective-permute-done.7.three.refs_2_ = bf16[2,2,256,128]{3,2,1,0:T(8,128)(2,1)S(1)} collective-permute-done((bf16[2,2,256,128]{3,2,1,0:T(8,128)(2,1)S(1)}, bf16[2,2,256,128]{3,2,1,0:T(8,128)(2,1)S(1)}, u32[]{:S(2)}, u32[]{:S(2)}) %collective-permute-start.7) | collective-permute-done | bytes 262176 | tf_op jit(solution)/shard_map/ppermute | solution.py:208
  55.3 1.5 %collective-permute-start.8 = (bf16[1,2,256,128]{3,2,1,0:T(8,128)(2,1)S(1)}, bf16[1,2,256,128]{3,2,1,0:T(8,128)(2,1)S(1)}, u32[]{:S(2)}, u32[]{:S(2)}) collective-permute-start(bf16[1,2,256,128]{3,2,1,0:T(8,128)(2,1)S(1)} %get-tuple-element.24), channel_id=1, source_target_pairs={{0,12},{4,8},{8,4},{12,0},{1,13},{5,9},{9,5},{13,1},{2,14},{6,10},... | collective-permute-start | bytes 393224 | tf_op jit(solution)/shard_map/ppermute | solution.py:208
  56.8 2.2 %collective-permute-start.9 = (bf16[1,2,256,128]{3,2,1,0:T(8,128)(2,1)S(1)}, bf16[1,2,256,128]{3,2,1,0:T(8,128)(2,1)S(1)}, u32[]{:S(2)}, u32[]{:S(2)}) collective-permute-start(bf16[1,2,256,128]{3,2,1,0:T(8,128)(2,1)S(1)} %get-tuple-element.25), channel_id=1, source_target_pairs={{0,4},{4,0},{8,12},{12,8},{1,5},{5,1},{9,13},{13,9},{2,6},{6,2},{1... | collective-permute-start | bytes 393224 | tf_op jit(solution)/shard_map/ppermute | solution.py:208
  59.0 0.5 left_near.1.left
  59.7 2.2 %collective-permute-done.14.refs_1_ = bf16[96,2048]{1,0:T(8,128)(2,1)S(1)} collective-permute-done((bf16[96,2048]{1,0:T(8,128)(2,1)S(1)}, bf16[96,2048]{1,0:T(8,128)(2,1)S(1)}, u32[]{:S(2)}, u32[]{:S(2)}) %collective-permute-start.14) | collective-permute-done | bytes 393248 | tf_op jit(solution)/shard_map/ppermute | solution.py:208
  62.2 0.4 collective-permute-done.8.low
  62.6 1.8 %collective-permute-done.9.high = bf16[1,2,256,128]{3,2,1,0:T(8,128)(2,1)S(1)} collective-permute-done((bf16[1,2,256,128]{3,2,1,0:T(8,128)(2,1)S(1)}, bf16[1,2,256,128]{3,2,1,0:T(8,128)(2,1)S(1)}, u32[]{:S(2)}, u32[]{:S(2)}) %collective-permute-start.9) | collective-permute-done | bytes 131104 | tf_op jit(solution)/shard_map/ppermute | solution.py:208
  64.6 4.0 %product.2.refs_0_ = bf16[2,2,512,2048]{3,2,1,0:T(8,128)(2,1)} custom-call(bf16[2,2,512,512]{3,2,1,0:T(8,128)(2,1)S(1)} %left_far.1.left, bf16[320,2048]{1,0:T(8,128)(2,1)S(1)} %stack.2.near, bf16[192,2048]{1,0:T(8,128)(2,1)S(1)} %stack.3.far), custom_call_target="tpu_custom_call" | custom-call | tf_op jit(solution)/shard_map/product/pallas_call | solution.py:195
  68.6 4.0 %product.3 = bf16[2,2,512,2048]{3,2,1,0:T(8,128)(2,1)} custom-call(bf16[2,2,512,512]{3,2,1,0:T(8,128)(2,1)S(1)} %left_far.1.left, bf16[320,2048]{1,0:T(8,128)(2,1)S(1)} %collective-permute-done.16.near, bf16[192,2048]{1,0:T(8,128)(2,1)S(1)} %collective-permute-done.17.far, bf16[2,2,512,2048]{3,2,1,0:T(8,128)(2,1)} %product.2.refs_0_), custom_call_target="tpu_custom_call", output_to_operand_aliasing={{}: (3, {})} | custom-call | tf_op jit(solution)/shard_map/product/pallas_call | solution.py:195
  (24 shorter events, 0.9 us)
Async XLA Ops:
  0.0 0.9 %copy-start = (bf16[8,2,64,128]{3,2,1,0:T(8,128)(2,1)S(1)}, bf16[8,2,64,128]{3,2,1,0:T(8,128)(2,1)}, u32[]{:S(2)}) copy-start(bf16[8,2,64,128]{3,2,1,0:T(8,128)(2,1)} %spectra.1) | copy-start | bytes 786436
  1.0 0.7 copy-start.1
  2.5 18.3 %all-to-all-start = ((bf16[64,16,128]{2,1,0:T(8,128)(2,1)}), bf16[64,16,128]{2,1,0:T(8,128)(2,1)S(1)}, u32[]{:S(2)}, u32[]{:S(2)}) async-start(bf16[64,16,128]{2,1,0:T(8,128)(2,1)} %bitcast.2), calls=%async_computation | async-start | bytes 524288 | tf_op jit(solution)/shard_map/all_to_all | solution.py:218
  11.9 16.4 %collective-permute-start.2 = (bf16[2,2,64,128]{3,2,1,0:T(8,128)(2,1)S(1)}, bf16[2,2,64,128]{3,2,1,0:T(8,128)(2,1)S(1)}, u32[]{:S(2)}, u32[]{:S(2)}) collective-permute-start(bf16[2,2,64,128]{3,2,1,0:T(8,128)(2,1)S(1)} %get-tuple-element.31), channel_id=1, source_target_pairs={{0,3},{1,2},{2,1},{3,0},{4,7},{5,6},{6,5},{7,4},{8,11},{9,10},{10,... | collective-permute-start | bytes 196616 | tf_op jit(solution)/shard_map/ppermute | solution.py:208
  13.4 15.8 %collective-permute-start.1 = (bf16[2,2,64,128]{3,2,1,0:T(8,128)(2,1)S(1)}, bf16[2,2,64,128]{3,2,1,0:T(8,128)(2,1)S(1)}, u32[]{:S(2)}, u32[]{:S(2)}) collective-permute-start(bf16[2,2,64,128]{3,2,1,0:T(8,128)(2,1)S(1)} %get-tuple-element.32), channel_id=1, source_target_pairs={{0,2},{1,3},{2,0},{3,1},{4,6},{5,7},{6,4},{7,5},{8,10},{9,11},{10,... | collective-permute-start | bytes 196616 | tf_op jit(solution)/shard_map/ppermute | solution.py:208
  14.5 14.8 %collective-permute-start = (bf16[2,2,64,128]{3,2,1,0:T(8,128)(2,1)S(1)}, bf16[2,2,64,128]{3,2,1,0:T(8,128)(2,1)S(1)}, u32[]{:S(2)}, u32[]{:S(2)}) collective-permute-start(bf16[2,2,64,128]{3,2,1,0:T(8,128)(2,1)S(1)} %get-tuple-element.33), channel_id=1, source_target_pairs={{0,1},{1,0},{2,3},{3,2},{4,5},{5,4},{6,7},{7,6},{8,9},{9,8},{10,11... | collective-permute-start | bytes 196616 | tf_op jit(solution)/shard_map/ppermute | solution.py:208
  21.4 10.4 %collective-permute-start.3 = (bf16[64,512]{1,0:T(8,128)(2,1)S(1)}, bf16[64,512]{1,0:T(8,128)(2,1)S(1)}, u32[]{:S(2)}, u32[]{:S(2)}) collective-permute-start(bf16[64,512]{1,0:T(8,128)(2,1)S(1)} %get-tuple-element.21), channel_id=1, source_target_pairs={{0,8},{4,12},{8,0},{12,4},{1,9},{5,13},{9,1},{13,5},{2,10},{6,14},... | collective-permute-start | bytes 196616 | tf_op jit(solution)/shard_map/ppermute | solution.py:208
  27.8 6.9 %collective-permute-start.4 = (bf16[64,512]{1,0:T(8,128)(2,1)S(1)}, bf16[64,512]{1,0:T(8,128)(2,1)S(1)}, u32[]{:S(2)}, u32[]{:S(2)}) collective-permute-start(bf16[64,512]{1,0:T(8,128)(2,1)S(1)} %get-tuple-element.22), channel_id=1, source_target_pairs={{0,12},{4,8},{8,4},{12,0},{1,13},{5,9},{9,5},{13,1},{2,14},{6,10},... | collective-permute-start | bytes 196616 | tf_op jit(solution)/shard_map/ppermute | solution.py:208
  28.3 6.4 %collective-permute-start.5 = (bf16[64,512]{1,0:T(8,128)(2,1)S(1)}, bf16[64,512]{1,0:T(8,128)(2,1)S(1)}, u32[]{:S(2)}, u32[]{:S(2)}) collective-permute-start(bf16[64,512]{1,0:T(8,128)(2,1)S(1)} %get-tuple-element.23), channel_id=1, source_target_pairs={{0,4},{4,0},{8,12},{12,8},{1,5},{5,1},{9,13},{13,9},{2,6},{6,2},{1... | collective-permute-start | bytes 196616 | tf_op jit(solution)/shard_map/ppermute | solution.py:208
  34.8 12.1 %collective-permute-start.12 = (bf16[64,2048]{1,0:T(8,128)(2,1)S(1)}, bf16[64,2048]{1,0:T(8,128)(2,1)S(1)}, u32[]{:S(2)}, u32[]{:S(2)}) collective-permute-start(bf16[64,2048]{1,0:T(8,128)(2,1)S(1)} %merge.1.refs_4_.refs_0_), channel_id=1, source_target_pairs={{0,32},{16,48},{32,0},{48,16},{64,96},{80,112},{96,64},{112,80},{1... | collective-permute-start | bytes 786440 | tf_op jit(solution)/shard_map/ppermute | solution.py:208
  35.2 11.7 %collective-permute-start.11 = (bf16[64,2048]{1,0:T(8,128)(2,1)S(1)}, bf16[64,2048]{1,0:T(8,128)(2,1)S(1)}, u32[]{:S(2)}, u32[]{:S(2)}) collective-permute-start(bf16[64,2048]{1,0:T(8,128)(2,1)S(1)} %merge.1.refs_4_.refs_0_), channel_id=1, source_target_pairs={{0,64},{16,80},{32,96},{48,112},{64,0},{80,16},{96,32},{112,48},{1... | collective-permute-start | bytes 786440 | tf_op jit(solution)/shard_map/ppermute | solution.py:208
  35.8 11.1 %collective-permute-start.10 = (bf16[64,2048]{1,0:T(8,128)(2,1)S(1)}, bf16[64,2048]{1,0:T(8,128)(2,1)S(1)}, u32[]{:S(2)}, u32[]{:S(2)}) collective-permute-start(bf16[64,2048]{1,0:T(8,128)(2,1)S(1)} %merge.1.refs_4_.refs_0_), channel_id=1, source_target_pairs={{0,192},{16,208},{32,224},{48,240},{64,128},{80,144},{96,160},{112... | collective-permute-start | bytes 786440 | tf_op jit(solution)/shard_map/ppermute | solution.py:208
  37.6 17.7 %collective-permute-start.7 = (bf16[2,2,256,128]{3,2,1,0:T(8,128)(2,1)S(1)}, bf16[2,2,256,128]{3,2,1,0:T(8,128)(2,1)S(1)}, u32[]{:S(2)}, u32[]{:S(2)}) collective-permute-start(bf16[2,2,256,128]{3,2,1,0:T(8,128)(2,1)S(1)} %hours.1.after.refs_0_), channel_id=1, source_target_pairs={{0,12},{4,8},{8,4},{12,0},{1,13},{5,9},{9,5},{13,1},{2,14},{6,10},... | collective-permute-start | bytes 786440 | tf_op jit(solution)/shard_map/ppermute | solution.py:208
  41.0 14.3 %collective-permute-start.6 = (bf16[2,2,256,128]{3,2,1,0:T(8,128)(2,1)S(1)}, bf16[2,2,256,128]{3,2,1,0:T(8,128)(2,1)S(1)}, u32[]{:S(2)}, u32[]{:S(2)}) collective-permute-start(bf16[2,2,256,128]{3,2,1,0:T(8,128)(2,1)S(1)} %hours.1.after.refs_0_), channel_id=1, source_target_pairs={{0,4},{4,0},{8,12},{12,8},{1,5},{5,1},{9,13},{13,9},{2,6},{6,2},{1... | collective-permute-start | bytes 786440 | tf_op jit(solution)/shard_map/ppermute | solution.py:208
  46.9 12.8 %collective-permute-start.13 = (bf16[96,2048]{1,0:T(8,128)(2,1)S(1)}, bf16[96,2048]{1,0:T(8,128)(2,1)S(1)}, u32[]{:S(2)}, u32[]{:S(2)}) collective-permute-start(bf16[96,2048]{1,0:T(8,128)(2,1)S(1)} %get-tuple-element.26), channel_id=1, source_target_pairs={{0,64},{16,80},{32,96},{48,112},{64,0},{80,16},{96,32},{112,48},{1... | collective-permute-start | bytes 1179656 | tf_op jit(solution)/shard_map/ppermute | solution.py:208
  50.1 11.8 %collective-permute-start.14 = (bf16[96,2048]{1,0:T(8,128)(2,1)S(1)}, bf16[96,2048]{1,0:T(8,128)(2,1)S(1)}, u32[]{:S(2)}, u32[]{:S(2)}) collective-permute-start(bf16[96,2048]{1,0:T(8,128)(2,1)S(1)} %get-tuple-element.27), channel_id=1, source_target_pairs={{0,192},{16,208},{32,224},{48,240},{64,128},{80,144},{96,160},{112... | collective-permute-start | bytes 1179656 | tf_op jit(solution)/shard_map/ppermute | solution.py:208
  50.1 9.4 %collective-permute-start.15 = (bf16[64,2048]{1,0:T(8,128)(2,1)S(1)}, bf16[64,2048]{1,0:T(8,128)(2,1)S(1)}, u32[]{:S(2)}, u32[]{:S(2)}) collective-permute-start(bf16[64,2048]{1,0:T(8,128)(2,1)S(1)} %collective-permute-done.12.other.refs_1_), channel_id=1, source_target_pairs={{0,128},{16,144},{32,160},{48,176},{64,192},{80,208},{96,224},{112... | collective-permute-start | bytes 786440 | tf_op jit(solution)/shard_map/ppermute | solution.py:208
  55.3 7.3 %collective-permute-start.8 = (bf16[1,2,256,128]{3,2,1,0:T(8,128)(2,1)S(1)}, bf16[1,2,256,128]{3,2,1,0:T(8,128)(2,1)S(1)}, u32[]{:S(2)}, u32[]{:S(2)}) collective-permute-start(bf16[1,2,256,128]{3,2,1,0:T(8,128)(2,1)S(1)} %get-tuple-element.24), channel_id=1, source_target_pairs={{0,12},{4,8},{8,4},{12,0},{1,13},{5,9},{9,5},{13,1},{2,14},{6,10},... | collective-permute-start | bytes 393224 | tf_op jit(solution)/shard_map/ppermute | solution.py:208
  56.8 7.5 %collective-permute-start.9 = (bf16[1,2,256,128]{3,2,1,0:T(8,128)(2,1)S(1)}, bf16[1,2,256,128]{3,2,1,0:T(8,128)(2,1)S(1)}, u32[]{:S(2)}, u32[]{:S(2)}) collective-permute-start(bf16[1,2,256,128]{3,2,1,0:T(8,128)(2,1)S(1)} %get-tuple-element.25), channel_id=1, source_target_pairs={{0,4},{4,0},{8,12},{12,8},{1,5},{5,1},{9,13},{13,9},{2,6},{6,2},{1... | collective-permute-start | bytes 393224 | tf_op jit(solution)/shard_map/ppermute | solution.py:208
  59.6 9.0 %collective-permute-start.16 = (bf16[320,2048]{1,0:T(8,128)(2,1)S(1)}, bf16[320,2048]{1,0:T(8,128)(2,1)S(1)}, u32[]{:S(2)}, u32[]{:S(2)}) collective-permute-start(bf16[320,2048]{1,0:T(8,128)(2,1)S(1)} %stack.2.near), channel_id=1, source_target_pairs={{0,16},{16,0},{32,48},{48,32},{64,80},{80,64},{96,112},{112,96},{1... | collective-permute-start | bytes 3932168 | tf_op jit(solution)/shard_map/ppermute | solution.py:208
  61.9 6.6 %collective-permute-start.17 = (bf16[192,2048]{1,0:T(8,128)(2,1)S(1)}, bf16[192,2048]{1,0:T(8,128)(2,1)S(1)}, u32[]{:S(2)}, u32[]{:S(2)}) collective-permute-start(bf16[192,2048]{1,0:T(8,128)(2,1)S(1)} %stack.3.far), channel_id=1, source_target_pairs={{0,16},{16,0},{32,48},{48,32},{64,80},{80,64},{96,112},{112,96},{1... | collective-permute-start | bytes 2359304 | tf_op jit(solution)/shard_map/ppermute | solution.py:208

commit v6 on v5

--- a/solution.py
+++ b/solution.py
@@ -178,15 +178,20 @@
     for j in range(STRIPS):
         columns = slice(WIDE * j, WIDE * j + WIDE)
         right = jnp.concatenate([near[:, columns], far[:, columns]], axis=0)
-        result = jnp.dot(both, right, preferred_element_type=jnp.float32)
-        held[j] = result.astype(BF).reshape(2, 512, WIDE)
-        for i, d in enumerate((0, 1, 3, 2)):
-            rows = pl.ds(pl.multiple_of((col ^ d) * 128, 128), 128)
-            copy = pltpu.make_async_copy(
-                held.at[j, :, pl.ds(128 * i, 128)], out.at[f, :, rows, columns], sem.at[j, i]
-            )
-            copy.start()
-            copies.append(copy)
+        last = j == STRIPS - 1
+        for n in range(2 if last else 1):
+            parts = slice(n, n + 1) if last else slice(0, 2)
+            count = parts.stop - parts.start
+            some = left[f, parts].reshape(512 * count, 512) if last else both
+            result = jnp.dot(some, right, preferred_element_type=jnp.float32)
+            held[j, parts] = result.astype(BF).reshape(count, 512, WIDE)
+            for i, d in enumerate((0, 1, 3, 2)):
+                rows = pl.ds(pl.multiple_of((col ^ d) * 128, 128), 128)
+                copy = pltpu.make_async_copy(
+                    held.at[j, parts, pl.ds(128 * i, 128)], out.at[f, parts, rows, columns], sem.at[j + n, i]
+                )
+                copy.start()
+                copies.append(copy)
     for copy in copies:
         copy.wait()
 
@@ -198,7 +203,7 @@
         in_specs=[VMEM] * 3 + [ANY] * other,
         out_specs=ANY,
         input_output_aliases={3: 0} if other else {},
-        scratch_shapes=[pltpu.VMEM((STRIPS, 2, 512, WIDE), BF), pltpu.SemaphoreType.DMA((STRIPS, 4))],
+        scratch_shapes=[pltpu.VMEM((STRIPS, 2, 512, WIDE), BF), pltpu.SemaphoreType.DMA((STRIPS + 1, 4))],
         compiler_params=pltpu.CompilerParams(vmem_limit_bytes=10 * 1024 * 1024),
         name="product",
     )(*operands)

time: 73.5 us -> 73.3 us (level)
  transfers between devices with their start and end apart: 19 -> 19, of which waited for: 8 -> 8; matrix products, arithmetic and copies ran while one was open for 1% -> 1% of each run, Pallas kernels for 8% -> 7%
where the time goes in v6:
time: 73.3 us; the launch traced here: 72.4 us
  starting transfers between devices  37.8 us (52%)
  waiting for transfers between devices  21.8 us (30%)
  Pallas kernels  10 us (14%)
  local copies, waits for them, and re-layouts  1.63 us (2%)
    ppermute x18, starting transfers between devices, swap(): lax.ppermute(value, axis, [(i, i ^ bits) for i in range(lax.axis_size(axi...  28.5 us
    ppermute x18, waiting for transfers between devices, swap(): lax.ppermute(value, axis, [(i, i ^ bits) for i in range(lax.axis_size(axi...  17.9 us
    all_to_all x1, starting transfers between devices, per_device(): lax.all_to_all(spread.reshape(64, 16, 128), ('row', 'hour'), 0, 0, tiled=...  9.37 us
    pallas_call x2, Pallas kernels, product(): pl.pallas_call(functools.partial(product_kernel, other), out_shape=struct...  7.63 us
    all_to_all x1, waiting for transfers between devices, per_device(): lax.all_to_all(spread.reshape(64, 16, 128), ('row', 'hour'), 0, 0, tiled=...  3.98 us
    pallas_call x10, Pallas kernels, call(): pl.pallas_call(kernel, out_shape=out_shape, input_output_aliases=aliases,...  2.4 us
    unnamed x4, local copies, waits for them, and re-layouts  1.6 us
  transfers between devices with their start and end apart: 19, of which 8 were waited for; matrix products, arithmetic and copies ran while one was open for 1% of the time, Pallas kernels for 7%

profile of v6, /device:TPU:2, one launch (start us, length us, event | category | flops | bytes accessed | tf_op | source)
XLA Modules:
  0.0 72.4 jit_solution(1484634647363103307)
XLA Ops:
  0.0 0.9 %copy-done = bf16[8,2,64,128]{3,2,1,0:T(8,128)(2,1)S(1)} copy-done((bf16[8,2,64,128]{3,2,1,0:T(8,128)(2,1)S(1)}, bf16[8,2,64,128]{3,2,1,0:T(8,128)(2,1)}, u32[]{:S(2)}) %copy-start) | copy-done | bytes 262168
  1.0 0.7 copy-done.1
  1.6 0.8 %whiten.1 = (bf16[8,2,64,128]{3,2,1,0:T(8,128)(2,1)S(1)}, bf16[4,2,2,4,16,128]{5,4,3,2,1,0:T(8,128)(2,1)}) custom-call(bf16[8,2,64,128]{3,2,1,0:T(8,128)(2,1)S(1)} %copy-done, s32[1,64]{1,0:T(1,128)S(1)} %bitcast.5), custom_call_target="tpu_custom_call" | custom-call | tf_op jit(solution)/shard_map/whiten/pallas_call | solution.py:26
  2.5 9.4 %all-to-all-start = ((bf16[64,16,128]{2,1,0:T(8,128)(2,1)}), bf16[64,16,128]{2,1,0:T(8,128)(2,1)S(1)}, u32[]{:S(2)}, u32[]{:S(2)}) async-start(bf16[64,16,128]{2,1,0:T(8,128)(2,1)} %bitcast.2), calls=%async_computation | async-start | bytes 524288 | tf_op jit(solution)/shard_map/all_to_all | solution.py:223
  11.9 1.6 %collective-permute-start.2 = (bf16[2,2,64,128]{3,2,1,0:T(8,128)(2,1)S(1)}, bf16[2,2,64,128]{3,2,1,0:T(8,128)(2,1)S(1)}, u32[]{:S(2)}, u32[]{:S(2)}) collective-permute-start(bf16[2,2,64,128]{3,2,1,0:T(8,128)(2,1)S(1)} %get-tuple-element.31), channel_id=1, source_target_pairs={{0,3},{1,2},{2,1},{3,0},{4,7},{5,6},{6,5},{7,4},{8,11},{9,10},{10,... | collective-permute-start | bytes 196616 | tf_op jit(solution)/shard_map/ppermute | solution.py:213
  13.4 1.1 %collective-permute-start.1 = (bf16[2,2,64,128]{3,2,1,0:T(8,128)(2,1)S(1)}, bf16[2,2,64,128]{3,2,1,0:T(8,128)(2,1)S(1)}, u32[]{:S(2)}, u32[]{:S(2)}) collective-permute-start(bf16[2,2,64,128]{3,2,1,0:T(8,128)(2,1)S(1)} %get-tuple-element.32), channel_id=1, source_target_pairs={{0,2},{1,3},{2,0},{3,1},{4,6},{5,7},{6,4},{7,5},{8,10},{9,11},{10,... | collective-permute-start | bytes 196616 | tf_op jit(solution)/shard_map/ppermute | solution.py:213
  14.5 1.6 %collective-permute-start = (bf16[2,2,64,128]{3,2,1,0:T(8,128)(2,1)S(1)}, bf16[2,2,64,128]{3,2,1,0:T(8,128)(2,1)S(1)}, u32[]{:S(2)}, u32[]{:S(2)}) collective-permute-start(bf16[2,2,64,128]{3,2,1,0:T(8,128)(2,1)S(1)} %get-tuple-element.33), channel_id=1, source_target_pairs={{0,1},{1,0},{2,3},{3,2},{4,5},{5,4},{6,7},{7,6},{8,9},{9,8},{10,11... | collective-permute-start | bytes 196616 | tf_op jit(solution)/shard_map/ppermute | solution.py:213
  16.1 0.7 %pad_add_fusion.place = s32[17]{0:T(128)S(1)} fusion(s32[16]{0:T(128)} %param.5, s32[1]{0:T(128)} %bitcast.1), kind=kLoop, calls=%fused_computation.4 | loop fusion | flops 17 | bytes 136 | tf_op jit(solution)/shard_map/concatenate | solution.py:218
  16.8 4.0 %all-to-all-done = bf16[64,16,128]{2,1,0:T(8,128)(2,1)S(1)} async-done(((bf16[64,16,128]{2,1,0:T(8,128)(2,1)}), bf16[64,16,128]{2,1,0:T(8,128)(2,1)S(1)}, u32[]{:S(2)}, u32[]{:S(2)}) %all-to-all-start) | async-done | bytes 262176 | tf_op jit(solution)/shard_map/all_to_all | solution.py:223
  20.8 0.6 select.1
  21.4 6.4 %collective-permute-start.3 = (bf16[64,512]{1,0:T(8,128)(2,1)S(1)}, bf16[64,512]{1,0:T(8,128)(2,1)S(1)}, u32[]{:S(2)}, u32[]{:S(2)}) collective-permute-start(bf16[64,512]{1,0:T(8,128)(2,1)S(1)} %get-tuple-element.21), channel_id=1, source_target_pairs={{0,8},{4,12},{8,0},{12,4},{1,9},{5,13},{9,1},{13,5},{2,10},{6,14},... | collective-permute-start | bytes 196616 | tf_op jit(solution)/shard_map/ppermute | solution.py:213
  27.8 0.6 collective-permute-start.4
  28.3 0.9 %collective-permute-start.5 = (bf16[64,512]{1,0:T(8,128)(2,1)S(1)}, bf16[64,512]{1,0:T(8,128)(2,1)S(1)}, u32[]{:S(2)}, u32[]{:S(2)}) collective-permute-start(bf16[64,512]{1,0:T(8,128)(2,1)S(1)} %get-tuple-element.23), channel_id=1, source_target_pairs={{0,4},{4,0},{8,12},{12,8},{1,5},{5,1},{9,13},{13,9},{2,6},{6,2},{1... | collective-permute-start | bytes 196616 | tf_op jit(solution)/shard_map/ppermute | solution.py:213
  29.3 2.6 %collective-permute-done.3.refs_1_ = bf16[64,512]{1,0:T(8,128)(2,1)S(1)} collective-permute-done((bf16[64,512]{1,0:T(8,128)(2,1)S(1)}, bf16[64,512]{1,0:T(8,128)(2,1)S(1)}, u32[]{:S(2)}, u32[]{:S(2)}) %collective-permute-start.3) | collective-permute-done | bytes 65568 | tf_op jit(solution)/shard_map/ppermute | solution.py:213
  31.8 2.9 %collective-permute-done.4.refs_2_ = bf16[64,512]{1,0:T(8,128)(2,1)S(1)} collective-permute-done((bf16[64,512]{1,0:T(8,128)(2,1)S(1)}, bf16[64,512]{1,0:T(8,128)(2,1)S(1)}, u32[]{:S(2)}, u32[]{:S(2)}) %collective-permute-start.4) | collective-permute-done | bytes 65568 | tf_op jit(solution)/shard_map/ppermute | solution.py:213
  34.8 0.4 collective-permute-start.12
  35.2 0.6 collective-permute-start.11
  35.8 1.8 %collective-permute-start.10 = (bf16[64,2048]{1,0:T(8,128)(2,1)S(1)}, bf16[64,2048]{1,0:T(8,128)(2,1)S(1)}, u32[]{:S(2)}, u32[]{:S(2)}) collective-permute-start(bf16[64,2048]{1,0:T(8,128)(2,1)S(1)} %merge.1.refs_4_.refs_0_), channel_id=1, source_target_pairs={{0,192},{16,208},{32,224},{48,240},{64,128},{80,144},{96,160},{112... | collective-permute-start | bytes 786440 | tf_op jit(solution)/shard_map/ppermute | solution.py:213
  37.6 3.4 %collective-permute-start.7 = (bf16[2,2,256,128]{3,2,1,0:T(8,128)(2,1)S(1)}, bf16[2,2,256,128]{3,2,1,0:T(8,128)(2,1)S(1)}, u32[]{:S(2)}, u32[]{:S(2)}) collective-permute-start(bf16[2,2,256,128]{3,2,1,0:T(8,128)(2,1)S(1)} %hours.1.after.refs_0_), channel_id=1, source_target_pairs={{0,12},{4,8},{8,4},{12,0},{1,13},{5,9},{9,5},{13,1},{2,14},{6,10},... | collective-permute-start | bytes 786440 | tf_op jit(solution)/shard_map/ppermute | solution.py:213
  41.0 0.9 %collective-permute-start.6 = (bf16[2,2,256,128]{3,2,1,0:T(8,128)(2,1)S(1)}, bf16[2,2,256,128]{3,2,1,0:T(8,128)(2,1)S(1)}, u32[]{:S(2)}, u32[]{:S(2)}) collective-permute-start(bf16[2,2,256,128]{3,2,1,0:T(8,128)(2,1)S(1)} %hours.1.after.refs_0_), channel_id=1, source_target_pairs={{0,4},{4,0},{8,12},{12,8},{1,5},{5,1},{9,13},{13,9},{2,6},{6,2},{1... | collective-permute-start | bytes 786440 | tf_op jit(solution)/shard_map/ppermute | solution.py:213
  41.8 5.0 %collective-permute-done.12.other.refs_1_ = bf16[64,2048]{1,0:T(8,128)(2,1)S(1)} collective-permute-done((bf16[64,2048]{1,0:T(8,128)(2,1)S(1)}, bf16[64,2048]{1,0:T(8,128)(2,1)S(1)}, u32[]{:S(2)}, u32[]{:S(2)}) %collective-permute-start.12) | collective-permute-done | bytes 262176 | tf_op jit(solution)/shard_map/ppermute | solution.py:213
  46.9 3.2 %collective-permute-start.13 = (bf16[96,2048]{1,0:T(8,128)(2,1)S(1)}, bf16[96,2048]{1,0:T(8,128)(2,1)S(1)}, u32[]{:S(2)}, u32[]{:S(2)}) collective-permute-start(bf16[96,2048]{1,0:T(8,128)(2,1)S(1)} %get-tuple-element.26), channel_id=1, source_target_pairs={{0,64},{16,80},{32,96},{48,112},{64,0},{80,16},{96,32},{112,48},{1... | collective-permute-start | bytes 1179656 | tf_op jit(solution)/shard_map/ppermute | solution.py:213
  50.1 2.2 %collective-permute-start.15 = (bf16[64,2048]{1,0:T(8,128)(2,1)S(1)}, bf16[64,2048]{1,0:T(8,128)(2,1)S(1)}, u32[]{:S(2)}, u32[]{:S(2)}) collective-permute-start(bf16[64,2048]{1,0:T(8,128)(2,1)S(1)} %collective-permute-done.12.other.refs_1_), channel_id=1, source_target_pairs={{0,128},{16,144},{32,160},{48,176},{64,192},{80,208},{96,224},{112... | collective-permute-start | bytes 786440 | tf_op jit(solution)/shard_map/ppermute | solution.py:213
  52.2 3.1 %collective-permute-done.7.three.refs_2_ = bf16[2,2,256,128]{3,2,1,0:T(8,128)(2,1)S(1)} collective-permute-done((bf16[2,2,256,128]{3,2,1,0:T(8,128)(2,1)S(1)}, bf16[2,2,256,128]{3,2,1,0:T(8,128)(2,1)S(1)}, u32[]{:S(2)}, u32[]{:S(2)}) %collective-permute-start.7) | collective-permute-done | bytes 262176 | tf_op jit(solution)/shard_map/ppermute | solution.py:213
  55.3 1.5 %collective-permute-start.8 = (bf16[1,2,256,128]{3,2,1,0:T(8,128)(2,1)S(1)}, bf16[1,2,256,128]{3,2,1,0:T(8,128)(2,1)S(1)}, u32[]{:S(2)}, u32[]{:S(2)}) collective-permute-start(bf16[1,2,256,128]{3,2,1,0:T(8,128)(2,1)S(1)} %get-tuple-element.24), channel_id=1, source_target_pairs={{0,12},{4,8},{8,4},{12,0},{1,13},{5,9},{9,5},{13,1},{2,14},{6,10},... | collective-permute-start | bytes 393224 | tf_op jit(solution)/shard_map/ppermute | solution.py:213
  56.8 2.2 %collective-permute-start.9 = (bf16[1,2,256,128]{3,2,1,0:T(8,128)(2,1)S(1)}, bf16[1,2,256,128]{3,2,1,0:T(8,128)(2,1)S(1)}, u32[]{:S(2)}, u32[]{:S(2)}) collective-permute-start(bf16[1,2,256,128]{3,2,1,0:T(8,128)(2,1)S(1)} %get-tuple-element.25), channel_id=1, source_target_pairs={{0,4},{4,0},{8,12},{12,8},{1,5},{5,1},{9,13},{13,9},{2,6},{6,2},{1... | collective-permute-start | bytes 393224 | tf_op jit(solution)/shard_map/ppermute | solution.py:213
  59.0 0.5 left_near.1.left
  59.7 2.2 %collective-permute-done.14.refs_1_ = bf16[96,2048]{1,0:T(8,128)(2,1)S(1)} collective-permute-done((bf16[96,2048]{1,0:T(8,128)(2,1)S(1)}, bf16[96,2048]{1,0:T(8,128)(2,1)S(1)}, u32[]{:S(2)}, u32[]{:S(2)}) %collective-permute-start.14) | collective-permute-done | bytes 393248 | tf_op jit(solution)/shard_map/ppermute | solution.py:213
  62.2 0.4 collective-permute-done.8.low
  62.6 1.8 %collective-permute-done.9.high = bf16[1,2,256,128]{3,2,1,0:T(8,128)(2,1)S(1)} collective-permute-done((bf16[1,2,256,128]{3,2,1,0:T(8,128)(2,1)S(1)}, bf16[1,2,256,128]{3,2,1,0:T(8,128)(2,1)S(1)}, u32[]{:S(2)}, u32[]{:S(2)}) %collective-permute-start.9) | collective-permute-done | bytes 131104 | tf_op jit(solution)/shard_map/ppermute | solution.py:213
  64.6 3.8 %product.2.refs_0_ = bf16[2,2,512,2048]{3,2,1,0:T(8,128)(2,1)} custom-call(bf16[2,2,512,512]{3,2,1,0:T(8,128)(2,1)S(1)} %left_far.1.left, bf16[320,2048]{1,0:T(8,128)(2,1)S(1)} %stack.2.near, bf16[192,2048]{1,0:T(8,128)(2,1)S(1)} %stack.3.far), custom_call_target="tpu_custom_call" | custom-call | tf_op jit(solution)/shard_map/product/pallas_call | solution.py:200
  68.4 3.8 %product.3 = bf16[2,2,512,2048]{3,2,1,0:T(8,128)(2,1)} custom-call(bf16[2,2,512,512]{3,2,1,0:T(8,128)(2,1)S(1)} %left_far.1.left, bf16[320,2048]{1,0:T(8,128)(2,1)S(1)} %collective-permute-done.16.near, bf16[192,2048]{1,0:T(8,128)(2,1)S(1)} %collective-permute-done.17.far, bf16[2,2,512,2048]{3,2,1,0:T(8,128)(2,1)} %product.2.refs_0_), custom_call_target="tpu_custom_call", output_to_operand_aliasing={{}: (3, {})} | custom-call | tf_op jit(solution)/shard_map/product/pallas_call | solution.py:200
  (24 shorter events, 0.9 us)
Async XLA Ops:
  0.0 0.9 %copy-start = (bf16[8,2,64,128]{3,2,1,0:T(8,128)(2,1)S(1)}, bf16[8,2,64,128]{3,2,1,0:T(8,128)(2,1)}, u32[]{:S(2)}) copy-start(bf16[8,2,64,128]{3,2,1,0:T(8,128)(2,1)} %spectra.1) | copy-start | bytes 786436
  1.0 0.7 copy-start.1
  2.5 18.3 %all-to-all-start = ((bf16[64,16,128]{2,1,0:T(8,128)(2,1)}), bf16[64,16,128]{2,1,0:T(8,128)(2,1)S(1)}, u32[]{:S(2)}, u32[]{:S(2)}) async-start(bf16[64,16,128]{2,1,0:T(8,128)(2,1)} %bitcast.2), calls=%async_computation | async-start | bytes 524288 | tf_op jit(solution)/shard_map/all_to_all | solution.py:223
  11.9 16.4 %collective-permute-start.2 = (bf16[2,2,64,128]{3,2,1,0:T(8,128)(2,1)S(1)}, bf16[2,2,64,128]{3,2,1,0:T(8,128)(2,1)S(1)}, u32[]{:S(2)}, u32[]{:S(2)}) collective-permute-start(bf16[2,2,64,128]{3,2,1,0:T(8,128)(2,1)S(1)} %get-tuple-element.31), channel_id=1, source_target_pairs={{0,3},{1,2},{2,1},{3,0},{4,7},{5,6},{6,5},{7,4},{8,11},{9,10},{10,... | collective-permute-start | bytes 196616 | tf_op jit(solution)/shard_map/ppermute | solution.py:213
  13.4 15.8 %collective-permute-start.1 = (bf16[2,2,64,128]{3,2,1,0:T(8,128)(2,1)S(1)}, bf16[2,2,64,128]{3,2,1,0:T(8,128)(2,1)S(1)}, u32[]{:S(2)}, u32[]{:S(2)}) collective-permute-start(bf16[2,2,64,128]{3,2,1,0:T(8,128)(2,1)S(1)} %get-tuple-element.32), channel_id=1, source_target_pairs={{0,2},{1,3},{2,0},{3,1},{4,6},{5,7},{6,4},{7,5},{8,10},{9,11},{10,... | collective-permute-start | bytes 196616 | tf_op jit(solution)/shard_map/ppermute | solution.py:213
  14.5 14.8 %collective-permute-start = (bf16[2,2,64,128]{3,2,1,0:T(8,128)(2,1)S(1)}, bf16[2,2,64,128]{3,2,1,0:T(8,128)(2,1)S(1)}, u32[]{:S(2)}, u32[]{:S(2)}) collective-permute-start(bf16[2,2,64,128]{3,2,1,0:T(8,128)(2,1)S(1)} %get-tuple-element.33), channel_id=1, source_target_pairs={{0,1},{1,0},{2,3},{3,2},{4,5},{5,4},{6,7},{7,6},{8,9},{9,8},{10,11... | collective-permute-start | bytes 196616 | tf_op jit(solution)/shard_map/ppermute | solution.py:213
  21.4 10.4 %collective-permute-start.3 = (bf16[64,512]{1,0:T(8,128)(2,1)S(1)}, bf16[64,512]{1,0:T(8,128)(2,1)S(1)}, u32[]{:S(2)}, u32[]{:S(2)}) collective-permute-start(bf16[64,512]{1,0:T(8,128)(2,1)S(1)} %get-tuple-element.21), channel_id=1, source_target_pairs={{0,8},{4,12},{8,0},{12,4},{1,9},{5,13},{9,1},{13,5},{2,10},{6,14},... | collective-permute-start | bytes 196616 | tf_op jit(solution)/shard_map/ppermute | solution.py:213
  27.8 6.9 %collective-permute-start.4 = (bf16[64,512]{1,0:T(8,128)(2,1)S(1)}, bf16[64,512]{1,0:T(8,128)(2,1)S(1)}, u32[]{:S(2)}, u32[]{:S(2)}) collective-permute-start(bf16[64,512]{1,0:T(8,128)(2,1)S(1)} %get-tuple-element.22), channel_id=1, source_target_pairs={{0,12},{4,8},{8,4},{12,0},{1,13},{5,9},{9,5},{13,1},{2,14},{6,10},... | collective-permute-start | bytes 196616 | tf_op jit(solution)/shard_map/ppermute | solution.py:213
  28.3 6.4 %collective-permute-start.5 = (bf16[64,512]{1,0:T(8,128)(2,1)S(1)}, bf16[64,512]{1,0:T(8,128)(2,1)S(1)}, u32[]{:S(2)}, u32[]{:S(2)}) collective-permute-start(bf16[64,512]{1,0:T(8,128)(2,1)S(1)} %get-tuple-element.23), channel_id=1, source_target_pairs={{0,4},{4,0},{8,12},{12,8},{1,5},{5,1},{9,13},{13,9},{2,6},{6,2},{1... | collective-permute-start | bytes 196616 | tf_op jit(solution)/shard_map/ppermute | solution.py:213
  34.8 12.1 %collective-permute-start.12 = (bf16[64,2048]{1,0:T(8,128)(2,1)S(1)}, bf16[64,2048]{1,0:T(8,128)(2,1)S(1)}, u32[]{:S(2)}, u32[]{:S(2)}) collective-permute-start(bf16[64,2048]{1,0:T(8,128)(2,1)S(1)} %merge.1.refs_4_.refs_0_), channel_id=1, source_target_pairs={{0,32},{16,48},{32,0},{48,16},{64,96},{80,112},{96,64},{112,80},{1... | collective-permute-start | bytes 786440 | tf_op jit(solution)/shard_map/ppermute | solution.py:213
  35.2 11.7 %collective-permute-start.11 = (bf16[64,2048]{1,0:T(8,128)(2,1)S(1)}, bf16[64,2048]{1,0:T(8,128)(2,1)S(1)}, u32[]{:S(2)}, u32[]{:S(2)}) collective-permute-start(bf16[64,2048]{1,0:T(8,128)(2,1)S(1)} %merge.1.refs_4_.refs_0_), channel_id=1, source_target_pairs={{0,64},{16,80},{32,96},{48,112},{64,0},{80,16},{96,32},{112,48},{1... | collective-permute-start | bytes 786440 | tf_op jit(solution)/shard_map/ppermute | solution.py:213
  35.8 11.1 %collective-permute-start.10 = (bf16[64,2048]{1,0:T(8,128)(2,1)S(1)}, bf16[64,2048]{1,0:T(8,128)(2,1)S(1)}, u32[]{:S(2)}, u32[]{:S(2)}) collective-permute-start(bf16[64,2048]{1,0:T(8,128)(2,1)S(1)} %merge.1.refs_4_.refs_0_), channel_id=1, source_target_pairs={{0,192},{16,208},{32,224},{48,240},{64,128},{80,144},{96,160},{112... | collective-permute-start | bytes 786440 | tf_op jit(solution)/shard_map/ppermute | solution.py:213
  37.6 17.7 %collective-permute-start.7 = (bf16[2,2,256,128]{3,2,1,0:T(8,128)(2,1)S(1)}, bf16[2,2,256,128]{3,2,1,0:T(8,128)(2,1)S(1)}, u32[]{:S(2)}, u32[]{:S(2)}) collective-permute-start(bf16[2,2,256,128]{3,2,1,0:T(8,128)(2,1)S(1)} %hours.1.after.refs_0_), channel_id=1, source_target_pairs={{0,12},{4,8},{8,4},{12,0},{1,13},{5,9},{9,5},{13,1},{2,14},{6,10},... | collective-permute-start | bytes 786440 | tf_op jit(solution)/shard_map/ppermute | solution.py:213
  41.0 14.3 %collective-permute-start.6 = (bf16[2,2,256,128]{3,2,1,0:T(8,128)(2,1)S(1)}, bf16[2,2,256,128]{3,2,1,0:T(8,128)(2,1)S(1)}, u32[]{:S(2)}, u32[]{:S(2)}) collective-permute-start(bf16[2,2,256,128]{3,2,1,0:T(8,128)(2,1)S(1)} %hours.1.after.refs_0_), channel_id=1, source_target_pairs={{0,4},{4,0},{8,12},{12,8},{1,5},{5,1},{9,13},{13,9},{2,6},{6,2},{1... | collective-permute-start | bytes 786440 | tf_op jit(solution)/shard_map/ppermute | solution.py:213
  46.9 12.8 %collective-permute-start.13 = (bf16[96,2048]{1,0:T(8,128)(2,1)S(1)}, bf16[96,2048]{1,0:T(8,128)(2,1)S(1)}, u32[]{:S(2)}, u32[]{:S(2)}) collective-permute-start(bf16[96,2048]{1,0:T(8,128)(2,1)S(1)} %get-tuple-element.26), channel_id=1, source_target_pairs={{0,64},{16,80},{32,96},{48,112},{64,0},{80,16},{96,32},{112,48},{1... | collective-permute-start | bytes 1179656 | tf_op jit(solution)/shard_map/ppermute | solution.py:213
  50.1 11.8 %collective-permute-start.14 = (bf16[96,2048]{1,0:T(8,128)(2,1)S(1)}, bf16[96,2048]{1,0:T(8,128)(2,1)S(1)}, u32[]{:S(2)}, u32[]{:S(2)}) collective-permute-start(bf16[96,2048]{1,0:T(8,128)(2,1)S(1)} %get-tuple-element.27), channel_id=1, source_target_pairs={{0,192},{16,208},{32,224},{48,240},{64,128},{80,144},{96,160},{112... | collective-permute-start | bytes 1179656 | tf_op jit(solution)/shard_map/ppermute | solution.py:213
  50.1 9.4 %collective-permute-start.15 = (bf16[64,2048]{1,0:T(8,128)(2,1)S(1)}, bf16[64,2048]{1,0:T(8,128)(2,1)S(1)}, u32[]{:S(2)}, u32[]{:S(2)}) collective-permute-start(bf16[64,2048]{1,0:T(8,128)(2,1)S(1)} %collective-permute-done.12.other.refs_1_), channel_id=1, source_target_pairs={{0,128},{16,144},{32,160},{48,176},{64,192},{80,208},{96,224},{112... | collective-permute-start | bytes 786440 | tf_op jit(solution)/shard_map/ppermute | solution.py:213
  55.3 7.3 %collective-permute-start.8 = (bf16[1,2,256,128]{3,2,1,0:T(8,128)(2,1)S(1)}, bf16[1,2,256,128]{3,2,1,0:T(8,128)(2,1)S(1)}, u32[]{:S(2)}, u32[]{:S(2)}) collective-permute-start(bf16[1,2,256,128]{3,2,1,0:T(8,128)(2,1)S(1)} %get-tuple-element.24), channel_id=1, source_target_pairs={{0,12},{4,8},{8,4},{12,0},{1,13},{5,9},{9,5},{13,1},{2,14},{6,10},... | collective-permute-start | bytes 393224 | tf_op jit(solution)/shard_map/ppermute | solution.py:213
  56.8 7.5 %collective-permute-start.9 = (bf16[1,2,256,128]{3,2,1,0:T(8,128)(2,1)S(1)}, bf16[1,2,256,128]{3,2,1,0:T(8,128)(2,1)S(1)}, u32[]{:S(2)}, u32[]{:S(2)}) collective-permute-start(bf16[1,2,256,128]{3,2,1,0:T(8,128)(2,1)S(1)} %get-tuple-element.25), channel_id=1, source_target_pairs={{0,4},{4,0},{8,12},{12,8},{1,5},{5,1},{9,13},{13,9},{2,6},{6,2},{1... | collective-permute-start | bytes 393224 | tf_op jit(solution)/shard_map/ppermute | solution.py:213
  59.6 8.8 %collective-permute-start.16 = (bf16[320,2048]{1,0:T(8,128)(2,1)S(1)}, bf16[320,2048]{1,0:T(8,128)(2,1)S(1)}, u32[]{:S(2)}, u32[]{:S(2)}) collective-permute-start(bf16[320,2048]{1,0:T(8,128)(2,1)S(1)} %stack.2.near), channel_id=1, source_target_pairs={{0,16},{16,0},{32,48},{48,32},{64,80},{80,64},{96,112},{112,96},{1... | collective-permute-start | bytes 3932168 | tf_op jit(solution)/shard_map/ppermute | solution.py:213
  61.9 6.5 %collective-permute-start.17 = (bf16[192,2048]{1,0:T(8,128)(2,1)S(1)}, bf16[192,2048]{1,0:T(8,128)(2,1)S(1)}, u32[]{:S(2)}, u32[]{:S(2)}) collective-permute-start(bf16[192,2048]{1,0:T(8,128)(2,1)S(1)} %stack.3.far), channel_id=1, source_target_pairs={{0,16},{16,0},{32,48},{48,32},{64,80},{80,64},{96,112},{112,96},{1... | collective-permute-start | bytes 2359304 | tf_op jit(solution)/shard_map/ppermute | solution.py:213
